TPU v7x, 256 devices: a whole 4x4x8 slice. The times are simulated.
256 devices in a mesh: dp: 4 (over y), seq: 64 (over z, x, core).
Axes of the slice: x: 4, y: 4, z: 8, core: 2. Of those that a mesh axis runs over, the one named last changes fastest.
Arguments:
- query: bfloat16 [4, 16384, 1536], P('dp', 'seq'), may hold values from -6 to 6
- key: bfloat16 [4, 16384, 1536], P('dp', 'seq'), may hold values from -6 to 6
- value: bfloat16 [4, 16384, 1536], P('dp', 'seq'), may hold values from -6 to 6
- segments: int32 [4, 16384], P('dp', 'seq'), may hold values from 0 to 95, never falling along the last dimension, each value on 1 to 256 neighbouring positions
- out_proj: bfloat16 [1536, 1536], replicated, may hold values from -0.15625 to 0.15625
- conv_kernel: bfloat16 [31, 1536], replicated, may hold values from -1 to 1
- cotangent: bfloat16 [4, 16384, 1536], P('dp', 'seq'), may hold values from -6 to 6
Outputs:
- block_out: bfloat16 [4, 16384, 1536], P('dp', 'seq')
- grad_query: bfloat16 [4, 16384, 1536], P('dp', 'seq')
- grad_key: bfloat16 [4, 16384, 1536], P('dp', 'seq')
- grad_value: bfloat16 [4, 16384, 1536], P('dp', 'seq')
- grad_kernel: float32 [31, 1536], replicated
- grad_out_proj: float32 [1536, 1536], P(('dp', 'seq'))
Inputs may be any that keep to these rules, and one draw needn't show every extreme that they name: `segments`: along the frames of a data group the utterance number never falls; every utterance holds 1 to 256 frames and one holds exactly 256.
All inputs are finite; a program needn't handle non-finite values.
Results may differ from a plain program's by a relative error of at most 0.02.
Values may be sent and summed in bfloat16 or wider, within the bound.
No kernel may reach another device: no remote copies, remote signals or barrier semaphores. Data moves between devices by JAX's collectives and lax.ppermute only.
A program may use at most 128 MiB of HBM per device.

v0:
```python
import jax
import jax.numpy as jnp
from jax import lax
from jax.sharding import PartitionSpec as P

HD = 64
KW = 31


def extended(block, sides, width):
    for axis, dim in sides:
        count = lax.axis_size(axis)
        forward = [(i, i + 1) for i in range(count - 1)]
        backward = [(target, source) for source, target in forward]
        low = lax.ppermute(
            lax.slice_in_dim(block, block.shape[dim] - width, None, axis=dim), axis, forward
        )
        high = lax.ppermute(lax.slice_in_dim(block, 0, width, axis=dim), axis, backward)
        block = jnp.concatenate([low, block, high], axis=dim)
    return block


def from_behind(value, axis, steps):
    count = lax.axis_size(axis)
    first, last = (max(0, -steps), min(count, count - steps))
    return lax.ppermute(value, axis, [(source, source + steps) for source in range(first, last)])


def head_scores(queries, keys_block, query_ids, key_ids):
    query_heads = queries.reshape(queries.shape[0], -1, HD)
    key_heads = keys_block.reshape(keys_block.shape[0], -1, HD)
    scores = jnp.einsum(
        "rhe,whe->hrw", query_heads, key_heads, preferred_element_type=jnp.float32
    ) * HD ** (-0.5)
    allowed = query_ids[:, None] == key_ids[None, :]
    return jnp.where(allowed[None], scores, -1e30)


def to_groups(matrix):
    return jnp.moveaxis(matrix.reshape(matrix.shape[0], -1, 4 * HD), 1, 0)


def from_groups(stacked):
    return jnp.moveaxis(stacked, 0, 1).reshape(stacked.shape[1], -1)


def attend(queries, keys_block, values_block, query_ids, key_ids):
    scores = head_scores(queries, keys_block, query_ids, key_ids)
    highest = jnp.max(scores, axis=2)
    weights = jnp.exp(scores - highest[:, :, None])
    totals = jnp.sum(weights, axis=2)
    probs = (weights / totals[:, :, None]).astype(jnp.bfloat16)
    value_heads = values_block.reshape(values_block.shape[0], -1, HD)
    context = jnp.einsum("hrw,whe->rhe", probs, value_heads, preferred_element_type=jnp.float32)
    return (context.reshape(queries.shape[0], -1), highest, totals)


def score_grads(
    queries, keys_block, values_block, upstream, highest, totals, deltas, query_ids, key_ids
):
    scores = head_scores(queries, keys_block, query_ids, key_ids)
    probs = jnp.exp(scores - highest[:, :, None]) / totals[:, :, None]
    upstream_heads = upstream.reshape(upstream.shape[0], -1, HD)
    value_heads = values_block.reshape(values_block.shape[0], -1, HD)
    prob_grads = jnp.einsum(
        "rhe,whe->hrw", upstream_heads, value_heads, preferred_element_type=jnp.float32
    )
    score_grad = (probs * (prob_grads - deltas[:, :, None]) * HD ** (-0.5)).astype(jnp.bfloat16)
    return (probs.astype(jnp.bfloat16), score_grad, upstream_heads)


def query_side(queries, keys_block, score_grad):
    key_heads = keys_block.reshape(keys_block.shape[0], -1, HD)
    grads = jnp.einsum("hrw,whe->rhe", score_grad, key_heads, preferred_element_type=jnp.float32)
    return grads.reshape(queries.shape[0], -1)


def key_side(queries, keys_block, probs, score_grad, upstream_heads):
    query_heads = queries.reshape(queries.shape[0], -1, HD)
    key_part = jnp.einsum(
        "hrw,rhe->whe", score_grad, query_heads, preferred_element_type=jnp.float32
    )
    value_part = jnp.einsum(
        "hrw,rhe->whe", probs, upstream_heads, preferred_element_type=jnp.float32
    )
    return (key_part.reshape(keys_block.shape[0], -1), value_part.reshape(keys_block.shape[0], -1))


def per_device(query, key, value, segments, out_proj, conv_kernel, cotangent):
    frame_count = query.shape[1]
    width = query.shape[2]
    group_count = width // (4 * HD)
    reach = KW // 2
    queries = query[0]
    keys_local = key[0]
    values_local = value[0]
    own_ids = segments[0] + 1
    wide_ids = extended(own_ids, (("seq", 0),), frame_count)
    paired = extended(jnp.stack([keys_local, values_local]), (("seq", 1),), frame_count)

    def forward_group(items):
        return attend(items[0], items[1], items[2], own_ids, wide_ids)

    context_groups, highest, totals = lax.map(
        forward_group, (to_groups(queries), to_groups(paired[0]), to_groups(paired[1]))
    )
    context = from_groups(context_groups)
    context_b = context.astype(jnp.bfloat16)
    attended = jnp.dot(context_b, out_proj, preferred_element_type=jnp.float32).astype(jnp.bfloat16)
    attended_wide = extended(attended, (("seq", 0),), reach)
    conv_ids = wide_ids[frame_count - reach : 2 * frame_count + reach]
    kernel = conv_kernel.astype(jnp.float32)
    masks = [(conv_ids[offset : offset + frame_count] == own_ids)[:, None] for offset in range(KW)]
    convolved = jnp.zeros((frame_count, width), jnp.float32)
    for offset in range(KW):
        convolved = convolved + jnp.where(
            masks[offset],
            kernel[offset] * attended_wide[offset : offset + frame_count].astype(jnp.float32),
            0.0,
        )
    gate = jax.nn.sigmoid(convolved)
    block_out = (convolved * gate).astype(jnp.bfloat16)
    conv_grad = (cotangent[0].astype(jnp.float32) * gate * (1.0 + convolved * (1.0 - gate))).astype(
        jnp.bfloat16
    )
    conv_grad_wide = extended(conv_grad, (("seq", 0),), reach)
    conv_grad_f = conv_grad.astype(jnp.float32)
    attended_grad = jnp.zeros((frame_count, width), jnp.float32)
    kernel_rows = []
    for offset in range(KW):
        mirror = 2 * reach - offset
        attended_grad = attended_grad + jnp.where(
            masks[mirror],
            kernel[offset] * conv_grad_wide[mirror : mirror + frame_count].astype(jnp.float32),
            0.0,
        )
        kernel_rows.append(
            jnp.sum(
                jnp.where(
                    masks[offset],
                    conv_grad_f * attended_wide[offset : offset + frame_count].astype(jnp.float32),
                    0.0,
                ),
                axis=0,
            )
        )
    scale_out = (lax.axis_size("dp") * lax.axis_size("seq") * frame_count) ** (-0.5)
    grad_kernel = lax.psum(jnp.stack(kernel_rows), ("dp", "seq")) * scale_out
    attended_grad_b = attended_grad.astype(jnp.bfloat16)
    reduced = lax.psum_scatter(
        lax.dot_general(
            context_b, attended_grad_b, (((0,), (0,)), ((), ())), preferred_element_type=jnp.float32
        ),
        ("dp", "seq"),
        scatter_dimension=0,
        tiled=True,
    )
    grad_out_proj = reduced * scale_out
    context_grad = lax.dot_general(
        attended_grad_b, out_proj, (((1,), (1,)), ((), ())), preferred_element_type=jnp.float32
    ).astype(jnp.bfloat16)
    products = (to_groups(context_grad).astype(jnp.float32) * to_groups(context)).reshape(
        group_count, frame_count, 4, HD
    )
    deltas = jnp.moveaxis(jnp.sum(products, axis=3), 2, 1)

    def both_group(items):
        probs, score_grad, upstream_heads = score_grads(
            items[0], items[1], items[2], items[3], items[4], items[5], items[6], own_ids, wide_ids
        )
        key_part, value_part = key_side(items[0], items[1], probs, score_grad, upstream_heads)
        return (query_side(items[0], items[1], score_grad), key_part, value_part)

    query_part, key_part, value_part = lax.map(
        both_group,
        (
            to_groups(queries),
            to_groups(paired[0]),
            to_groups(paired[1]),
            to_groups(context_grad),
            highest,
            totals,
            deltas,
        ),
    )
    key_wide = from_groups(key_part)
    value_wide = from_groups(value_part)
    earlier = jnp.stack([key_wide[:frame_count], value_wide[:frame_count]])
    later = jnp.stack([key_wide[2 * frame_count :], value_wide[2 * frame_count :]])
    from_later = from_behind(earlier.astype(jnp.bfloat16), "seq", -1).astype(earlier.dtype)
    from_earlier = from_behind(later.astype(jnp.bfloat16), "seq", 1).astype(later.dtype)
    key_total = key_wide[frame_count : 2 * frame_count] + from_later[0] + from_earlier[0]
    value_total = value_wide[frame_count : 2 * frame_count] + from_later[1] + from_earlier[1]
    grad_query = from_groups(query_part).astype(jnp.bfloat16)
    grad_key = key_total.astype(jnp.bfloat16)
    grad_value = value_total.astype(jnp.bfloat16)
    return (
        block_out[None],
        grad_query[None],
        grad_key[None],
        grad_value[None],
        grad_kernel,
        grad_out_proj,
    )


def solution(mesh):
    in_specs = (
        P("dp", "seq", None),
        P("dp", "seq", None),
        P("dp", "seq", None),
        P("dp", "seq"),
        P(),
        P(),
        P("dp", "seq", None),
    )
    out_specs = (
        P("dp", "seq", None),
        P("dp", "seq", None),
        P("dp", "seq", None),
        P("dp", "seq", None),
        P(),
        P(("dp", "seq"), None),
    )
    return jax.shard_map(
        per_device, mesh=mesh, in_specs=in_specs, out_specs=out_specs, check_vma=False
    )
```

profile of v0, /device:TPU:31, one launch (start us, length us, event | category | flops | bytes accessed | tf_op | source)
XLA Modules:
  0.0 1730.5 jit_solution(641398557045694055)
XLA Ops:
  8.6 14.1 collective-permute-start.1
  59.1 38.1 %while.30 = (s32[]{:T(128)}, f32[6,256,256]{1,2,0:T(8,128)}, f32[6,4,256]{2,1,0:T(4,128)}, f32[6,4,256]{2,1,0:T(4,128)}, bf16[6,768,256]{1,2,0:T(8,128)(2,1)S(1)...) while((s32[]{:T(128)}, f32[6,256,256]{1,2,0:T(8,128)}, ...), condition=%wide.region_3.4_spmd.clone, body=%wide.region_0.3_spmd.sunk.clone | while | flops 210958336 | bytes 13804649 | solution.py:104
  113.4 22.7 %fusion.142 = (f32[1536]{0:T(1024)}, f32[1536]{0:T(1024)}, f32[1536]{0:T(1024)}, f32[1536]{0:T(1024)}, f32[1536]{0:T(1024)}, /*index=5*/f32[1536]{0:T(1024)}, bf16[256,1536]{1,0:T(8,128)(2,1)S(1)}, f32[256,1536]{1,0:T(8,128)}) fusion(pred[256]{0:T(512)(128)(4,1)S(1)} %get-tuple-element.289, bf16[15,1536]{1,0:T(8,128)(2,1)S(1)} %collective-permute-done.5, ...), kind=kLoop, calls=%fused_computation.286 | loop fusion | flops 104193024 | bytes 4259328 | tf_op jit(solution)/shard_map/reduce_sum | solution.py:138
  145.8 24.2 %fusion.149 = bf16[256,1536]{1,0:T(8,128)(2,1)S(1)} fusion(bf16[256,1536]{1,0:T(8,128)(2,1)S(1)} %get-tuple-element.248, bf16[15,1536]{1,0:T(8,128)(2,1)} %collective-permute-done.7, bf16[15,1536]{1,0:T(8,128)(2,1)} %copy-done.74, f32[1536]{0:T(1024)S(1)} %get-tuple-element.174, f32[1536]{0:T(1024)S(1)} %get-tuple-element.175, ...), kind=kLoop, calls=%fused_computation.304 | loop fusion | flops 83755008 | bytes 1863168 | tf_op jit(solution)/shard_map/convert_element_type | solution.py:149
  175.1 622.1 %fusion = f32[8,1536]{1,0:T(8,128)S(1)} fusion(f32[1536,1536]{1,0:T(8,128)} %fusion.216), kind=kCustom, calls=%all-reduce-scatter | all-reduce-scatter fusion | flops 3145729 | bytes 9486336
  797.3 99.7 %collective-permute-start.10 = (f32[8,1536]{1,0:T(8,128)S(1)}, f32[8,1536]{1,0:T(8,128)S(1)}, u32[]{:S(2)}, u32[]{:S(2)}) collective-permute-start(f32[8,1536]{1,0:T(8,128)S(1)} %fusion), channel_id=1, source_target_pairs={{0,1},{1,2},{2,3},{3,4},{4,5},{5,6},{6,7},{7,8},{8,9},{9,10},{10,1... | collective-permute-start | bytes 147464
  914.8 15.1 collective-permute-start.12
  929.9 13.1 collective-permute-start.13
  943.1 13.1 collective-permute-start.14
  956.2 13.1 collective-permute-start.15
  969.4 13.1 collective-permute-start.16
  1001.6 13.1 collective-permute-start.18
  1110.4 13.3 collective-permute-start.26
  1140.3 13.1 collective-permute-start.28
  1153.4 13.1 collective-permute-start.29
  1166.6 13.1 collective-permute-start.30
  1179.7 13.1 collective-permute-start.31
  1199.0 13.3 collective-permute-start.32
  1266.6 13.1 collective-permute-start.37
  1279.7 13.1 collective-permute-start.38
  1292.9 13.1 collective-permute-start.39
  1315.7 52.4 %while.31 = (s32[]{:T(128)}, bf16[6,256,256]{1,2,0:T(8,128)(2,1)S(1)}, f32[6,768,256]{1,2,0:T(8,128)}, f32[6,768,256]{1,2,0:T(8,128)}, bf16[6,768,256]{1,2,0:T(8...) while((s32[]{:T(128)}, ...), condition=%wide.region_6.7_spmd.clone, body=%wide.region_5.6_spmd.sunk.clone | while | flops 510590976 | bytes 23504016 | solution.py:174
  1483.7 96.9 %concatenate.118 = f32[518,1536]{1,0:T(8,128)} concatenate(f32[6,1536]{1,0:T(8,128)S(1)} %collective-permute-done.73, f32[8,1536]{1,0:T(8,128)} %collective-permute-done.72, f32[8,1536]{1,0:T(8,128)} %collective-permute-done.71, f32[8,1536]{1,0:T(8,128)} %collective-permute-done.70, f32[8,1536]{1,0:T(8,128)} %collective-permute-done.69, f32[8,1536]{1,0:T(8,128)} %collective-permute-done.68, ...), dimensions={0} | concatenate | bytes 6365184
  1582.2 132.7 %all-reduce.4.cloned.1.call-done = f32[31,1536]{1,0:T(8,128)} async-done(((f32[31,1536]{1,0:T(8,128)}), f32[31,1536]{1,0:T(8,128)}) %all-reduce.4.cloned.1.call-update) | async-done | bytes 190480 | tf_op jit(solution)/shard_map/psum | solution.py:148
  (664 shorter events, 500.4 us)
Async XLA Ops:
  7.2 1707.7 %all-reduce.4.cloned.1.call-start = ((), (), s32[]{:S(2)}) async-start(), calls=%async_computation | async-start | bytes 393216 | tf_op jit(solution)/shard_map/psum | solution.py:148
  797.3 158.9 %collective-permute-start.10 = (f32[8,1536]{1,0:T(8,128)S(1)}, f32[8,1536]{1,0:T(8,128)S(1)}, u32[]{:S(2)}, u32[]{:S(2)}) collective-permute-start(f32[8,1536]{1,0:T(8,128)S(1)} %fusion), channel_id=1, source_target_pairs={{0,1},{1,2},{2,3},{3,4},{4,5},{5,6},{6,7},{7,8},{8,9},{9,10},{10,1... | collective-permute-start | bytes 147464
  896.9 72.4 %collective-permute-start.11 = (f32[8,1536]{1,0:T(8,128)S(1)}, f32[8,1536]{1,0:T(8,128)S(1)}, u32[]{:S(2)}, u32[]{:S(2)}) collective-permute-start(f32[8,1536]{1,0:T(8,128)S(1)} %fusion), channel_id=1, source_target_pairs={{0,2},{1,3},{2,4},{3,5},{4,6},{5,7},{6,8},{7,9},{8,10},{9,11},{10,... | collective-permute-start | bytes 147464
  914.8 73.6 %collective-permute-start.12 = (f32[8,1536]{1,0:T(8,128)S(1)}, f32[8,1536]{1,0:T(8,128)S(1)}, u32[]{:S(2)}, u32[]{:S(2)}) collective-permute-start(f32[8,1536]{1,0:T(8,128)S(1)} %fusion), channel_id=1, source_target_pairs={{0,3},{1,4},{2,5},{3,6},{4,7},{5,8},{6,9},{7,10},{8,11},{9,12},{10... | collective-permute-start | bytes 147464
  929.9 71.6 %collective-permute-start.13 = (f32[8,1536]{1,0:T(8,128)S(1)}, f32[8,1536]{1,0:T(8,128)S(1)}, u32[]{:S(2)}, u32[]{:S(2)}) collective-permute-start(f32[8,1536]{1,0:T(8,128)S(1)} %fusion), channel_id=1, source_target_pairs={{0,4},{1,5},{2,6},{3,7},{4,8},{5,9},{6,10},{7,11},{8,12},{9,13},{1... | collective-permute-start | bytes 147464
  943.1 71.6 %collective-permute-start.14 = (f32[8,1536]{1,0:T(8,128)S(1)}, f32[8,1536]{1,0:T(8,128)S(1)}, u32[]{:S(2)}, u32[]{:S(2)}) collective-permute-start(f32[8,1536]{1,0:T(8,128)S(1)} %fusion), channel_id=1, source_target_pairs={{0,5},{1,6},{2,7},{3,8},{4,9},{5,10},{6,11},{7,12},{8,13},{9,14},{... | collective-permute-start | bytes 147464
  956.2 71.7 %collective-permute-start.15 = (f32[8,1536]{1,0:T(8,128)S(1)}, f32[8,1536]{1,0:T(8,128)S(1)}, u32[]{:S(2)}, u32[]{:S(2)}) collective-permute-start(f32[8,1536]{1,0:T(8,128)S(1)} %fusion), channel_id=1, source_target_pairs={{0,6},{1,7},{2,8},{3,9},{4,10},{5,11},{6,12},{7,13},{8,14},{9,15},... | collective-permute-start | bytes 147464
  969.4 71.7 %collective-permute-start.16 = (f32[8,1536]{1,0:T(8,128)S(1)}, f32[8,1536]{1,0:T(8,128)S(1)}, u32[]{:S(2)}, u32[]{:S(2)}) collective-permute-start(f32[8,1536]{1,0:T(8,128)S(1)} %fusion), channel_id=1, source_target_pairs={{0,7},{1,8},{2,9},{3,10},{4,11},{5,12},{6,13},{7,14},{8,15},{9,16}... | collective-permute-start | bytes 147464
  988.5 69.4 %collective-permute-start.17 = (f32[8,1536]{1,0:T(8,128)S(1)}, f32[8,1536]{1,0:T(8,128)S(1)}, u32[]{:S(2)}, u32[]{:S(2)}) collective-permute-start(f32[8,1536]{1,0:T(8,128)S(1)} %fusion), channel_id=1, source_target_pairs={{0,8},{1,9},{2,10},{3,11},{4,12},{5,13},{6,14},{7,15},{8,16},{9,17... | collective-permute-start | bytes 147464
  1001.6 69.3 %collective-permute-start.18 = (f32[8,1536]{1,0:T(8,128)S(1)}, f32[8,1536]{1,0:T(8,128)S(1)}, u32[]{:S(2)}, u32[]{:S(2)}) collective-permute-start(f32[8,1536]{1,0:T(8,128)S(1)} %fusion), channel_id=1, source_target_pairs={{0,9},{1,10},{2,11},{3,12},{4,13},{5,14},{6,15},{7,16},{8,17},{9,1... | collective-permute-start | bytes 147464
  1014.7 69.3 %collective-permute-start.19 = (f32[8,1536]{1,0:T(8,128)S(1)}, f32[8,1536]{1,0:T(8,128)S(1)}, u32[]{:S(2)}, u32[]{:S(2)}) collective-permute-start(f32[8,1536]{1,0:T(8,128)S(1)} %fusion), channel_id=1, source_target_pairs={{0,10},{1,11},{2,12},{3,13},{4,14},{5,15},{6,16},{7,17},{8,18},{9,... | collective-permute-start | bytes 147464
  1027.9 69.3 %collective-permute-start.20 = (f32[8,1536]{1,0:T(8,128)S(1)}, f32[8,1536]{1,0:T(8,128)S(1)}, u32[]{:S(2)}, u32[]{:S(2)}) collective-permute-start(f32[8,1536]{1,0:T(8,128)S(1)} %fusion), channel_id=1, source_target_pairs={{0,11},{1,12},{2,13},{3,14},{4,15},{5,16},{6,17},{7,18},{8,19},{9,... | collective-permute-start | bytes 147464
  1041.0 69.3 %collective-permute-start.21 = (f32[8,1536]{1,0:T(8,128)S(1)}, f32[8,1536]{1,0:T(8,128)S(1)}, u32[]{:S(2)}, u32[]{:S(2)}) collective-permute-start(f32[8,1536]{1,0:T(8,128)S(1)} %fusion), channel_id=1, source_target_pairs={{0,12},{1,13},{2,14},{3,15},{4,16},{5,17},{6,18},{7,19},{8,20},{9,... | collective-permute-start | bytes 147464
  1110.4 69.3 %collective-permute-start.26 = (f32[8,1536]{1,0:T(8,128)S(1)}, f32[8,1536]{1,0:T(8,128)S(1)}, u32[]{:S(2)}, u32[]{:S(2)}) collective-permute-start(f32[8,1536]{1,0:T(8,128)S(1)} %fusion), channel_id=1, source_target_pairs={{0,17},{1,18},{2,19},{3,20},{4,21},{5,22},{6,23},{7,24},{8,25},{9,... | collective-permute-start | bytes 147464
  1127.1 71.9 %collective-permute-start.27 = (f32[8,1536]{1,0:T(8,128)S(1)}, f32[8,1536]{1,0:T(8,128)S(1)}, u32[]{:S(2)}, u32[]{:S(2)}) collective-permute-start(f32[8,1536]{1,0:T(8,128)S(1)} %fusion), channel_id=1, source_target_pairs={{0,18},{1,19},{2,20},{3,21},{4,22},{5,23},{6,24},{7,25},{8,26},{9,... | collective-permute-start | bytes 147464
  1140.3 72.0 %collective-permute-start.28 = (f32[8,1536]{1,0:T(8,128)S(1)}, f32[8,1536]{1,0:T(8,128)}, u32[]{:S(2)}, u32[]{:S(2)}) collective-permute-start(f32[8,1536]{1,0:T(8,128)S(1)} %fusion), channel_id=1, source_target_pairs={{0,19},{1,20},{2,21},{3,22},{4,23},{5,24},{6,25},{7,26},{8,27},{9,... | collective-permute-start | bytes 147464
  1153.4 72.0 %collective-permute-start.29 = (f32[8,1536]{1,0:T(8,128)S(1)}, f32[8,1536]{1,0:T(8,128)}, u32[]{:S(2)}, u32[]{:S(2)}) collective-permute-start(f32[8,1536]{1,0:T(8,128)S(1)} %fusion), channel_id=1, source_target_pairs={{0,20},{1,21},{2,22},{3,23},{4,24},{5,25},{6,26},{7,27},{8,28},{9,... | collective-permute-start | bytes 147464
  1166.6 72.0 %collective-permute-start.30 = (f32[8,1536]{1,0:T(8,128)S(1)}, f32[8,1536]{1,0:T(8,128)}, u32[]{:S(2)}, u32[]{:S(2)}) collective-permute-start(f32[8,1536]{1,0:T(8,128)S(1)} %fusion), channel_id=1, source_target_pairs={{0,21},{1,22},{2,23},{3,24},{4,25},{5,26},{6,27},{7,28},{8,29},{9,... | collective-permute-start | bytes 147464
  1179.7 72.0 %collective-permute-start.31 = (f32[8,1536]{1,0:T(8,128)S(1)}, f32[8,1536]{1,0:T(8,128)}, u32[]{:S(2)}, u32[]{:S(2)}) collective-permute-start(f32[8,1536]{1,0:T(8,128)S(1)} %fusion), channel_id=1, source_target_pairs={{0,22},{1,23},{2,24},{3,25},{4,26},{5,27},{6,28},{7,29},{8,30},{9,... | collective-permute-start | bytes 147464
  1266.6 101.5 %collective-permute-start.37 = (f32[8,1536]{1,0:T(8,128)S(1)}, f32[8,1536]{1,0:T(8,128)}, u32[]{:S(2)}, u32[]{:S(2)}) collective-permute-start(f32[8,1536]{1,0:T(8,128)S(1)} %fusion), channel_id=1, source_target_pairs={{0,28},{1,29},{2,30},{3,31},{4,32},{5,33},{6,34},{7,35},{8,36},{9,... | collective-permute-start | bytes 147464
  1279.7 90.3 %collective-permute-start.38 = (f32[8,1536]{1,0:T(8,128)S(1)}, f32[8,1536]{1,0:T(8,128)}, u32[]{:S(2)}, u32[]{:S(2)}) collective-permute-start(f32[8,1536]{1,0:T(8,128)S(1)} %fusion), channel_id=1, source_target_pairs={{0,29},{1,30},{2,31},{3,32},{4,33},{5,34},{6,35},{7,36},{8,37},{9,... | collective-permute-start | bytes 147464
  1292.9 79.1 %collective-permute-start.39 = (f32[8,1536]{1,0:T(8,128)S(1)}, f32[8,1536]{1,0:T(8,128)}, u32[]{:S(2)}, u32[]{:S(2)}) collective-permute-start(f32[8,1536]{1,0:T(8,128)S(1)} %fusion), channel_id=1, source_target_pairs={{0,30},{1,31},{2,32},{3,33},{4,34},{5,35},{6,36},{7,37},{8,38},{9,... | collective-permute-start | bytes 147464
  1447.1 269.5 %collective-permute-start.8 = (bf16[2,256,1536]{1,2,0:T(8,128)(2,1)}, bf16[2,256,1536]{1,2,0:T(8,128)(2,1)}, u32[]{:S(2)}, u32[]{:S(2)}) collective-permute-start(bf16[2,256,1536]{1,2,0:T(8,128)(2,1)} %pad_maximum_fusion.1), channel_id=1, source_target_pairs={{1,0},{2,1},{3,2},{4,3},{5,4},{6,5},{7,6},{8,7},{9,8},{10,9},{11,1... | collective-permute-start | bytes 4718600 | tf_op jit(solution)/shard_map/ppermute | solution.py:26
  1450.2 268.0 %collective-permute-start.9 = (bf16[2,256,1536]{1,2,0:T(8,128)(2,1)}, bf16[2,256,1536]{1,2,0:T(8,128)(2,1)}, u32[]{:S(2)}, u32[]{:S(2)}) collective-permute-start(bf16[2,256,1536]{1,2,0:T(8,128)(2,1)} %pad_maximum_fusion.2), channel_id=1, source_target_pairs={{0,1},{1,2},{2,3},{3,4},{4,5},{5,6},{6,7},{7,8},{8,9},{9,10},{10,1... | collective-permute-start | bytes 4718600 | tf_op jit(solution)/shard_map/ppermute | solution.py:26
  (209 other events, 12731.1 us)
Sparse Core Ops, SparseCore 0:
  1459.7 255.1 all-reduce.3
where the time goes:
time: 1750 us; the launch traced here: 1730 us
  blocking collectives  622 us (36%)
  starting transfers between devices  603 us (34%)
  local copies, waits for them, and re-layouts  176 us (10%)
  waiting for transfers between devices  172 us (10%)
  other arithmetic  95.4 us (5%)
  matrix products  43.9 us (3%)
  between operations  18.1 us (1%)
    unnamed x1, blocking collectives  622 us
    unnamed x64, starting transfers between devices  549 us
    psum x1, waiting for transfers between devices, per_device(): grad_kernel = lax.psum(jnp.stack(kernel_rows), ('dp', 'seq')) * scale_out  133 us
    unnamed x323, local copies, waits for them, and re-layouts  104 us
    reduce_sum x6, other arithmetic, per_device(): jnp.sum(jnp.where(masks[offset], conv_grad_f * attended_wide[offset:offse...  40.2 us
  transfers between devices with their start and end apart: 75, of which 14 were waited for; matrix products, arithmetic and copies ran while one was open for 12% of the time, Pallas kernels for 0%

commit v1 on v0

v1 whole, which is shorter than its diff:
```python
import functools

import jax
import jax.numpy as jnp
from jax import lax
from jax.experimental import pallas as pl
from jax.experimental.pallas import tpu as pltpu
from jax.sharding import PartitionSpec as P

HD = 64
KW = 31
ROWS = 256
EDGE = 32
CEDGE = 16
QROWS = ROWS + 2 * EDGE
CROWS = ROWS + 2 * CEDGE
WINDOW = 3 * ROWS
WIDTH = 1536
PARTS = 2
PWIDTH = WIDTH // PARTS
LANES = 256
VMEM = 60 * 1024 * 1024
BF = jnp.bfloat16
F32 = jnp.float32
NT = (((1,), (1,)), ((), ()))
TN = (((0,), (0,)), ((), ()))


def half_masks(scale):
    lane = lax.broadcasted_iota(jnp.int32, (1, 2 * HD), 1)
    return [
        jnp.where((lane < HD) == (half == 0), scale, 0.0).astype(BF) for half in range(2)
    ]


def forward_kernel(
    row_ids, key_ids, q_low, q_own, q_high, k_low, k_own, k_high, v_low, v_own, v_high,
    context_ref, context_b_ref, probs_ref, bias,
):
    @pl.when(pl.program_id(0) == 0)
    def _():
        bias[...] = jnp.where(row_ids[...][:, :1] == key_ids[...], 0.0, -1e30)

    scales = half_masks(HD ** -0.5)
    lane = lax.broadcasted_iota(jnp.int32, (1, 2 * HD), 1) < HD
    for pair in range(q_own.shape[1] // (2 * HD)):
        cols = slice(pair * 2 * HD, (pair + 1) * 2 * HD)
        q = jnp.concatenate([q_low[:, cols], q_own[:, cols], q_high[:, cols]], axis=0)
        k = jnp.concatenate([k_low[:, cols], k_own[:, cols], k_high[:, cols]], axis=0)
        v = jnp.concatenate([v_low[:, cols], v_own[:, cols], v_high[:, cols]], axis=0)
        outs = []
        for half in range(2):
            scores = lax.dot_general(q * scales[half], k, NT, preferred_element_type=F32)
            scores = scores + bias[...]
            highest = jnp.max(scores, axis=1, keepdims=True)
            weights = jnp.exp(scores - highest)
            totals = jnp.sum(weights, axis=1, keepdims=True)
            probs = (weights * (1.0 / totals)).astype(BF)
            probs_ref[2 * pair + half] = probs[EDGE : EDGE + ROWS]
            outs.append(jnp.dot(probs, v, preferred_element_type=F32))
        context = jnp.where(lane, outs[0], outs[1])
        context_ref[:, cols] = context[EDGE : EDGE + ROWS]
        context_b_ref[:, cols] = context.astype(BF)


def attention_forward(row_ids, key_ids, q, k, v, width):
    step = 2 * HD
    heads = step // HD
    column = lambda rows: pl.BlockSpec((rows, step), lambda i: (0, i))
    whole = lambda shape: pl.BlockSpec(shape, lambda i: (0, 0))
    return pl.pallas_call(
        forward_kernel,
        grid=(width // step,),
        out_shape=(
            jax.ShapeDtypeStruct((ROWS, width), F32),
            jax.ShapeDtypeStruct((QROWS, width), BF),
            jax.ShapeDtypeStruct((width // HD, ROWS, WINDOW), BF),
        ),
        in_specs=[whole((QROWS, 128)), whole((1, WINDOW)), column(EDGE), column(ROWS), column(EDGE)]
        + [column(ROWS)] * 6,
        out_specs=(
            column(ROWS),
            column(QROWS),
            pl.BlockSpec((heads, ROWS, WINDOW), lambda i: (i, 0, 0)),
        ),
        scratch_shapes=[pltpu.VMEM((QROWS, WINDOW), F32)],
        compiler_params=pltpu.CompilerParams(vmem_limit_bytes=VMEM),
        cost_estimate=pl.CostEstimate(
            flops=8 * QROWS * WINDOW * width, bytes_accessed=20 << 20, transcendentals=0
        ),
        name="attention_forward",
    )(row_ids, key_ids, *q, *k, *v)


def conv_kernel_body(
    ids_ref, context_ref, weight_ref, taps_ref, cot_ref,
    block_ref, grad_ref, taps_grad_ref, context_grad_ref,
    shifted, cgrad, ids, gated, total, taps_acc,
):
    step = pl.program_id(0)

    @pl.when(step == 0)
    def _():
        ids[0] = ids_ref[...]
        for b in range(1, 8):
            ids[b, : QROWS - 8] = ids_ref[b : b + QROWS - 8, :]
        total[...] = jnp.zeros_like(total)

    shifted[0] = (
        jnp.dot(context_ref[...], weight_ref[...], preferred_element_type=F32).astype(BF).astype(F32)
    )
    for b in range(1, 8):
        shifted[b, : QROWS - 8] = shifted[0, b : b + QROWS - 8, :]
    taps_acc[...] = jnp.zeros_like(taps_acc)
    tiles = [slice(j * 128, (j + 1) * 128) for j in range(LANES // 128)]
    block = 32

    def forward_rows(i, carry):
        o = pl.multiple_of(i * block, block)
        own = ids[0, pl.ds(o + CEDGE, block), :]
        sums = [jnp.zeros((block, 128), F32) for _ in tiles]
        for e in range(1, KW + 1):
            a, b = divmod(e, 8)
            same = ids[b, pl.ds(o + 8 * a, block), :] == own
            for j, tile in enumerate(tiles):
                term = shifted[b, pl.ds(o + 8 * a, block), tile] * taps_ref[e - 1 : e, tile]
                sums[j] = sums[j] + jnp.where(same, term, 0.0)
        for j, tile in enumerate(tiles):
            gate = jax.nn.sigmoid(sums[j])
            gated[pl.ds(o, block), tile] = sums[j] * gate
            grad = cot_ref[pl.ds(o, block), tile].astype(F32) * gate * (1.0 + sums[j] * (1.0 - gate))
            cgrad[0, pl.ds(o, block), tile] = grad.astype(BF).astype(F32)
        return carry

    lax.fori_loop(0, CROWS // block, forward_rows, 0)
    block_ref[...] = gated[CEDGE : CEDGE + ROWS].astype(BF)
    for b in range(1, 8):
        cgrad[b, : CROWS - 8] = cgrad[0, b : b + CROWS - 8, :]

    def backward_rows(i, carry):
        s = pl.multiple_of(i * block, block)
        own = ids[0, pl.ds(s + EDGE, block), :]
        grads = [cgrad[0, pl.ds(s + CEDGE, block), tile] for tile in tiles]
        sums = [jnp.zeros((block, 128), F32) for _ in tiles]
        for e in range(1, KW + 1):
            a, b = divmod(e, 8)
            same = ids[b, pl.ds(s + CEDGE + 8 * a, block), :] == own
            for j, tile in enumerate(tiles):
                term = cgrad[b, pl.ds(s + 8 * a, block), tile] * taps_ref[KW - e : KW - e + 1, tile]
                sums[j] = sums[j] + jnp.where(same, term, 0.0)
                pair = grads[j] * shifted[b, pl.ds(s + CEDGE + 8 * a, block), tile]
                pair = jnp.where(same, pair, 0.0)
                taps_acc[e - 1, :, tile] += jnp.sum(pair.reshape(block // 8, 8, 128), axis=0)
        for j, tile in enumerate(tiles):
            grad_ref[pl.ds(s, block), tile] = sums[j].astype(BF)
        return carry

    lax.fori_loop(0, ROWS // block, backward_rows, 0)
    taps_grad_ref[...] = jnp.sum(taps_acc[...], axis=1)
    total[...] += lax.dot_general(grad_ref[...], weight_ref[...], NT, preferred_element_type=F32)

    @pl.when(step == pl.num_programs(0) - 1)
    def _():
        context_grad_ref[...] = total[...].astype(BF)


def conv_chain(row_ids, context_b, out_proj, taps, cot_wide):
    column = lambda rows: pl.BlockSpec((rows, LANES), lambda i: (0, i))
    whole = lambda shape: pl.BlockSpec(shape, lambda i: (0, 0))
    return pl.pallas_call(
        conv_kernel_body,
        grid=(WIDTH // LANES,),
        out_shape=(
            jax.ShapeDtypeStruct((ROWS, WIDTH), BF),
            jax.ShapeDtypeStruct((ROWS, WIDTH), BF),
            jax.ShapeDtypeStruct((KW + 1, WIDTH), F32),
            jax.ShapeDtypeStruct((ROWS, WIDTH), BF),
        ),
        in_specs=[
            whole((QROWS, 128)), whole((QROWS, WIDTH)), column(WIDTH), column(KW + 1), column(CROWS),
        ],
        out_specs=(column(ROWS), column(ROWS), column(KW + 1), whole((ROWS, WIDTH))),
        scratch_shapes=[
            pltpu.VMEM((8, QROWS, LANES), F32),
            pltpu.VMEM((8, CROWS, LANES), F32),
            pltpu.VMEM((8, QROWS, 128), F32),
            pltpu.VMEM((CROWS, LANES), F32),
            pltpu.VMEM((ROWS, WIDTH), F32),
            pltpu.VMEM((KW + 1, 8, LANES), F32),
        ],
        compiler_params=pltpu.CompilerParams(vmem_limit_bytes=VMEM),
        cost_estimate=pl.CostEstimate(flops=20 << 30, bytes_accessed=10 << 20, transcendentals=0),
        name="conv_chain",
    )(row_ids, context_b, out_proj, taps, cot_wide)


def backward_kernel(
    q_own, k_low, k_own, k_high, v_low, v_own, v_high, upstream, context, probs_ref,
    dq_ref, dk_low, dk_own, dk_high, dv_low, dv_own, dv_high,
):
    plain = half_masks(1.0)
    scales = half_masks(HD ** -0.5)
    lane = lax.broadcasted_iota(jnp.int32, (1, 2 * HD), 1) < HD
    for pair in range(q_own.shape[1] // (2 * HD)):
        cols = slice(pair * 2 * HD, (pair + 1) * 2 * HD)
        k = jnp.concatenate([k_low[:, cols], k_own[:, cols], k_high[:, cols]], axis=0)
        v = jnp.concatenate([v_low[:, cols], v_own[:, cols], v_high[:, cols]], axis=0)
        q = q_own[:, cols]
        up = upstream[:, cols]
        products = up.astype(F32) * context[:, cols]
        q_turned = q.astype(F32).T.astype(BF)
        up_turned = up.astype(F32).T.astype(BF)
        dqs, dks, dvs = [], [], []
        for half in range(2):
            rows = slice(half * HD, (half + 1) * HD)
            delta = jnp.sum(
                jnp.where(lane == (half == 0), products, 0.0), axis=1, keepdims=True
            ) * HD ** -0.5
            grads = lax.dot_general(up * scales[half], v, NT, preferred_element_type=F32)
            probs = probs_ref[2 * pair + half]
            score_grad = (probs.astype(F32) * (grads - delta)).astype(BF)
            dqs.append(jnp.dot(score_grad, k, preferred_element_type=F32))
            dks.append(jnp.dot(q_turned[rows], score_grad, preferred_element_type=F32))
            dvs.append(jnp.dot(up_turned[rows], probs, preferred_element_type=F32))
        dq_ref[:, cols] = jnp.where(lane, dqs[0], dqs[1]).astype(BF)
        for parts, low, own, high in ((dks, dk_low, dk_own, dk_high), (dvs, dv_low, dv_own, dv_high)):
            whole = jnp.concatenate(parts, axis=0).T
            low[:, cols] = whole[:ROWS].astype(BF)
            own[:, cols] = whole[ROWS : 2 * ROWS]
            high[:, cols] = whole[2 * ROWS :].astype(BF)


def attention_backward(q, k, v, upstream, context, probs):
    width = upstream.shape[1]
    step = 2 * HD
    heads = step // HD
    column = pl.BlockSpec((ROWS, step), lambda i: (0, i))
    bf = jax.ShapeDtypeStruct((ROWS, width), BF)
    own = jax.ShapeDtypeStruct((ROWS, width), F32)
    return pl.pallas_call(
        backward_kernel,
        grid=(width // step,),
        out_shape=(bf, bf, own, bf, bf, own, bf),
        in_specs=[column] * 9 + [pl.BlockSpec((heads, ROWS, WINDOW), lambda i: (i, 0, 0))],
        out_specs=(column,) * 7,
        compiler_params=pltpu.CompilerParams(vmem_limit_bytes=VMEM),
        cost_estimate=pl.CostEstimate(
            flops=10 * ROWS * WINDOW * width, bytes_accessed=20 << 20, transcendentals=0
        ),
        name="attention_backward",
    )(q, *k, *v, upstream, context, probs)


def product_kernel(mine, theirs, grad_mine, grad_theirs, taps_mine, taps_theirs, *outs):
    taps = (taps_mine[...] + taps_theirs[...]).astype(BF)
    count = outs[0].shape[0] - 8
    for part in range(PARTS):
        cols = slice(part * PWIDTH, (part + 1) * PWIDTH)
        for block in range(4):
            rows = slice(block * count, (block + 1) * count)
            out = outs[4 * part + block]
            out[:count] = (
                jnp.dot(mine[rows], grad_mine[:, cols], preferred_element_type=F32)
                + jnp.dot(theirs[rows], grad_theirs[:, cols], preferred_element_type=F32)
            ).astype(BF)
            out[count:] = taps[8 * block : 8 * block + 8, cols]


def product_blocks(mine, theirs, grad_mine, grad_theirs, taps_mine, taps_theirs):
    shape = jax.ShapeDtypeStruct((mine.shape[0] // 4 + 8, PWIDTH), BF)
    return pl.pallas_call(
        product_kernel,
        out_shape=(shape,) * (4 * PARTS),
        compiler_params=pltpu.CompilerParams(vmem_limit_bytes=VMEM),
        cost_estimate=pl.CostEstimate(flops=2 << 30, bytes_accessed=8 << 20, transcendentals=0),
        name="product_blocks",
    )(mine, theirs, grad_mine, grad_theirs, taps_mine, taps_theirs)


def combine_kernel(sources, pieces, count, *refs):
    ins, outs = refs[:sources], refs[sources : sources + pieces]
    held = refs[-1]
    total = ins[0][...].astype(F32)
    for ref in ins[1:]:
        total = total + ref[...].astype(F32)
    held[...] = total
    rows = count // pieces
    for piece in range(pieces):
        out = outs[piece]
        if out.shape[0] > rows + 8:
            out[...] = jnp.zeros_like(out)
        out[:rows] = held[piece * rows : (piece + 1) * rows].astype(out.dtype)
        out[rows : rows + 8] = held[count : count + 8].astype(out.dtype)


def combine(blocks, count, pieces, out_rows, dtype):
    shape = jax.ShapeDtypeStruct((out_rows, blocks[0].shape[1]), dtype)
    return pl.pallas_call(
        functools.partial(combine_kernel, len(blocks), pieces, count),
        out_shape=(shape,) * pieces,
        scratch_shapes=[pltpu.VMEM(blocks[0].shape, F32)],
        compiler_params=pltpu.CompilerParams(vmem_limit_bytes=VMEM),
        name="combine",
    )(*blocks)


def seq_pairs(shift):
    pairs = []
    for source in range(64):
        z, x, c = source // 8, (source // 2) % 4, source % 2
        tz, tx, tc = shift(z, x, c)
        pairs.append((source, ((tz % 8) * 4 + tx % 4) * 2 + tc))
    return pairs


SWAP = seq_pairs(lambda z, x, c: (z, x, 1 - c))
UP = [(i, i + 1) for i in range(63)]
DOWN = [(i + 1, i) for i in range(63)]


def per_device(query, key, value, segments, out_proj, conv_kernel, cotangent):
    q, k, v, cot = query[0], key[0], value[0], cotangent[0]
    dp = lax.axis_index("dp")
    seq = lax.axis_index("seq")
    z, x, c = seq // 8, (seq // 2) % 4, seq % 2
    own_ids = segments[0] + 1

    id_row = lax.pad(own_ids.astype(BF)[None], jnp.zeros((), BF), ((0, 15, 0), (0, WIDTH - ROWS, 0)))
    up_small = jnp.concatenate([q[ROWS - EDGE :], cot[ROWS - CEDGE :], id_row], axis=0)
    down_small = jnp.concatenate([q[:EDGE], cot[:CEDGE], id_row], axis=0)
    low_small = lax.ppermute(up_small, "seq", UP)
    high_small = lax.ppermute(down_small, "seq", DOWN)
    k_low = lax.ppermute(k, "seq", UP)
    k_high = lax.ppermute(k, "seq", DOWN)
    v_low = lax.ppermute(v, "seq", UP)
    v_high = lax.ppermute(v, "seq", DOWN)
    ids = jnp.concatenate(
        [
            low_small[EDGE + CEDGE, :ROWS].astype(F32),
            own_ids.astype(F32),
            high_small[EDGE + CEDGE, :ROWS].astype(F32),
        ]
    )
    row_ids = jnp.broadcast_to(ids[ROWS - EDGE : 2 * ROWS + EDGE, None], (QROWS, 128))
    key_ids = ids[None]
    cot_wide = jnp.concatenate(
        [low_small[EDGE : EDGE + CEDGE], cot, high_small[EDGE : EDGE + CEDGE]], axis=0
    )
    taps = lax.pad(conv_kernel.astype(F32), jnp.zeros((), F32), ((0, 1, 0), (0, 0, 0)))

    keys = (k_low, k, k_high)
    values = (v_low, v, v_high)
    context, context_b, probs = attention_forward(
        row_ids, key_ids, (low_small[:EDGE], q, high_small[:EDGE]), keys, values, WIDTH
    )

    place = lax.broadcasted_iota(jnp.int32, (WIDTH, 1), 0)
    tc = (place // 768) ^ c
    ty = (place // 192 + dp) % 4
    tx = (place // 48 + x) % 4
    tz = (place // 6 + z) % 8
    target = 6 * (64 * ty + 8 * tz + 2 * tx + tc) + place % 6
    chosen = (target == lax.broadcasted_iota(jnp.int32, (1, WIDTH), 1)).astype(BF)
    own_context = context_b[EDGE : EDGE + ROWS]
    half = WIDTH // 2
    sent = lax.dot_general(chosen[half:], own_context, NT, preferred_element_type=F32).astype(BF)
    mine = lax.dot_general(chosen[:half], own_context, NT, preferred_element_type=F32).astype(BF)
    theirs = lax.ppermute(sent, "seq", SWAP)

    block_out, attended_grad, taps_grad, context_grad = conv_chain(
        row_ids, context_b, out_proj, taps, cot_wide
    )
    taps_grad = jnp.roll(taps_grad, -8 * dp, axis=0)
    grad_theirs = lax.ppermute(attended_grad, "seq", SWAP)
    taps_theirs = lax.ppermute(taps_grad, "seq", SWAP)
    blocks = product_blocks(mine, theirs, attended_grad, grad_theirs, taps_grad, taps_theirs)

    weight_parts, taps_parts = [], []
    scale_out = (4 * 64 * ROWS) ** (-0.5)
    for part in range(PARTS):
        held = blocks[4 * part : 4 * part + 4]
        got = [
            lax.ppermute(held[n], "dp", [(i, (i + n) % 4) for i in range(4)]) for n in (1, 2, 3)
        ]
        held = combine([held[0]] + got, 192, 4, 56, BF)
        got = [
            lax.ppermute(held[n], "seq", seq_pairs(lambda z, x, c: (z, x + n, c))) for n in (1, 2, 3)
        ]
        held = combine([held[0]] + got, 48, 8, 16, BF)
        got = [
            lax.ppermute(held[n], "seq", seq_pairs(lambda z, x, c: (z + n, x, c)))
            for n in range(1, 8)
        ]
        (last,) = combine([held[0]] + got, 6, 1, 16, F32)
        weight_parts.append(last[:6])
        taps_parts.append(last[6:14])
    grad_out_proj = jnp.concatenate(weight_parts, axis=1) * scale_out
    taps_rows = jnp.concatenate(taps_parts, axis=1) * scale_out
    others = [
        lax.ppermute(taps_rows, "dp", [(i, (i - n) % 4) for i in range(4)]) for n in (1, 2, 3)
    ]
    ring = jnp.concatenate([taps_rows] + others, axis=0)
    grad_kernel = jnp.roll(ring, 8 * dp, axis=0)[:KW]

    dq, dk_low, dk_own, dk_high, dv_low, dv_own, dv_high = attention_backward(
        q, keys, values, context_grad, context, probs
    )
    dk_later = lax.ppermute(dk_low, "seq", DOWN)
    dk_earlier = lax.ppermute(dk_high, "seq", UP)
    dv_later = lax.ppermute(dv_low, "seq", DOWN)
    dv_earlier = lax.ppermute(dv_high, "seq", UP)
    dk = (dk_own + dk_later.astype(F32) + dk_earlier.astype(F32)).astype(BF)
    dv = (dv_own + dv_later.astype(F32) + dv_earlier.astype(F32)).astype(BF)
    return (block_out[None], dq[None], dk[None], dv[None], grad_kernel, grad_out_proj)


def solution(mesh):
    in_specs = (
        P("dp", "seq", None),
        P("dp", "seq", None),
        P("dp", "seq", None),
        P("dp", "seq"),
        P(),
        P(),
        P("dp", "seq", None),
    )
    out_specs = (
        P("dp", "seq", None),
        P("dp", "seq", None),
        P("dp", "seq", None),
        P("dp", "seq", None),
        P(),
        P(("dp", "seq"), None),
    )
    return jax.shard_map(
        per_device, mesh=mesh, in_specs=in_specs, out_specs=out_specs, check_vma=False
    )
```

time: 1750 us -> 235 us (0.13)
  the two profiles are of different devices: /device:TPU:31 before, /device:TPU:32 now
where the time goes in v1:
time: 235 us; the launch traced here: 232 us
  starting transfers between devices  98 us (42%)
  Pallas kernels  85.9 us (37%)
  waiting for transfers between devices  20.1 us (9%)
  other arithmetic  12.3 us (5%)
  local copies, waits for them, and re-layouts  10.8 us (5%)
  matrix products  3.96 us (2%)
    ppermute x14, starting transfers between devices, per_device(): lax.ppermute(held[n], 'seq', seq_pairs(lambda z, x, c: (z + n, x, c)))  35.8 us
    pallas_call x1, Pallas kernels, conv_chain(): pl.pallas_call(conv_kernel_body, grid=(WIDTH // LANES,), out_shape=(jax.S...  35.1 us
    pallas_call x1, Pallas kernels, attention_forward(): pl.pallas_call(forward_kernel, grid=(width // step,), out_shape=(jax.Shap...  18.6 us
    pallas_call x1, Pallas kernels, attention_backward(): pl.pallas_call(backward_kernel, grid=(width // step,), out_shape=(bf, bf,...  17.1 us
    ppermute x6, starting transfers between devices, per_device(): lax.ppermute(held[n], 'dp', [(i, (i + n) % 4) for i in range(4)])  11.9 us
    ppermute x6, starting transfers between devices, per_device(): lax.ppermute(held[n], 'seq', seq_pairs(lambda z, x, c: (z, x + n, c)))  11.8 us
    pallas_call x6, Pallas kernels, combine(): pl.pallas_call(functools.partial(combine_kernel, len(blocks), pieces, cou...  10.7 us
    ppermute x6, waiting for transfers between devices, per_device(): lax.ppermute(held[n], 'dp', [(i, (i + n) % 4) for i in range(4)])  9.16 us
  transfers between devices with their start and end apart: 42, of which 8 were waited for; matrix products, arithmetic and copies ran while one was open for 10% of the time, Pallas kernels for 13%

profile of v1, /device:TPU:32, one launch (start us, length us, event | category | flops | bytes accessed | tf_op | source)
XLA Modules:
  0.0 232.3 jit_solution(14982495747500099076)
XLA Ops:
  2.6 5.8 %collective-permute-start.3 = (bf16[256,1536]{1,0:T(8,128)(2,1)}, bf16[256,1536]{1,0:T(8,128)(2,1)}, u32[]{:S(2)}, u32[]{:S(2)}) collective-permute-start(bf16[256,1536]{1,0:T(8,128)(2,1)} %bitcast.25), channel_id=1, source_target_pairs={{1,0},{2,1},{3,2},{4,3},{5,4},{6,5},{7,6},{8,7},{9,8},{10,9},{11,1... | collective-permute-start | bytes 2359304 | tf_op jit(solution)/shard_map/ppermute | solution.py:334
  10.3 5.8 %collective-permute-start.5 = (bf16[256,1536]{1,0:T(8,128)(2,1)}, bf16[256,1536]{1,0:T(8,128)(2,1)}, u32[]{:S(2)}, u32[]{:S(2)}) collective-permute-start(bf16[256,1536]{1,0:T(8,128)(2,1)} %bitcast.29), channel_id=1, source_target_pairs={{1,0},{2,1},{3,2},{4,3},{5,4},{6,5},{7,6},{8,7},{9,8},{10,9},{11,1... | collective-permute-start | bytes 2359304 | tf_op jit(solution)/shard_map/ppermute | solution.py:336
  24.1 3.7 %collective-permute-done = bf16[64,1536]{1,0:T(8,128)(2,1)} collective-permute-done((bf16[64,1536]{1,0:T(8,128)(2,1)S(1)}, bf16[64,1536]{1,0:T(8,128)(2,1)}, u32[]{:S(2)}, u32[]{:S(2)}) %collective-permute-start) | collective-permute-done | bytes 196640 | tf_op jit(solution)/shard_map/ppermute | solution.py:331
  30.5 2.5 %collective-permute-done.1 = bf16[64,1536]{1,0:T(8,128)(2,1)S(1)} collective-permute-done((bf16[64,1536]{1,0:T(8,128)(2,1)S(1)}, bf16[64,1536]{1,0:T(8,128)(2,1)S(1)}, u32[]{:S(2)}, u32[]{:S(2)}) %collective-permute-start.1) | collective-permute-done | bytes 196640 | tf_op jit(solution)/shard_map/ppermute | solution.py:332
  38.4 18.6 %attention_forward.1 = (f32[256,1536]{1,0:T(8,128)}, bf16[320,1536]{1,0:T(8,128)(2,1)}, bf16[24,256,768]{2,1,0:T(8,128)(2,1)}) custom-call(f32[320,128]{1,0:T(8,128)} %broadcast_in_dim.22.row_ids.ids_ref, f32[1,768]{1,0:T(1,128)} %broadcast_in_dim.23.key_ids, bf16[32,1536]{1,0:T(8,128)(2,1)} %slice.94.q_low, bf16[256,1536]{1,0:T(8,128)(2,1)} %bitcast.21, ...), custom_call_target="tpu_custom_call" | custom-call | flops 3019898880 | bytes 20971520 | tf_op jit(solution)/shard_map/attention_forward/pallas_call | solution.py:71
  57.0 35.1 %conv_chain.1 = (bf16[256,1536]{1,0:T(8,128)(2,1)}, bf16[256,1536]{1,0:T(8,128)(2,1)}, f32[32,1536]{1,0:T(8,128)}, bf16[256,1536]{1,0:T(8,128)(2,1)}) custom-call(f32[320,128]{1,0:T(8,128)} %broadcast_in_dim.22.row_ids.ids_ref, bf16[320,1536]{1,0:T(8,128)(2,1)} %get-tuple-element.53.context_ref, bf16[1536,1536]{1,0:T(8,128)(2,1)} %weight_ref.1, ...), custom_call_target="tpu_custom_call" | custom-call | flops 21474836480 | bytes 10485760 | tf_op jit(solution)/shard_map/conv_chain/pallas_call | solution.py:170
  92.2 17.1 %attention_backward.1 = (bf16[256,1536]{1,0:T(8,128)(2,1)}, bf16[256,1536]{1,0:T(8,128)(2,1)}, f32[256,1536]{1,0:T(8,128)}, bf16[256,1536]{1,0:T(8,128)(2,1)}, b...) custom-call(bf16[256,1536]{1,0:T(8,128)(2,1)} %bitcast.22, ...), custom_call_target="tpu_custom_call" | custom-call | flops 3019898880 | bytes 20971520 | tf_op jit(solution)/shard_map/attention_backward/pallas_call | solution.py:240
  109.3 5.9 %collective-permute-start.8 = (bf16[256,1536]{1,0:T(8,128)(2,1)}, bf16[256,1536]{1,0:T(8,128)(2,1)S(1)}, u32[]{:S(2)}, u32[]{:S(2)}) collective-permute-start(bf16[256,1536]{1,0:T(8,128)(2,1)} %get-tuple-element.63), channel_id=1, source_target_pairs={{1,0},{2,1},{3,2},{4,3},{5,4},{6,5},{7,6},{8,7},{9,8},{10,9},{11,1... | collective-permute-start | bytes 2359304 | tf_op jit(solution)/shard_map/ppermute | solution.py:410
  122.9 4.5 %product_blocks.1 = (bf16[200,768]{1,0:T(8,128)(2,1)}, bf16[200,768]{1,0:T(8,128)(2,1)}, bf16[200,768]{1,0:T(8,128)(2,1)}, bf16[200,768]{1,0:T(8,128)(2,1)}, bf1...) custom-call(bf16[768,256]{1,0:T(8,128)(2,1)} %fusion.4.mine, ...), custom_call_target="tpu_custom_call" | custom-call | flops 2147483648 | bytes 8388608 | tf_op jit(solution)/shard_map/product_blocks/pallas_call | solution.py:271
  128.9 5.5 %collective-permute-start.6 = (bf16[256,1536]{1,0:T(8,128)(2,1)}, bf16[256,1536]{1,0:T(8,128)(2,1)S(1)}, u32[]{:S(2)}, u32[]{:S(2)}) collective-permute-start(bf16[256,1536]{1,0:T(8,128)(2,1)} %get-tuple-element.60), channel_id=1, source_target_pairs={{1,0},{2,1},{3,2},{4,3},{5,4},{6,5},{7,6},{8,7},{9,8},{10,9},{11,1... | collective-permute-start | bytes 2359304 | tf_op jit(solution)/shard_map/ppermute | solution.py:408
  134.4 3.0 %collective-permute-start.14 = (bf16[200,768]{1,0:T(8,128)(2,1)}, bf16[200,768]{1,0:T(8,128)(2,1)S(1)}, u32[]{:S(2)}, u32[]{:S(2)}) collective-permute-start(bf16[200,768]{1,0:T(8,128)(2,1)} %get-tuple-element.69), channel_id=1, source_target_pairs={{0,128},{64,192},{128,0},{192,64},{1,129},{65,193},{129,1},{193,65... | collective-permute-start | bytes 921608 | tf_op jit(solution)/shard_map/ppermute | solution.py:383
  141.4 5.3 %collective-permute-done.14.refs_2_ = bf16[200,768]{1,0:T(8,128)(2,1)S(1)} collective-permute-done((bf16[200,768]{1,0:T(8,128)(2,1)}, bf16[200,768]{1,0:T(8,128)(2,1)S(1)}, u32[]{:S(2)}, u32[]{:S(2)}) %collective-permute-start.14) | collective-permute-done | bytes 307232 | tf_op jit(solution)/shard_map/ppermute | solution.py:383
  146.8 2.5 %collective-permute-start.27 = (bf16[200,768]{1,0:T(8,128)(2,1)}, bf16[200,768]{1,0:T(8,128)(2,1)}, u32[]{:S(2)}, u32[]{:S(2)}) collective-permute-start(bf16[200,768]{1,0:T(8,128)(2,1)} %get-tuple-element.85), channel_id=1, source_target_pairs={{0,128},{64,192},{128,0},{192,64},{1,129},{65,193},{129,1},{193,65... | collective-permute-start | bytes 921608 | tf_op jit(solution)/shard_map/ppermute | solution.py:383
  151.2 2.7 %collective-permute-start.28 = (bf16[200,768]{1,0:T(8,128)(2,1)}, bf16[200,768]{1,0:T(8,128)(2,1)}, u32[]{:S(2)}, u32[]{:S(2)}) collective-permute-start(bf16[200,768]{1,0:T(8,128)(2,1)} %get-tuple-element.86), channel_id=1, source_target_pairs={{0,192},{64,0},{128,64},{192,128},{1,193},{65,1},{129,65},{193,129... | collective-permute-start | bytes 921608 | tf_op jit(solution)/shard_map/ppermute | solution.py:383
  161.5 4.0 %collective-permute-start.18 = (bf16[56,768]{1,0:T(8,128)(2,1)}, bf16[56,768]{1,0:T(8,128)(2,1)S(1)}, u32[]{:S(2)}, u32[]{:S(2)}) collective-permute-start(bf16[56,768]{1,0:T(8,128)(2,1)} %get-tuple-element.74), channel_id=1, source_target_pairs={{0,6},{1,7},{2,0},{3,1},{4,2},{5,3},{6,4},{7,5},{8,14},{9,15},{10,... | collective-permute-start | bytes 258056 | tf_op jit(solution)/shard_map/ppermute | solution.py:387
  169.1 2.8 %collective-permute-start.31 = (bf16[56,768]{1,0:T(8,128)(2,1)}, bf16[56,768]{1,0:T(8,128)(2,1)S(1)}, u32[]{:S(2)}, u32[]{:S(2)}) collective-permute-start(bf16[56,768]{1,0:T(8,128)(2,1)} %get-tuple-element.90), channel_id=1, source_target_pairs={{0,6},{1,7},{2,0},{3,1},{4,2},{5,3},{6,4},{7,5},{8,14},{9,15},{10,... | collective-permute-start | bytes 258056 | tf_op jit(solution)/shard_map/ppermute | solution.py:387
  175.6 9.8 %collective-permute-start.20 = (bf16[16,768]{1,0:T(8,128)(2,1)}, bf16[16,768]{1,0:T(8,128)(2,1)S(1)}, u32[]{:S(2)}, u32[]{:S(2)}) collective-permute-start(bf16[16,768]{1,0:T(8,128)(2,1)} %get-tuple-element.77), channel_id=1, source_target_pairs={{0,16},{1,17},{2,18},{3,19},{4,20},{5,21},{6,22},{7,23},{8,24},{9,... | collective-permute-start | bytes 73736 | tf_op jit(solution)/shard_map/ppermute | solution.py:391
  186.6 2.6 %collective-permute-start.22 = (bf16[16,768]{1,0:T(8,128)(2,1)}, bf16[16,768]{1,0:T(8,128)(2,1)S(1)}, u32[]{:S(2)}, u32[]{:S(2)}) collective-permute-start(bf16[16,768]{1,0:T(8,128)(2,1)} %get-tuple-element.79), channel_id=1, source_target_pairs={{0,32},{1,33},{2,34},{3,35},{4,36},{5,37},{6,38},{7,39},{8,40},{9,... | collective-permute-start | bytes 73736 | tf_op jit(solution)/shard_map/ppermute | solution.py:391
  190.9 2.6 %collective-permute-start.23 = (bf16[16,768]{1,0:T(8,128)(2,1)}, bf16[16,768]{1,0:T(8,128)(2,1)S(1)}, u32[]{:S(2)}, u32[]{:S(2)}) collective-permute-start(bf16[16,768]{1,0:T(8,128)(2,1)} %get-tuple-element.80), channel_id=1, source_target_pairs={{0,40},{1,41},{2,42},{3,43},{4,44},{5,45},{6,46},{7,47},{8,48},{9,... | collective-permute-start | bytes 73736 | tf_op jit(solution)/shard_map/ppermute | solution.py:391
  194.7 4.2 %collective-permute-start.25 = (bf16[16,768]{1,0:T(8,128)(2,1)}, bf16[16,768]{1,0:T(8,128)(2,1)S(1)}, u32[]{:S(2)}, u32[]{:S(2)}) collective-permute-start(bf16[16,768]{1,0:T(8,128)(2,1)} %get-tuple-element.82), channel_id=1, source_target_pairs={{0,56},{1,57},{2,58},{3,59},{4,60},{5,61},{6,62},{7,63},{8,0},{9,1... | collective-permute-start | bytes 73736 | tf_op jit(solution)/shard_map/ppermute | solution.py:391
  202.2 2.4 %collective-permute-start.34 = (bf16[16,768]{1,0:T(8,128)(2,1)S(1)}, bf16[16,768]{1,0:T(8,128)(2,1)S(1)}, u32[]{:S(2)}, u32[]{:S(2)}) collective-permute-start(bf16[16,768]{1,0:T(8,128)(2,1)S(1)} %copy-done.35), channel_id=1, source_target_pairs={{0,24},{1,25},{2,26},{3,27},{4,28},{5,29},{6,30},{7,31},{8,32},{9,... | collective-permute-start | bytes 73736 | tf_op jit(solution)/shard_map/ppermute | solution.py:391
  204.6 3.6 %collective-permute-start.35 = (bf16[16,768]{1,0:T(8,128)(2,1)S(1)}, bf16[16,768]{1,0:T(8,128)(2,1)S(1)}, u32[]{:S(2)}, u32[]{:S(2)}) collective-permute-start(bf16[16,768]{1,0:T(8,128)(2,1)S(1)} %copy-done.34), channel_id=1, source_target_pairs={{0,32},{1,33},{2,34},{3,35},{4,36},{5,37},{6,38},{7,39},{8,40},{9,... | collective-permute-start | bytes 73736 | tf_op jit(solution)/shard_map/ppermute | solution.py:391
  208.2 4.0 %collective-permute-start.36 = (bf16[16,768]{1,0:T(8,128)(2,1)S(1)}, bf16[16,768]{1,0:T(8,128)(2,1)S(1)}, u32[]{:S(2)}, u32[]{:S(2)}) collective-permute-start(bf16[16,768]{1,0:T(8,128)(2,1)S(1)} %copy-done.33), channel_id=1, source_target_pairs={{0,40},{1,41},{2,42},{3,43},{4,44},{5,45},{6,46},{7,47},{8,48},{9,... | collective-permute-start | bytes 73736 | tf_op jit(solution)/shard_map/ppermute | solution.py:391
  227.1 2.8 %collective-permute-done.40 = f32[8,1536]{1,0:T(8,128)S(1)} collective-permute-done((f32[8,1536]{1,0:T(8,128)S(1)}, f32[8,1536]{1,0:T(8,128)S(1)}, u32[]{:S(2)}, u32[]{:S(2)}) %collective-permute-start.40) | collective-permute-done | bytes 49184 | tf_op jit(solution)/shard_map/ppermute | solution.py:400
  (174 shorter events, 74.6 us)
Async XLA Ops:
  0.6 37.0 %collective-permute-start.2 = (bf16[256,1536]{1,0:T(8,128)(2,1)}, bf16[256,1536]{1,0:T(8,128)(2,1)}, u32[]{:S(2)}, u32[]{:S(2)}) collective-permute-start(bf16[256,1536]{1,0:T(8,128)(2,1)} %bitcast.24), channel_id=1, source_target_pairs={{0,1},{1,2},{2,3},{3,4},{4,5},{5,6},{6,7},{7,8},{8,9},{9,10},{10,1... | collective-permute-start | bytes 2359304 | tf_op jit(solution)/shard_map/ppermute | solution.py:333
  2.6 35.1 %collective-permute-start.3 = (bf16[256,1536]{1,0:T(8,128)(2,1)}, bf16[256,1536]{1,0:T(8,128)(2,1)}, u32[]{:S(2)}, u32[]{:S(2)}) collective-permute-start(bf16[256,1536]{1,0:T(8,128)(2,1)} %bitcast.25), channel_id=1, source_target_pairs={{1,0},{2,1},{3,2},{4,3},{5,4},{6,5},{7,6},{8,7},{9,8},{10,9},{11,1... | collective-permute-start | bytes 2359304 | tf_op jit(solution)/shard_map/ppermute | solution.py:334
  8.3 29.3 %collective-permute-start.4 = (bf16[256,1536]{1,0:T(8,128)(2,1)}, bf16[256,1536]{1,0:T(8,128)(2,1)}, u32[]{:S(2)}, u32[]{:S(2)}) collective-permute-start(bf16[256,1536]{1,0:T(8,128)(2,1)} %bitcast.28), channel_id=1, source_target_pairs={{0,1},{1,2},{2,3},{3,4},{4,5},{5,6},{6,7},{7,8},{8,9},{9,10},{10,1... | collective-permute-start | bytes 2359304 | tf_op jit(solution)/shard_map/ppermute | solution.py:335
  10.3 27.4 %collective-permute-start.5 = (bf16[256,1536]{1,0:T(8,128)(2,1)}, bf16[256,1536]{1,0:T(8,128)(2,1)}, u32[]{:S(2)}, u32[]{:S(2)}) collective-permute-start(bf16[256,1536]{1,0:T(8,128)(2,1)} %bitcast.29), channel_id=1, source_target_pairs={{1,0},{2,1},{3,2},{4,3},{5,4},{6,5},{7,6},{8,7},{9,8},{10,9},{11,1... | collective-permute-start | bytes 2359304 | tf_op jit(solution)/shard_map/ppermute | solution.py:336
  92.1 29.9 %collective-permute-start.11 = (bf16[256,1536]{1,0:T(8,128)(2,1)}, bf16[256,1536]{1,0:T(8,128)(2,1)}, u32[]{:S(2)}, u32[]{:S(2)}) collective-permute-start(bf16[256,1536]{1,0:T(8,128)(2,1)} %get-tuple-element.65.grad_mine), channel_id=1, source_target_pairs={{0,1},{1,0},{2,3},{3,2},{4,5},{5,4},{6,7},{7,6},{8,9},{9,8},{10,11... | collective-permute-start | bytes 2359304 | tf_op jit(solution)/shard_map/ppermute | solution.py:374
  109.3 28.1 %collective-permute-start.8 = (bf16[256,1536]{1,0:T(8,128)(2,1)}, bf16[256,1536]{1,0:T(8,128)(2,1)S(1)}, u32[]{:S(2)}, u32[]{:S(2)}) collective-permute-start(bf16[256,1536]{1,0:T(8,128)(2,1)} %get-tuple-element.63), channel_id=1, source_target_pairs={{1,0},{2,1},{3,2},{4,3},{5,4},{6,5},{7,6},{8,7},{9,8},{10,9},{11,1... | collective-permute-start | bytes 2359304 | tf_op jit(solution)/shard_map/ppermute | solution.py:410
  115.3 23.5 %collective-permute-start.9 = (bf16[256,1536]{1,0:T(8,128)(2,1)}, bf16[256,1536]{1,0:T(8,128)(2,1)}, u32[]{:S(2)}, u32[]{:S(2)}) collective-permute-start(bf16[256,1536]{1,0:T(8,128)(2,1)} %get-tuple-element.64), channel_id=1, source_target_pairs={{0,1},{1,2},{2,3},{3,4},{4,5},{5,6},{6,7},{7,8},{8,9},{9,10},{10,1... | collective-permute-start | bytes 2359304 | tf_op jit(solution)/shard_map/ppermute | solution.py:411
  127.4 13.3 %collective-permute-start.13 = (bf16[200,768]{1,0:T(8,128)(2,1)}, bf16[200,768]{1,0:T(8,128)(2,1)S(1)}, u32[]{:S(2)}, u32[]{:S(2)}) collective-permute-start(bf16[200,768]{1,0:T(8,128)(2,1)} %get-tuple-element.68), channel_id=1, source_target_pairs={{0,64},{64,128},{128,192},{192,0},{1,65},{65,129},{129,193},{193,1... | collective-permute-start | bytes 921608 | tf_op jit(solution)/shard_map/ppermute | solution.py:383
  128.9 44.7 %collective-permute-start.6 = (bf16[256,1536]{1,0:T(8,128)(2,1)}, bf16[256,1536]{1,0:T(8,128)(2,1)S(1)}, u32[]{:S(2)}, u32[]{:S(2)}) collective-permute-start(bf16[256,1536]{1,0:T(8,128)(2,1)} %get-tuple-element.60), channel_id=1, source_target_pairs={{1,0},{2,1},{3,2},{4,3},{5,4},{6,5},{7,6},{8,7},{9,8},{10,9},{11,1... | collective-permute-start | bytes 2359304 | tf_op jit(solution)/shard_map/ppermute | solution.py:408
  134.4 12.4 %collective-permute-start.14 = (bf16[200,768]{1,0:T(8,128)(2,1)}, bf16[200,768]{1,0:T(8,128)(2,1)S(1)}, u32[]{:S(2)}, u32[]{:S(2)}) collective-permute-start(bf16[200,768]{1,0:T(8,128)(2,1)} %get-tuple-element.69), channel_id=1, source_target_pairs={{0,128},{64,192},{128,0},{192,64},{1,129},{65,193},{129,1},{193,65... | collective-permute-start | bytes 921608 | tf_op jit(solution)/shard_map/ppermute | solution.py:383
  137.4 13.8 %collective-permute-start.15 = (bf16[200,768]{1,0:T(8,128)(2,1)}, bf16[200,768]{1,0:T(8,128)(2,1)S(1)}, u32[]{:S(2)}, u32[]{:S(2)}) collective-permute-start(bf16[200,768]{1,0:T(8,128)(2,1)} %get-tuple-element.70), channel_id=1, source_target_pairs={{0,192},{64,0},{128,64},{192,128},{1,193},{65,1},{129,65},{193,129... | collective-permute-start | bytes 921608 | tf_op jit(solution)/shard_map/ppermute | solution.py:383
  138.7 52.2 %collective-permute-start.7 = (bf16[256,1536]{1,0:T(8,128)(2,1)}, bf16[256,1536]{1,0:T(8,128)(2,1)}, u32[]{:S(2)}, u32[]{:S(2)}) collective-permute-start(bf16[256,1536]{1,0:T(8,128)(2,1)} %get-tuple-element.61), channel_id=1, source_target_pairs={{0,1},{1,2},{2,3},{3,4},{4,5},{5,6},{6,7},{7,8},{8,9},{9,10},{10,1... | collective-permute-start | bytes 2359304 | tf_op jit(solution)/shard_map/ppermute | solution.py:409
  140.7 15.4 %collective-permute-start.26 = (bf16[200,768]{1,0:T(8,128)(2,1)}, bf16[200,768]{1,0:T(8,128)(2,1)S(1)}, u32[]{:S(2)}, u32[]{:S(2)}) collective-permute-start(bf16[200,768]{1,0:T(8,128)(2,1)} %get-tuple-element.84), channel_id=1, source_target_pairs={{0,64},{64,128},{128,192},{192,0},{1,65},{65,129},{129,193},{193,1... | collective-permute-start | bytes 921608 | tf_op jit(solution)/shard_map/ppermute | solution.py:383
  167.6 17.8 %collective-permute-start.30 = (bf16[56,768]{1,0:T(8,128)(2,1)}, bf16[56,768]{1,0:T(8,128)(2,1)S(1)}, u32[]{:S(2)}, u32[]{:S(2)}) collective-permute-start(bf16[56,768]{1,0:T(8,128)(2,1)} %get-tuple-element.89), channel_id=1, source_target_pairs={{0,4},{1,5},{2,6},{3,7},{4,0},{5,1},{6,2},{7,3},{8,12},{9,13},{10,... | collective-permute-start | bytes 258056 | tf_op jit(solution)/shard_map/ppermute | solution.py:387
  169.1 17.5 %collective-permute-start.31 = (bf16[56,768]{1,0:T(8,128)(2,1)}, bf16[56,768]{1,0:T(8,128)(2,1)S(1)}, u32[]{:S(2)}, u32[]{:S(2)}) collective-permute-start(bf16[56,768]{1,0:T(8,128)(2,1)} %get-tuple-element.90), channel_id=1, source_target_pairs={{0,6},{1,7},{2,0},{3,1},{4,2},{5,3},{6,4},{7,5},{8,14},{9,15},{10,... | collective-permute-start | bytes 258056 | tf_op jit(solution)/shard_map/ppermute | solution.py:387
  173.6 19.9 %collective-permute-start.19 = (bf16[16,768]{1,0:T(8,128)(2,1)}, bf16[16,768]{1,0:T(8,128)(2,1)S(1)}, u32[]{:S(2)}, u32[]{:S(2)}) collective-permute-start(bf16[16,768]{1,0:T(8,128)(2,1)} %get-tuple-element.76), channel_id=1, source_target_pairs={{0,8},{1,9},{2,10},{3,11},{4,12},{5,13},{6,14},{7,15},{8,16},{9,17... | collective-permute-start | bytes 73736 | tf_op jit(solution)/shard_map/ppermute | solution.py:391
  175.6 19.1 %collective-permute-start.20 = (bf16[16,768]{1,0:T(8,128)(2,1)}, bf16[16,768]{1,0:T(8,128)(2,1)S(1)}, u32[]{:S(2)}, u32[]{:S(2)}) collective-permute-start(bf16[16,768]{1,0:T(8,128)(2,1)} %get-tuple-element.77), channel_id=1, source_target_pairs={{0,16},{1,17},{2,18},{3,19},{4,20},{5,21},{6,22},{7,23},{8,24},{9,... | collective-permute-start | bytes 73736 | tf_op jit(solution)/shard_map/ppermute | solution.py:391
  185.4 13.5 %collective-permute-start.21 = (bf16[16,768]{1,0:T(8,128)(2,1)}, bf16[16,768]{1,0:T(8,128)(2,1)S(1)}, u32[]{:S(2)}, u32[]{:S(2)}) collective-permute-start(bf16[16,768]{1,0:T(8,128)(2,1)} %get-tuple-element.78), channel_id=1, source_target_pairs={{0,24},{1,25},{2,26},{3,27},{4,28},{5,29},{6,30},{7,31},{8,32},{9,... | collective-permute-start | bytes 73736 | tf_op jit(solution)/shard_map/ppermute | solution.py:391
  186.6 12.4 %collective-permute-start.22 = (bf16[16,768]{1,0:T(8,128)(2,1)}, bf16[16,768]{1,0:T(8,128)(2,1)S(1)}, u32[]{:S(2)}, u32[]{:S(2)}) collective-permute-start(bf16[16,768]{1,0:T(8,128)(2,1)} %get-tuple-element.79), channel_id=1, source_target_pairs={{0,32},{1,33},{2,34},{3,35},{4,36},{5,37},{6,38},{7,39},{8,40},{9,... | collective-permute-start | bytes 73736 | tf_op jit(solution)/shard_map/ppermute | solution.py:391
  194.7 13.4 %collective-permute-start.25 = (bf16[16,768]{1,0:T(8,128)(2,1)}, bf16[16,768]{1,0:T(8,128)(2,1)S(1)}, u32[]{:S(2)}, u32[]{:S(2)}) collective-permute-start(bf16[16,768]{1,0:T(8,128)(2,1)} %get-tuple-element.82), channel_id=1, source_target_pairs={{0,56},{1,57},{2,58},{3,59},{4,60},{5,61},{6,62},{7,63},{8,0},{9,1... | collective-permute-start | bytes 73736 | tf_op jit(solution)/shard_map/ppermute | solution.py:391
  199.0 13.2 %collective-permute-start.32 = (bf16[16,768]{1,0:T(8,128)(2,1)}, bf16[16,768]{1,0:T(8,128)(2,1)S(1)}, u32[]{:S(2)}, u32[]{:S(2)}) collective-permute-start(bf16[16,768]{1,0:T(8,128)(2,1)} %get-tuple-element.92), channel_id=1, source_target_pairs={{0,8},{1,9},{2,10},{3,11},{4,12},{5,13},{6,14},{7,15},{8,16},{9,17... | collective-permute-start | bytes 73736 | tf_op jit(solution)/shard_map/ppermute | solution.py:391
  199.0 13.5 %collective-permute-start.33 = (bf16[16,768]{1,0:T(8,128)(2,1)}, bf16[16,768]{1,0:T(8,128)(2,1)S(1)}, u32[]{:S(2)}, u32[]{:S(2)}) collective-permute-start(bf16[16,768]{1,0:T(8,128)(2,1)} %get-tuple-element.93), channel_id=1, source_target_pairs={{0,16},{1,17},{2,18},{3,19},{4,20},{5,21},{6,22},{7,23},{8,24},{9,... | collective-permute-start | bytes 73736 | tf_op jit(solution)/shard_map/ppermute | solution.py:391
  202.2 17.0 %collective-permute-start.34 = (bf16[16,768]{1,0:T(8,128)(2,1)S(1)}, bf16[16,768]{1,0:T(8,128)(2,1)S(1)}, u32[]{:S(2)}, u32[]{:S(2)}) collective-permute-start(bf16[16,768]{1,0:T(8,128)(2,1)S(1)} %copy-done.35), channel_id=1, source_target_pairs={{0,24},{1,25},{2,26},{3,27},{4,28},{5,29},{6,30},{7,31},{8,32},{9,... | collective-permute-start | bytes 73736 | tf_op jit(solution)/shard_map/ppermute | solution.py:391
  204.6 14.6 %collective-permute-start.35 = (bf16[16,768]{1,0:T(8,128)(2,1)S(1)}, bf16[16,768]{1,0:T(8,128)(2,1)S(1)}, u32[]{:S(2)}, u32[]{:S(2)}) collective-permute-start(bf16[16,768]{1,0:T(8,128)(2,1)S(1)} %copy-done.34), channel_id=1, source_target_pairs={{0,32},{1,33},{2,34},{3,35},{4,36},{5,37},{6,38},{7,39},{8,40},{9,... | collective-permute-start | bytes 73736 | tf_op jit(solution)/shard_map/ppermute | solution.py:391
  (55 other events, 399.8 us)

commit v2 on v1

v2 whole, which is shorter than its diff:
```python
import functools

import jax
import jax.numpy as jnp
from jax import lax
from jax.experimental import pallas as pl
from jax.experimental.pallas import tpu as pltpu
from jax.sharding import PartitionSpec as P

HD = 64
KW = 31
ROWS = 256
EDGE = 32
CEDGE = 16
QROWS = ROWS + 2 * EDGE
CROWS = ROWS + 2 * CEDGE
WINDOW = 3 * ROWS
WIDTH = 1536
CALLS = ((0, 3), (3, 2), (5, 1))
CHUNKS = 2
CWIDTH = WIDTH // CHUNKS
LANES = 256
VMEM = 60 * 1024 * 1024
BF = jnp.bfloat16
F32 = jnp.float32
NT = (((1,), (1,)), ((), ()))
TN = (((0,), (0,)), ((), ()))


def half_masks(scale):
    lane = lax.broadcasted_iota(jnp.int32, (1, 2 * HD), 1)
    return [
        jnp.where((lane < HD) == (half == 0), scale, 0.0).astype(BF) for half in range(2)
    ]


def forward_kernel(
    row_ids, key_ids, q_low, q_own, q_high, k_low, k_own, k_high, v_low, v_own, v_high,
    context_ref, context_b_ref, probs_ref, bias,
):
    @pl.when(pl.program_id(0) == 0)
    def _():
        bias[...] = jnp.where(row_ids[...][:, :1] == key_ids[...], 0.0, -1e30)

    scales = half_masks(HD ** -0.5)
    lane = lax.broadcasted_iota(jnp.int32, (1, 2 * HD), 1) < HD
    for pair in range(q_own.shape[1] // (2 * HD)):
        cols = slice(pair * 2 * HD, (pair + 1) * 2 * HD)
        q = jnp.concatenate([q_low[:, cols], q_own[:, cols], q_high[:, cols]], axis=0)
        k = jnp.concatenate([k_low[:, cols], k_own[:, cols], k_high[:, cols]], axis=0)
        v = jnp.concatenate([v_low[:, cols], v_own[:, cols], v_high[:, cols]], axis=0)
        outs = []
        for half in range(2):
            scores = lax.dot_general(q * scales[half], k, NT, preferred_element_type=F32)
            scores = scores + bias[...]
            highest = jnp.max(scores, axis=1, keepdims=True)
            weights = jnp.exp(scores - highest)
            totals = jnp.sum(weights, axis=1, keepdims=True)
            probs = (weights * (1.0 / totals)).astype(BF)
            probs_ref[2 * pair + half] = probs[EDGE : EDGE + ROWS]
            outs.append(jnp.dot(probs, v, preferred_element_type=F32))
        context = jnp.where(lane, outs[0], outs[1])
        context_ref[:, cols] = context[EDGE : EDGE + ROWS]
        context_b_ref[:, cols] = context.astype(BF)


def attention_forward(row_ids, key_ids, q, k, v, low, high, chunk):
    step = 2 * HD
    heads = step // HD
    first = chunk * (CWIDTH // step)
    column = lambda rows: pl.BlockSpec((rows, step), lambda i: (0, i))
    offset = lambda rows, at=0: pl.BlockSpec((rows, step), lambda i: (at, i + first))
    second = pl.BlockSpec((ROWS, step), lambda i: (1, i))
    edge = pl.BlockSpec((EDGE, step), lambda i: (2 * ROWS // EDGE, i))
    whole = lambda shape: pl.BlockSpec(shape, lambda i: (0, 0))
    return pl.pallas_call(
        forward_kernel,
        grid=(CWIDTH // step,),
        out_shape=(
            jax.ShapeDtypeStruct((ROWS, CWIDTH), F32),
            jax.ShapeDtypeStruct((QROWS, CWIDTH), BF),
            jax.ShapeDtypeStruct((CWIDTH // HD, ROWS, WINDOW), BF),
        ),
        in_specs=[
            whole((QROWS, 128)), whole((1, WINDOW)), edge, offset(ROWS), edge,
            column(ROWS), offset(ROWS), column(ROWS), second, offset(ROWS), second,
        ],
        out_specs=(
            column(ROWS),
            column(QROWS),
            pl.BlockSpec((heads, ROWS, WINDOW), lambda i: (i, 0, 0)),
        ),
        scratch_shapes=[pltpu.VMEM((QROWS, WINDOW), F32)],
        compiler_params=pltpu.CompilerParams(vmem_limit_bytes=VMEM),
        cost_estimate=pl.CostEstimate(
            flops=12 << 30, bytes_accessed=10 << 20, transcendentals=0
        ),
        name="attention_forward",
    )(row_ids, key_ids, low, q, high, low, k, high, low, v, high)


def conv_kernel_body(*refs):
    ids_ref = refs[0]
    contexts = refs[1 : 1 + CHUNKS]
    weight_ref, taps_ref, cot_low, cot_own, cot_high = refs[1 + CHUNKS : 6 + CHUNKS]
    rest = refs[6 + CHUNKS :]
    block_ref, grad_ref, shifted, cgrad, ids, gated, taps_acc, cot_ref = rest[-8:]
    step = pl.program_id(0)

    @pl.when(step == 0)
    def _():
        ids[0] = ids_ref[...]
        for b in range(1, 8):
            ids[b, : QROWS - 8] = ids_ref[b : b + QROWS - 8, :]

    cot_ref[:CEDGE] = cot_low[...].astype(F32)
    cot_ref[CEDGE : CEDGE + ROWS] = cot_own[...].astype(F32)
    cot_ref[CEDGE + ROWS :] = cot_high[...].astype(F32)
    attended = jnp.zeros((QROWS, LANES), F32)
    for n, context_ref in enumerate(contexts):
        attended = attended + jnp.dot(
            context_ref[...], weight_ref[n * CWIDTH : (n + 1) * CWIDTH], preferred_element_type=F32
        )
    shifted[0] = attended.astype(BF).astype(F32)
    for b in range(1, 8):
        shifted[b, : QROWS - 8] = shifted[0, b : b + QROWS - 8, :]
    taps_acc[...] = jnp.zeros_like(taps_acc)
    tiles = [slice(j * 128, (j + 1) * 128) for j in range(LANES // 128)]
    block = 32

    def forward_rows(i, carry):
        o = pl.multiple_of(i * block, block)
        own = ids[0, pl.ds(o + CEDGE, block), :]
        sums = [jnp.zeros((block, 128), F32) for _ in tiles]
        for e in range(1, KW + 1):
            a, b = divmod(e, 8)
            same = ids[b, pl.ds(o + 8 * a, block), :] == own
            for j, tile in enumerate(tiles):
                term = shifted[b, pl.ds(o + 8 * a, block), tile] * taps_ref[e - 1 : e, tile]
                sums[j] = sums[j] + jnp.where(same, term, 0.0)
        for j, tile in enumerate(tiles):
            gate = jax.nn.sigmoid(sums[j])
            gated[pl.ds(o, block), tile] = sums[j] * gate
            grad = cot_ref[pl.ds(o, block), tile] * gate * (1.0 + sums[j] * (1.0 - gate))
            cgrad[0, pl.ds(o, block), tile] = grad.astype(BF).astype(F32)
        return carry

    lax.fori_loop(0, CROWS // block, forward_rows, 0)
    block_ref[...] = gated[CEDGE : CEDGE + ROWS].astype(BF)
    for b in range(1, 8):
        cgrad[b, : CROWS - 8] = cgrad[0, b : b + CROWS - 8, :]

    def backward_rows(i, carry):
        s = pl.multiple_of(i * block, block)
        own = ids[0, pl.ds(s + EDGE, block), :]
        grads = [cgrad[0, pl.ds(s + CEDGE, block), tile] for tile in tiles]
        sums = [jnp.zeros((block, 128), F32) for _ in tiles]
        for e in range(1, KW + 1):
            a, b = divmod(e, 8)
            same = ids[b, pl.ds(s + CEDGE + 8 * a, block), :] == own
            for j, tile in enumerate(tiles):
                term = cgrad[b, pl.ds(s + 8 * a, block), tile] * taps_ref[KW - e : KW - e + 1, tile]
                sums[j] = sums[j] + jnp.where(same, term, 0.0)
                pair = grads[j] * shifted[b, pl.ds(s + CEDGE + 8 * a, block), tile]
                pair = jnp.where(same, pair, 0.0)
                taps_acc[e - 1, :, tile] += jnp.sum(pair.reshape(block // 8, 8, 128), axis=0)
        for j, tile in enumerate(tiles):
            grad_ref[pl.ds(s, block), tile] = sums[j].astype(BF)
        return carry

    lax.fori_loop(0, ROWS // block, backward_rows, 0)
    grad_ref[ROWS:] = jnp.sum(taps_acc[...], axis=1).astype(BF)


def conv_chain(row_ids, contexts, out_proj, taps, lows, cot, highs, block_out, after, call):
    begin, steps = CALLS[call]
    first = call == 0
    width = steps * LANES
    column = lambda rows: pl.BlockSpec((rows, LANES), lambda i: (0, i))
    offset = lambda rows, at=0: pl.BlockSpec((rows, LANES), lambda i: (at, i + begin))
    whole = lambda shape: pl.BlockSpec(shape, lambda i: (0, 0))
    anywhere = pl.BlockSpec(memory_space=pl.ANY)
    chunk = begin * LANES // CWIDTH
    local = begin - chunk * (CWIDTH // LANES)
    edge = pl.BlockSpec((CEDGE, LANES), lambda i: ((2 * ROWS + EDGE) // CEDGE, i + local))
    carried = after if first else [block_out] + after
    return pl.pallas_call(
        conv_kernel_body,
        grid=(steps,),
        out_shape=(
            jax.ShapeDtypeStruct((ROWS, WIDTH), BF),
            jax.ShapeDtypeStruct((ROWS + KW + 1, width), BF),
        ),
        in_specs=[whole((QROWS, 128))]
        + [whole((QROWS, CWIDTH))] * CHUNKS
        + [
            offset(WIDTH), offset(KW + 1),
            edge, offset(ROWS), edge,
        ]
        + [anywhere] * len(carried),
        out_specs=(offset(ROWS), column(ROWS + KW + 1)),
        scratch_shapes=[
            pltpu.VMEM((8, QROWS, LANES), F32),
            pltpu.VMEM((8, CROWS, LANES), F32),
            pltpu.VMEM((8, QROWS, 128), F32),
            pltpu.VMEM((CROWS, LANES), F32),
            pltpu.VMEM((KW + 1, 8, LANES), F32),
            pltpu.VMEM((CROWS, LANES), F32),
        ],
        input_output_aliases={} if first else {6 + CHUNKS: 0},
        compiler_params=pltpu.CompilerParams(vmem_limit_bytes=VMEM),
        cost_estimate=pl.CostEstimate(
            flops=steps * (5 << 30), bytes_accessed=10 << 20, transcendentals=0
        ),
        name="conv_chain",
    )(row_ids, *contexts, out_proj, taps, lows[chunk], cot, highs[chunk], *carried)


def context_grad_kernel(weight_ref, *refs):
    grads, out = refs[: len(CALLS)], refs[-1]
    total = jnp.zeros(out.shape[::-1], F32)
    for (begin, steps), grad in zip(CALLS, grads):
        cols = slice(begin * LANES, (begin + steps) * LANES)
        total = total + lax.dot_general(
            weight_ref[:, cols], grad[:ROWS], NT, preferred_element_type=F32
        )
    out[...] = total.T.astype(BF)


def context_gradient(out_proj, grads, after):
    step = 512
    return pl.pallas_call(
        context_grad_kernel,
        grid=(WIDTH // step,),
        out_shape=jax.ShapeDtypeStruct((ROWS, WIDTH), BF),
        in_specs=[pl.BlockSpec((step, WIDTH), lambda i: (i, 0))]
        + [pl.BlockSpec(grad.shape, lambda i: (0, 0)) for grad in grads]
        + [pl.BlockSpec(memory_space=pl.ANY)] * len(after),
        out_specs=pl.BlockSpec((ROWS, step), lambda i: (0, i)),
        compiler_params=pltpu.CompilerParams(vmem_limit_bytes=VMEM),
        cost_estimate=pl.CostEstimate(flops=3 << 30, bytes_accessed=8 << 20, transcendentals=0),
        name="context_gradient",
    )(out_proj, *grads, *after)


def backward_kernel(
    q_own, k_low, k_own, k_high, v_low, v_own, v_high, upstream, context, probs_ref, *rest,
):
    dq_ref, low_ref, dk_own, dv_own, high_ref = rest[-5:]
    plain = half_masks(1.0)
    scales = half_masks(HD ** -0.5)
    lane = lax.broadcasted_iota(jnp.int32, (1, 2 * HD), 1) < HD
    for pair in range(q_own.shape[1] // (2 * HD)):
        cols = slice(pair * 2 * HD, (pair + 1) * 2 * HD)
        k = jnp.concatenate([k_low[:, cols], k_own[:, cols], k_high[:, cols]], axis=0)
        v = jnp.concatenate([v_low[:, cols], v_own[:, cols], v_high[:, cols]], axis=0)
        q = q_own[:, cols]
        up = upstream[:, cols]
        products = up.astype(F32) * context[:, cols]
        q_turned = q.astype(F32).T.astype(BF)
        up_turned = up.astype(F32).T.astype(BF)
        dqs, dks, dvs = [], [], []
        for half in range(2):
            rows = slice(half * HD, (half + 1) * HD)
            delta = jnp.sum(
                jnp.where(lane == (half == 0), products, 0.0), axis=1, keepdims=True
            ) * HD ** -0.5
            grads = lax.dot_general(up * scales[half], v, NT, preferred_element_type=F32)
            probs = probs_ref[2 * pair + half]
            score_grad = (probs.astype(F32) * (grads - delta)).astype(BF)
            dqs.append(jnp.dot(score_grad, k, preferred_element_type=F32))
            dks.append(jnp.dot(q_turned[rows], score_grad, preferred_element_type=F32))
            dvs.append(jnp.dot(up_turned[rows], probs, preferred_element_type=F32))
        dq_ref[:, cols] = jnp.where(lane, dqs[0], dqs[1]).astype(BF)
        for n, (parts, own) in enumerate(((dks, dk_own), (dvs, dv_own))):
            whole = jnp.concatenate(parts, axis=0).T
            low_ref[n * ROWS : (n + 1) * ROWS, cols] = whole[:ROWS].astype(BF)
            own[:, cols] = whole[ROWS : 2 * ROWS]
            high_ref[n * ROWS : (n + 1) * ROWS, cols] = whole[2 * ROWS :].astype(BF)


def attention_backward(q, k, v, low, high, upstream, context, probs, previous, after, chunk):
    step = 2 * HD
    heads = step // HD
    first = chunk * (CWIDTH // step)
    column = lambda rows: pl.BlockSpec((rows, step), lambda i: (0, i))
    offset = lambda rows: pl.BlockSpec((rows, step), lambda i: (0, i + first))
    second = pl.BlockSpec((ROWS, step), lambda i: (1, i))
    own = jax.ShapeDtypeStruct((ROWS, WIDTH), F32)
    both = jax.ShapeDtypeStruct((2 * ROWS, WIDTH), BF)
    carried = list(previous) + after
    return pl.pallas_call(
        backward_kernel,
        grid=(CWIDTH // step,),
        out_shape=(jax.ShapeDtypeStruct((ROWS, WIDTH), BF), both, own, own, both),
        in_specs=[
            offset(ROWS), column(ROWS), offset(ROWS), column(ROWS), second, offset(ROWS), second,
            offset(ROWS), column(ROWS),
            pl.BlockSpec((heads, ROWS, WINDOW), lambda i: (i, 0, 0)),
        ]
        + [pl.BlockSpec(memory_space=pl.ANY)] * len(carried),
        out_specs=(
            offset(ROWS), offset(2 * ROWS), offset(ROWS), offset(ROWS), offset(2 * ROWS),
        ),
        input_output_aliases={10 + n: n for n in range(len(previous))},
        compiler_params=pltpu.CompilerParams(vmem_limit_bytes=VMEM),
        cost_estimate=pl.CostEstimate(
            flops=10 << 30, bytes_accessed=10 << 20, transcendentals=0
        ),
        name="attention_backward",
    )(q, low, k, high, low, v, high, upstream, context, probs, *carried)


def order_kernel(place_ref, *refs):
    contexts, outs = refs[:CHUNKS], refs[CHUNKS:]
    dp, z, x, c = (place_ref[n] for n in range(4))
    span = WIDTH // 4
    row = lax.broadcasted_iota(jnp.int32, (span, 1), 0)
    quarter = row // 96
    tc = lax.rem(quarter + c, 2)
    tl = lax.rem(quarter // 2 + z, 2)
    tx = lax.rem(lax.rem(row, 96) // 24 + x, 4)
    th = lax.rem(lax.rem(row, 24) // 6 + z // 2, 4)
    target = 48 * (2 * th + tl) + 12 * tx + 6 * tc + lax.rem(row, 6)
    chosen = jnp.where(
        target == lax.broadcasted_iota(jnp.int32, (1, span), 1), 1.0, 0.0
    ).astype(BF)
    turned = []
    for ref in contexts:
        for n in range(CWIDTH // span):
            part = ref[EDGE : EDGE + ROWS, n * span : (n + 1) * span]
            turned.append(lax.dot_general(chosen, part, NT, preferred_element_type=F32).astype(BF))
    for n in range(4):
        at = pl.ds(pl.multiple_of(96 * lax.rem(n - dp + 4, 4), 32), 96)
        for index, out in enumerate(outs):
            out[at] = turned[n][96 * index : 96 * (index + 1)]


def order_context(place, contexts):
    shape = jax.ShapeDtypeStruct((WIDTH // 4, ROWS), BF)
    vmem = pl.BlockSpec(memory_space=pltpu.VMEM)
    return pl.pallas_call(
        order_kernel,
        out_shape=(shape,) * 4,
        in_specs=[pl.BlockSpec(memory_space=pltpu.SMEM)] + [vmem] * CHUNKS,
        out_specs=(vmem,) * 4,
        compiler_params=pltpu.CompilerParams(vmem_limit_bytes=VMEM),
        name="order_context",
    )(place, *contexts)


def product_kernel(place_ref, *refs):
    contexts, grads, outs = refs[:4], refs[4:-4], refs[-4:]
    at = pl.ds(pl.multiple_of(ROWS + 16 * place_ref[3], 16), 16)
    context = jnp.concatenate([ref[...] for ref in contexts], axis=1)
    for call, (begin, steps) in enumerate(CALLS):
        cols = slice(begin * LANES, (begin + steps) * LANES)
        group = grads[4 * call : 4 * call + 4]
        taps = sum(grad[at].astype(F32) for grad in group).astype(BF)
        grad = jnp.concatenate([ref[:ROWS] for ref in group], axis=0)
        product = jnp.dot(context, grad, preferred_element_type=F32).astype(BF)
        for block in range(4):
            outs[block][:96, cols] = product[block * 96 : (block + 1) * 96]
            outs[block][96:, cols] = taps


def product_blocks(place, contexts, grads):
    shape = jax.ShapeDtypeStruct((112, WIDTH), BF)
    vmem = pl.BlockSpec(memory_space=pltpu.VMEM)
    return pl.pallas_call(
        product_kernel,
        out_shape=(shape,) * 4,
        in_specs=[pl.BlockSpec(memory_space=pltpu.SMEM)] + [vmem] * (4 + len(grads)),
        out_specs=(vmem,) * 4,
        compiler_params=pltpu.CompilerParams(vmem_limit_bytes=VMEM),
        cost_estimate=pl.CostEstimate(flops=3 << 30, bytes_accessed=8 << 20, transcendentals=0),
        name="product_blocks",
    )(place, *contexts, *grads)


def combine_kernel(parts, sources, pieces, count, scale, *refs):
    ins, outs = refs[: parts * sources], refs[-1 - pieces : -1]
    held = refs[-1]
    start = 0
    for part in range(parts):
        group = ins[part * sources : (part + 1) * sources]
        total = group[0][...].astype(F32)
        for ref in group[1:]:
            total = total + ref[...].astype(F32)
        held[:, start : start + group[0].shape[1]] = total * scale
        start = start + group[0].shape[1]
    rows = count // pieces
    for piece in range(pieces):
        out = outs[piece]
        if out.shape[0] > rows + 16:
            out[...] = jnp.zeros_like(out)
        out[:rows] = held[piece * rows : (piece + 1) * rows].astype(out.dtype)
        out[rows : rows + 16] = held[count : count + 16].astype(out.dtype)


def combine(parts, count, pieces, out_rows, after):
    shape = jax.ShapeDtypeStruct((out_rows, WIDTH), BF)
    blocks = [block for part in parts for block in part]
    vmem = pl.BlockSpec(memory_space=pltpu.VMEM)
    return pl.pallas_call(
        functools.partial(combine_kernel, len(parts), len(parts[0]), pieces, count, 1.0),
        out_shape=(shape,) * pieces,
        in_specs=[vmem] * len(blocks) + [pl.BlockSpec(memory_space=pl.ANY)] * len(after),
        out_specs=(vmem,) * pieces,
        scratch_shapes=[pltpu.VMEM((blocks[0].shape[0], WIDTH), F32)],
        compiler_params=pltpu.CompilerParams(vmem_limit_bytes=VMEM),
        cost_estimate=pl.CostEstimate(flops=0, bytes_accessed=1024, transcendentals=0),
        name="combine",
    )(*blocks, *after)


def last_kernel(scale, *refs):
    ins, (weight_out, taps_out, held) = refs[:-3], refs[-3:]
    total = ins[0][...].astype(F32)
    for ref in ins[1:]:
        total = total + ref[...].astype(F32)
    held[...] = total * scale
    weight_out[...] = held[:6]
    taps_out[...] = held[6:22]


def last_combine(blocks, scale):
    return pl.pallas_call(
        functools.partial(last_kernel, scale),
        out_shape=(
            jax.ShapeDtypeStruct((6, WIDTH), F32),
            jax.ShapeDtypeStruct((16, WIDTH), F32),
        ),
        scratch_shapes=[pltpu.VMEM(blocks[0].shape, F32)],
        name="last_combine",
    )(*blocks)


def join_kernel(place_ref, mine, theirs, out, held):
    c = place_ref[3]
    held[pl.ds(pl.multiple_of(16 * c, 16), 16)] = mine[...]
    held[pl.ds(pl.multiple_of(16 * (1 - c), 16), 16)] = theirs[...]
    out[...] = held[:KW]


def join_taps(place, mine, theirs):
    vmem = pl.BlockSpec(memory_space=pltpu.VMEM)
    return pl.pallas_call(
        join_kernel,
        out_shape=jax.ShapeDtypeStruct((KW, WIDTH), F32),
        in_specs=[pl.BlockSpec(memory_space=pltpu.SMEM), vmem, vmem],
        out_specs=vmem,
        scratch_shapes=[pltpu.VMEM((KW + 1, WIDTH), F32)],
        name="join_taps",
    )(place, mine, theirs)


def finish_kernel(*refs):
    dk, dv, later, earlier = refs[:4]
    for own, out, rows in ((dk, refs[-2], slice(0, ROWS)), (dv, refs[-1], slice(ROWS, 2 * ROWS))):
        total = own[...] + later[rows].astype(F32) + earlier[rows].astype(F32)
        out[...] = total.astype(BF)


def finish(operands):
    shape = jax.ShapeDtypeStruct((ROWS, WIDTH), BF)
    column = lambda rows: pl.BlockSpec((rows, 512), lambda i: (0, i))
    return pl.pallas_call(
        finish_kernel,
        grid=(WIDTH // 512,),
        out_shape=(shape, shape),
        in_specs=[column(ROWS), column(ROWS), column(2 * ROWS), column(2 * ROWS)],
        out_specs=(column(ROWS), column(ROWS)),
        compiler_params=pltpu.CompilerParams(vmem_limit_bytes=VMEM),
        cost_estimate=pl.CostEstimate(flops=0, bytes_accessed=1024, transcendentals=0),
        name="finish",
    )(*operands)


def seq_pairs(shift):
    pairs = []
    for source in range(64):
        z, x, c = source // 8, (source // 2) % 4, source % 2
        tz, tx, tc = shift(z, x, c)
        pairs.append((source, ((tz % 8) * 4 + tx % 4) * 2 + tc))
    return pairs


SWAP = seq_pairs(lambda z, x, c: (z, x, 1 - c))
PAIR = seq_pairs(lambda z, x, c: (z ^ 1, x, c))
BOTH = seq_pairs(lambda z, x, c: (z ^ 1, x, 1 - c))
UP = [(i, i + 1) for i in range(63)]
DOWN = [(i + 1, i) for i in range(63)]


def per_device(query, key, value, segments, out_proj, conv_kernel, cotangent):
    q, k, v, cot = query[0], key[0], value[0], cotangent[0]
    dp = lax.axis_index("dp")
    seq = lax.axis_index("seq")
    place = jnp.stack([dp, seq // 8, (seq // 2) % 4, seq % 2]).astype(jnp.int32)
    own_ids = segments[0] + 1

    id_row = lax.pad(
        own_ids.astype(BF)[None], jnp.zeros((), BF), ((0, 15, 0), (0, CWIDTH - ROWS, 0))
    )
    lows, highs = [], []
    for chunk in range(CHUNKS):
        cols = slice(chunk * CWIDTH, (chunk + 1) * CWIDTH)
        sent_up = [k[:, cols], v[:, cols], q[ROWS - EDGE :, cols], cot[ROWS - CEDGE :, cols], id_row]
        sent_down = [k[:, cols], v[:, cols], q[:EDGE, cols], cot[:CEDGE, cols], id_row]
        lows.append(lax.ppermute(jnp.concatenate(sent_up, axis=0), "seq", UP))
        highs.append(lax.ppermute(jnp.concatenate(sent_down, axis=0), "seq", DOWN))
    id_at = 2 * ROWS + EDGE + CEDGE
    ids = jnp.concatenate(
        [
            lows[0][id_at, :ROWS].astype(F32),
            own_ids.astype(F32),
            highs[0][id_at, :ROWS].astype(F32),
        ]
    )
    row_ids = jnp.broadcast_to(ids[ROWS - EDGE : 2 * ROWS + EDGE, None], (QROWS, 128))
    key_ids = ids[None]
    taps = lax.pad(conv_kernel.astype(F32), jnp.zeros((), F32), ((0, 1, 0), (0, 0, 0)))

    attended = [
        attention_forward(
            row_ids, key_ids, q, k, v, lows[chunk], highs[chunk], chunk
        )
        for chunk in range(CHUNKS)
    ]
    contexts = [entry[1] for entry in attended]
    ordered = order_context(place, contexts)
    ordered = [ordered[0]] + [
        lax.ppermute(part, "seq", pairs) for part, pairs in zip(ordered[1:], (SWAP, PAIR, BOTH))
    ]

    block_out, after = None, []
    grads, gathered = [], []
    relayed = None
    for call in range(len(CALLS)):
        block_out, grad = conv_chain(
            row_ids, contexts, out_proj, taps, lows, cot, highs, block_out, after, call
        )
        grads.append(grad)
        across = lax.ppermute(grad, "seq", PAIR)
        if call == 0:
            diagonal = lax.ppermute(across, "seq", SWAP)
        elif call == 1:
            relayed, diagonal = across, None
        else:
            diagonal = lax.ppermute(grad, "seq", BOTH)
            relayed, _ = lax.optimization_barrier((relayed, grad))
            gathered[7] = lax.ppermute(relayed, "seq", SWAP)
        group = [grad, lax.ppermute(grad, "seq", SWAP), across, diagonal]
        after = ordered[1:] if call == 0 else gathered[1:3]
        gathered += group
    context_grad = context_gradient(out_proj, grads, [gathered[3]])
    blocks = product_blocks(place, ordered, gathered)
    got = [lax.ppermute(blocks[n], "dp", [(i, (i + n) % 4) for i in range(4)]) for n in (1, 2, 3)]

    results, after = (), [blocks[0]]
    for chunk in range(CHUNKS):
        results = attention_backward(
            q, k, v, lows[chunk], highs[chunk], context_grad, attended[chunk][0],
            attended[chunk][2], results, after, chunk,
        )
        if chunk == 0:
            held = combine([[blocks[0]] + got], 96, 4, 40, [results[2]])
            after = [held[0]]
            got = [
                lax.ppermute(held[n], "seq", seq_pairs(lambda z, x, c: (z, x + n, c)))
                for n in (1, 2, 3)
            ]
    dq, low, dk, dv, high = results
    low, high, *got = lax.optimization_barrier((low, high, *got))
    later, earlier = lax.ppermute(low, "seq", DOWN), lax.ppermute(high, "seq", UP)
    held = combine([[held[0]] + got], 24, 4, 24, [dk])
    got = [
        lax.ppermute(held[n], "seq", seq_pairs(lambda z, x, c: (z + 2 * n, x, c))) for n in (1, 2, 3)
    ]
    scale_out = (4 * 64 * ROWS) ** (-0.5)
    grad_out_proj, taps_rows = last_combine([held[0]] + got, scale_out)
    grad_kernel = join_taps(place, taps_rows, lax.ppermute(taps_rows, "seq", SWAP))
    dk, dv = finish([dk, dv, later, earlier])
    return (block_out[None], dq[None], dk[None], dv[None], grad_kernel, grad_out_proj)


def solution(mesh):
    in_specs = (
        P("dp", "seq", None),
        P("dp", "seq", None),
        P("dp", "seq", None),
        P("dp", "seq"),
        P(),
        P(),
        P("dp", "seq", None),
    )
    out_specs = (
        P("dp", "seq", None),
        P("dp", "seq", None),
        P("dp", "seq", None),
        P("dp", "seq", None),
        P(),
        P(("dp", "seq"), None),
    )
    return jax.shard_map(
        per_device, mesh=mesh, in_specs=in_specs, out_specs=out_specs, check_vma=False
    )
```

time: 235 us -> 195 us (0.83)
  the two profiles are of different devices: /device:TPU:32 before, /device:TPU:31 now
where the time goes in v2:
time: 195 us; the launch traced here: 191 us
  Pallas kernels  100 us (51%)
  starting transfers between devices  47.6 us (24%)
  waiting for transfers between devices  27.3 us (14%)
  local copies, waits for them, and re-layouts  11.6 us (6%)
  other arithmetic  3.55 us (2%)
    pallas_call x3, Pallas kernels, conv_chain(): pl.pallas_call(conv_kernel_body, grid=(steps,), out_shape=(jax.ShapeDtype...  35.4 us
    pallas_call x2, Pallas kernels, attention_forward(): pl.pallas_call(forward_kernel, grid=(CWIDTH // step,), out_shape=(jax.Sha...  20.9 us
    pallas_call x2, Pallas kernels, attention_backward(): pl.pallas_call(backward_kernel, grid=(CWIDTH // step,), out_shape=(jax.Sh...  19.1 us
    ppermute x3, waiting for transfers between devices, per_device(): lax.ppermute(held[n], 'seq', seq_pairs(lambda z, x, c: (z + 2 * n, x, c)))  17.3 us
    ppermute x3, starting transfers between devices, per_device(): lax.ppermute(held[n], 'seq', seq_pairs(lambda z, x, c: (z + 2 * n, x, c)))  11.1 us
    ppermute x2, starting transfers between devices, per_device(): lows.append(lax.ppermute(jnp.concatenate(sent_up, axis=0), 'seq', UP))  10.8 us
    unnamed x59, local copies, waits for them, and re-layouts  10.1 us
    pallas_call x1, Pallas kernels, context_gradient(): pl.pallas_call(context_grad_kernel, grid=(WIDTH // step,), out_shape=jax....  5.22 us
  transfers between devices with their start and end apart: 28, of which 6 were waited for; matrix products, arithmetic and copies ran while one was open for 3% of the time, Pallas kernels for 39%

profile of v2, /device:TPU:31, one launch (start us, length us, event | category | flops | bytes accessed | tf_op | source)
XLA Modules:
  0.0 191.4 jit_solution(1523079209128662236)
XLA Ops:
  4.7 2.6 %collective-permute-start.1 = (bf16[576,768]{1,0:T(8,128)(2,1)S(1)}, bf16[576,768]{1,0:T(8,128)(2,1)}, u32[]{:S(2)}, u32[]{:S(2)}) collective-permute-start(bf16[576,768]{1,0:T(8,128)(2,1)S(1)} %get-tuple-element.115), channel_id=1, source_target_pairs={{1,0},{2,1},{3,2},{4,3},{5,4},{6,5},{7,6},{8,7},{9,8},{10,9},{11,1... | collective-permute-start | bytes 2654216 | tf_op jit(solution)/shard_map/ppermute | solution.py:512
  7.3 5.1 %collective-permute-start = (bf16[576,768]{1,0:T(8,128)(2,1)S(1)}, bf16[576,768]{1,0:T(8,128)(2,1)}, u32[]{:S(2)}, u32[]{:S(2)}) collective-permute-start(bf16[576,768]{1,0:T(8,128)(2,1)S(1)} %get-tuple-element.117), channel_id=1, source_target_pairs={{0,1},{1,2},{2,3},{3,4},{4,5},{5,6},{6,7},{7,8},{8,9},{9,10},{10,1... | collective-permute-start | bytes 2654216 | tf_op jit(solution)/shard_map/ppermute | solution.py:511
  14.3 5.8 %collective-permute-start.2 = (bf16[576,768]{1,0:T(8,128)(2,1)S(1)}, bf16[576,768]{1,0:T(8,128)(2,1)}, u32[]{:S(2)}, u32[]{:S(2)}) collective-permute-start(bf16[576,768]{1,0:T(8,128)(2,1)S(1)} %get-tuple-element.116), channel_id=1, source_target_pairs={{0,1},{1,2},{2,3},{3,4},{4,5},{5,6},{6,7},{7,8},{8,9},{9,10},{10,1... | collective-permute-start | bytes 2654216 | tf_op jit(solution)/shard_map/ppermute | solution.py:511
  25.1 10.4 %attention_forward.2 = (f32[256,768]{1,0:T(8,128)}, bf16[320,768]{1,0:T(8,128)(2,1)}, bf16[12,256,768]{2,1,0:T(8,128)(2,1)}) custom-call(f32[320,128]{1,0:T(8,128)} %broadcast_in_dim.22.row_ids.refs_0_, f32[1,768]{1,0:T(1,128)} %broadcast_in_dim.23.key_ids, bf16[576,768]{1,0:T(8,128)(2,1)} %collective-permute-done.q_low.k_low.v_low.refs_5_, ...), custom_call_target="tpu_custom_call" | custom-call | flops 12884901888 | bytes 10485760 | tf_op jit(solution)/shard_map/attention_forward/pallas_call | solution.py:76
  35.5 10.5 %attention_forward.3 = (f32[256,768]{1,0:T(8,128)}, bf16[320,768]{1,0:T(8,128)(2,1)}, bf16[12,256,768]{2,1,0:T(8,128)(2,1)}) custom-call(f32[320,128]{1,0:T(8,128)} %broadcast_in_dim.22.row_ids.refs_0_, f32[1,768]{1,0:T(1,128)} %broadcast_in_dim.23.key_ids, bf16[576,768]{1,0:T(8,128)(2,1)} %collective-permute-done.2.q_low.k_low.v_low.refs_5_, ...), custom_call_target="tpu_custom_call" | custom-call | flops 12884901888 | bytes 10485760 | tf_op jit(solution)/shard_map/attention_forward/pallas_call | solution.py:76
  46.0 3.2 %order_context.1 = (bf16[384,256]{1,0:T(8,128)(2,1)}, bf16[384,256]{1,0:T(8,128)(2,1)}, bf16[384,256]{1,0:T(8,128)(2,1)}, bf16[384,256]{1,0:T(8,128)(2,1)}) custom-call(s32[4]{0:T(128)} %pad_add_fusion.place_ref, bf16[320,768]{1,0:T(8,128)(2,1)} %get-tuple-element.54.refs_1_.refs_0_, bf16[320,768]{1,0:T(8,128)(2,1)} %get-tuple-element.55.refs_2_.refs_1_), custom_call_target="tpu_custom_call" | custom-call | tf_op jit(solution)/shard_map/order_context/pallas_call | solution.py:342
  51.4 16.6 %conv_chain.3 = (bf16[256,1536]{1,0:T(8,128)(2,1)}, bf16[288,768]{1,0:T(8,128)(2,1)}) custom-call(f32[320,128]{1,0:T(8,128)} %broadcast_in_dim.22.row_ids.refs_0_, bf16[320,768]{1,0:T(8,128)(2,1)} %get-tuple-element.54.refs_1_.refs_0_, bf16[320,768]{1,0:T(8,128)(2,1)} %get-tuple-element.55.refs_2_.refs_1_, bf16[1536,1536]{1,0:T(8,128)(2,1)} %weight_ref.1, ...), custom_call_target="tpu_custom_call" | custom-call | flops 16106127360 | bytes 10485760 | tf_op jit(solution)/shard_map/conv_chain/pallas_call | solution.py:187
  70.4 11.9 %conv_chain.4 = (bf16[256,1536]{1,0:T(8,128)(2,1)}, bf16[288,512]{1,0:T(8,128)(2,1)}) custom-call(f32[320,128]{1,0:T(8,128)} %broadcast_in_dim.22.row_ids.refs_0_, bf16[320,768]{1,0:T(8,128)(2,1)} %get-tuple-element.54.refs_1_.refs_0_, bf16[320,768]{1,0:T(8,128)(2,1)} %get-tuple-element.55.refs_2_.refs_1_, ...), custom_call_target="tpu_custom_call", output_to_operand_aliasing={{0}: (8, {})} | custom-call | flops 10737418240 | bytes 10485760 | tf_op jit(solution)/shard_map/conv_chain/pallas_call | solution.py:187
  84.2 7.0 %conv_chain.5 = (bf16[256,1536]{1,0:T(8,128)(2,1)}, bf16[288,256]{1,0:T(8,128)(2,1)}) custom-call(f32[320,128]{1,0:T(8,128)} %broadcast_in_dim.22.row_ids.refs_0_, bf16[320,768]{1,0:T(8,128)(2,1)} %get-tuple-element.54.refs_1_.refs_0_, bf16[320,768]{1,0:T(8,128)(2,1)} %get-tuple-element.55.refs_2_.refs_1_, ...), custom_call_target="tpu_custom_call", output_to_operand_aliasing={{0}: (8, {})} | custom-call | flops 5368709120 | bytes 10485760 | tf_op jit(solution)/shard_map/conv_chain/pallas_call | solution.py:187
  94.1 4.2 %collective-permute-done.15.refs_15_ = bf16[288,256]{1,0:T(8,128)(2,1)S(1)} collective-permute-done((bf16[288,256]{1,0:T(8,128)(2,1)}, bf16[288,256]{1,0:T(8,128)(2,1)S(1)}, u32[]{:S(2)}, u32[]{:S(2)}) %collective-permute-start.15) | collective-permute-done | bytes 147488 | tf_op jit(solution)/shard_map/ppermute | solution.py:551
  101.4 4.6 %product_blocks.1 = (bf16[112,1536]{1,0:T(8,128)(2,1)}, bf16[112,1536]{1,0:T(8,128)(2,1)}, bf16[112,1536]{1,0:T(8,128)(2,1)}, bf16[112,1536]{1,0:T(8,128)(2,1)}) custom-call(s32[4]{0:T(128)} %pad_add_fusion.place_ref, bf16[384,256]{1,0:T(8,128)(2,1)} %get-tuple-element.69.refs_0_, bf16[384,256]{1,0:T(8,128)(2,1)} %copy-done.20, bf16[384,256]{1,0:T(8,128)(2,1)} %copy-done.21, ...), custom_call_target="tpu_custom_call" | custom-call | flops 3221225472 | bytes 8388608 | tf_op jit(solution)/shard_map/product_blocks/pallas_call | solution.py:370
  106.0 2.2 %collective-permute-start.17 = (bf16[112,1536]{1,0:T(8,128)(2,1)}, bf16[112,1536]{1,0:T(8,128)(2,1)S(1)}, u32[]{:S(2)}, u32[]{:S(2)}) collective-permute-start(bf16[112,1536]{1,0:T(8,128)(2,1)} %get-tuple-element.78), channel_id=1, source_target_pairs={{0,128},{64,192},{128,0},{192,64},{1,129},{65,193},{129,1},{193,65... | collective-permute-start | bytes 1032200 | tf_op jit(solution)/shard_map/ppermute | solution.py:559
  108.3 5.2 %context_gradient.1.upstream = bf16[256,1536]{1,0:T(8,128)(2,1)} custom-call(bf16[1536,1536]{1,0:T(8,128)(2,1)} %weight_ref.1, bf16[288,768]{1,0:T(8,128)(2,1)} %get-tuple-element.61.refs_0_.refs_4_, bf16[288,512]{1,0:T(8,128)(2,1)} %get-tuple-element.63.refs_1_.refs_8_, bf16[288,256]{1,0:T(8,128)(2,1)} %get-tuple-element.64.refs_2_.refs_12_, ...), custom_call_target="tpu_custom_call" | custom-call | flops 3221225472 | bytes 8388608 | tf_op jit(solution)/shard_map/context_gradient/pallas_call | solution.py:232
  113.5 9.5 %attention_backward.2 = (bf16[256,1536]{1,0:T(8,128)(2,1)}, bf16[512,1536]{1,0:T(8,128)(2,1)}, f32[256,1536]{1,0:T(8,128)}, f32[256,1536]{1,0:T(8,128)}, bf16[512,1536]{1,0:T(8,128)(2,1)}) custom-call(bf16[256,1536]{1,0:T(8,128)(2,1)} %bitcast.29, bf16[576,768]{1,0:T(8,128)(2,1)} %collective-permute-done.q_low.k_low.v_low.refs_5_, ...), custom_call_target="tpu_custom_call" | custom-call | flops 10737418240 | bytes 10485760 | tf_op jit(solution)/shard_map/attention_backward/pallas_call | solution.py:292
  128.0 2.8 %collective-permute-start.19 = (bf16[40,1536]{1,0:T(8,128)(2,1)}, bf16[40,1536]{1,0:T(8,128)(2,1)S(1)}, u32[]{:S(2)}, u32[]{:S(2)}) collective-permute-start(bf16[40,1536]{1,0:T(8,128)(2,1)} %get-tuple-element.86), channel_id=1, source_target_pairs={{0,2},{1,3},{2,4},{3,5},{4,6},{5,7},{6,0},{7,1},{8,10},{9,11},{10,... | collective-permute-start | bytes 368648 | tf_op jit(solution)/shard_map/ppermute | solution.py:571
  131.5 9.6 %attention_backward.3 = (bf16[256,1536]{1,0:T(8,128)(2,1)}, bf16[512,1536]{1,0:T(8,128)(2,1)}, f32[256,1536]{1,0:T(8,128)}, f32[256,1536]{1,0:T(8,128)}, bf16[512,1536]{1,0:T(8,128)(2,1)}) custom-call(bf16[256,1536]{1,0:T(8,128)(2,1)} %bitcast.30, ...), custom_call_target="tpu_custom_call", output_to_operand_aliasing={{0}: (10, {}), {1}: (11, {}), {2}: (12, {}), {3}: (13, {}),... | custom-call | flops 10737418240 | bytes 10485760 | tf_op jit(solution)/shard_map/attention_backward/pallas_call | solution.py:292
  141.1 3.0 %collective-permute-start.22 = (bf16[512,1536]{1,0:T(8,128)(2,1)}, bf16[512,1536]{1,0:T(8,128)(2,1)S(1)}, u32[]{:S(2)}, u32[]{:S(2)}) collective-permute-start(bf16[512,1536]{1,0:T(8,128)(2,1)} %get-tuple-element.89), channel_id=1, source_target_pairs={{1,0},{2,1},{3,2},{4,3},{5,4},{6,5},{7,6},{8,7},{9,8},{10,9},{11,1... | collective-permute-start | bytes 4718600 | tf_op jit(solution)/shard_map/ppermute | solution.py:576
  144.1 4.7 %collective-permute-start.23 = (bf16[512,1536]{1,0:T(8,128)(2,1)}, bf16[512,1536]{1,0:T(8,128)(2,1)S(1)}, u32[]{:S(2)}, u32[]{:S(2)}) collective-permute-start(bf16[512,1536]{1,0:T(8,128)(2,1)} %get-tuple-element.90), channel_id=1, source_target_pairs={{0,1},{1,2},{2,3},{3,4},{4,5},{5,6},{6,7},{7,8},{8,9},{9,10},{10,1... | collective-permute-start | bytes 4718600 | tf_op jit(solution)/shard_map/ppermute | solution.py:576
  150.7 4.2 %collective-permute-start.24 = (bf16[24,1536]{1,0:T(8,128)(2,1)}, bf16[24,1536]{1,0:T(8,128)(2,1)S(1)}, u32[]{:S(2)}, u32[]{:S(2)}) collective-permute-start(bf16[24,1536]{1,0:T(8,128)(2,1)} %get-tuple-element.97), channel_id=1, source_target_pairs={{0,16},{1,17},{2,18},{3,19},{4,20},{5,21},{6,22},{7,23},{8,24},{9,... | collective-permute-start | bytes 221192 | tf_op jit(solution)/shard_map/ppermute | solution.py:579
  154.9 3.9 %collective-permute-start.25 = (bf16[24,1536]{1,0:T(8,128)(2,1)}, bf16[24,1536]{1,0:T(8,128)(2,1)S(1)}, u32[]{:S(2)}, u32[]{:S(2)}) collective-permute-start(bf16[24,1536]{1,0:T(8,128)(2,1)} %get-tuple-element.98), channel_id=1, source_target_pairs={{0,32},{1,33},{2,34},{3,35},{4,36},{5,37},{6,38},{7,39},{8,40},{9,... | collective-permute-start | bytes 221192 | tf_op jit(solution)/shard_map/ppermute | solution.py:579
  158.8 3.0 %collective-permute-start.26 = (bf16[24,1536]{1,0:T(8,128)(2,1)}, bf16[24,1536]{1,0:T(8,128)(2,1)S(1)}, u32[]{:S(2)}, u32[]{:S(2)}) collective-permute-start(bf16[24,1536]{1,0:T(8,128)(2,1)} %get-tuple-element.99), channel_id=1, source_target_pairs={{0,48},{1,49},{2,50},{3,51},{4,52},{5,53},{6,54},{7,55},{8,56},{9,... | collective-permute-start | bytes 221192 | tf_op jit(solution)/shard_map/ppermute | solution.py:579
  161.8 15.0 %collective-permute-done.24.refs_1_ = bf16[24,1536]{1,0:T(8,128)(2,1)S(1)} collective-permute-done((bf16[24,1536]{1,0:T(8,128)(2,1)}, bf16[24,1536]{1,0:T(8,128)(2,1)S(1)}, u32[]{:S(2)}, u32[]{:S(2)}) %collective-permute-start.24) | collective-permute-done | bytes 73760 | tf_op jit(solution)/shard_map/ppermute | solution.py:579
  176.8 2.4 %collective-permute-done.25.refs_2_ = bf16[24,1536]{1,0:T(8,128)(2,1)S(1)} collective-permute-done((bf16[24,1536]{1,0:T(8,128)(2,1)}, bf16[24,1536]{1,0:T(8,128)(2,1)S(1)}, u32[]{:S(2)}, u32[]{:S(2)}) %collective-permute-start.25) | collective-permute-done | bytes 73760 | tf_op jit(solution)/shard_map/ppermute | solution.py:579
  186.9 4.5 %finish.1 = (bf16[256,1536]{1,0:T(8,128)(2,1)}, bf16[256,1536]{1,0:T(8,128)(2,1)}) custom-call(f32[256,1536]{1,0:T(8,128)} %get-tuple-element.82.refs_0_.refs_4_, f32[256,1536]{1,0:T(8,128)} %get-tuple-element.83.refs_1_, bf16[512,1536]{1,0:T(8,128)(2,1)} %copy-done, bf16[512,1536]{1,0:T(8,128)(2,1)} %copy-done.1), custom_call_target="tpu_custom_call" | custom-call | bytes 1024 | tf_op jit(solution)/shard_map/finish/pallas_call | solution.py:468
  (116 shorter events, 38.7 us)
Async XLA Ops:
  4.7 17.6 %collective-permute-start.1 = (bf16[576,768]{1,0:T(8,128)(2,1)S(1)}, bf16[576,768]{1,0:T(8,128)(2,1)}, u32[]{:S(2)}, u32[]{:S(2)}) collective-permute-start(bf16[576,768]{1,0:T(8,128)(2,1)S(1)} %get-tuple-element.115), channel_id=1, source_target_pairs={{1,0},{2,1},{3,2},{4,3},{5,4},{6,5},{7,6},{8,7},{9,8},{10,9},{11,1... | collective-permute-start | bytes 2654216 | tf_op jit(solution)/shard_map/ppermute | solution.py:512
  7.3 15.7 %collective-permute-start = (bf16[576,768]{1,0:T(8,128)(2,1)S(1)}, bf16[576,768]{1,0:T(8,128)(2,1)}, u32[]{:S(2)}, u32[]{:S(2)}) collective-permute-start(bf16[576,768]{1,0:T(8,128)(2,1)S(1)} %get-tuple-element.117), channel_id=1, source_target_pairs={{0,1},{1,2},{2,3},{3,4},{4,5},{5,6},{6,7},{7,8},{8,9},{9,10},{10,1... | collective-permute-start | bytes 2654216 | tf_op jit(solution)/shard_map/ppermute | solution.py:511
  12.4 23.1 %collective-permute-start.3 = (bf16[576,768]{1,0:T(8,128)(2,1)S(1)}, bf16[576,768]{1,0:T(8,128)(2,1)}, u32[]{:S(2)}, u32[]{:S(2)}) collective-permute-start(bf16[576,768]{1,0:T(8,128)(2,1)S(1)} %get-tuple-element.114), channel_id=1, source_target_pairs={{1,0},{2,1},{3,2},{4,3},{5,4},{6,5},{7,6},{8,7},{9,8},{10,9},{11,1... | collective-permute-start | bytes 2654216 | tf_op jit(solution)/shard_map/ppermute | solution.py:512
  14.3 21.2 %collective-permute-start.2 = (bf16[576,768]{1,0:T(8,128)(2,1)S(1)}, bf16[576,768]{1,0:T(8,128)(2,1)}, u32[]{:S(2)}, u32[]{:S(2)}) collective-permute-start(bf16[576,768]{1,0:T(8,128)(2,1)S(1)} %get-tuple-element.116), channel_id=1, source_target_pairs={{0,1},{1,2},{2,3},{3,4},{4,5},{5,6},{6,7},{7,8},{8,9},{9,10},{10,1... | collective-permute-start | bytes 2654216 | tf_op jit(solution)/shard_map/ppermute | solution.py:511
  49.2 20.3 %collective-permute-start.4 = (bf16[384,256]{1,0:T(8,128)(2,1)}, bf16[384,256]{1,0:T(8,128)(2,1)S(1)}, u32[]{:S(2)}, u32[]{:S(2)}) collective-permute-start(bf16[384,256]{1,0:T(8,128)(2,1)} %get-tuple-element.57), channel_id=1, source_target_pairs={{0,1},{1,0},{2,3},{3,2},{4,5},{5,4},{6,7},{7,6},{8,9},{9,8},{10,11... | collective-permute-start | bytes 589832 | tf_op jit(solution)/shard_map/ppermute | solution.py:534
  49.2 20.4 %collective-permute-start.5 = (bf16[384,256]{1,0:T(8,128)(2,1)}, bf16[384,256]{1,0:T(8,128)(2,1)S(1)}, u32[]{:S(2)}, u32[]{:S(2)}) collective-permute-start(bf16[384,256]{1,0:T(8,128)(2,1)} %get-tuple-element.58), channel_id=1, source_target_pairs={{0,8},{1,9},{2,10},{3,11},{4,12},{5,13},{6,14},{7,15},{8,0},{9,1},... | collective-permute-start | bytes 589832 | tf_op jit(solution)/shard_map/ppermute | solution.py:534
  50.8 18.7 %collective-permute-start.6 = (bf16[384,256]{1,0:T(8,128)(2,1)}, bf16[384,256]{1,0:T(8,128)(2,1)S(1)}, u32[]{:S(2)}, u32[]{:S(2)}) collective-permute-start(bf16[384,256]{1,0:T(8,128)(2,1)} %get-tuple-element.59), channel_id=1, source_target_pairs={{0,9},{1,8},{2,11},{3,10},{4,13},{5,12},{6,15},{7,14},{8,1},{9,0},... | collective-permute-start | bytes 589832 | tf_op jit(solution)/shard_map/ppermute | solution.py:534
  67.9 15.3 %collective-permute-start.8 = (bf16[288,768]{1,0:T(8,128)(2,1)}, bf16[288,768]{1,0:T(8,128)(2,1)S(1)}, u32[]{:S(2)}, u32[]{:S(2)}) collective-permute-start(bf16[288,768]{1,0:T(8,128)(2,1)} %get-tuple-element.61.refs_0_.refs_4_), channel_id=1, source_target_pairs={{0,8},{1,9},{2,10},{3,11},{4,12},{5,13},{6,14},{7,15},{8,0},{9,1},... | collective-permute-start | bytes 1327112 | tf_op jit(solution)/shard_map/ppermute | solution.py:545
  69.6 13.9 %collective-permute-start.7 = (bf16[288,768]{1,0:T(8,128)(2,1)}, bf16[288,768]{1,0:T(8,128)(2,1)S(1)}, u32[]{:S(2)}, u32[]{:S(2)}) collective-permute-start(bf16[288,768]{1,0:T(8,128)(2,1)} %get-tuple-element.61.refs_0_.refs_4_), channel_id=1, source_target_pairs={{0,1},{1,0},{2,3},{3,2},{4,5},{5,4},{6,7},{7,6},{8,9},{9,8},{10,11... | collective-permute-start | bytes 1327112 | tf_op jit(solution)/shard_map/ppermute | solution.py:554
  82.3 8.9 %collective-permute-start.11 = (bf16[288,512]{1,0:T(8,128)(2,1)}, bf16[288,512]{1,0:T(8,128)(2,1)S(1)}, u32[]{:S(2)}, u32[]{:S(2)}) collective-permute-start(bf16[288,512]{1,0:T(8,128)(2,1)} %get-tuple-element.63.refs_1_.refs_8_), channel_id=1, source_target_pairs={{0,8},{1,9},{2,10},{3,11},{4,12},{5,13},{6,14},{7,15},{8,0},{9,1},... | collective-permute-start | bytes 884744 | tf_op jit(solution)/shard_map/ppermute | solution.py:545
  82.7 10.6 %collective-permute-start.10 = (bf16[288,512]{1,0:T(8,128)(2,1)}, bf16[288,512]{1,0:T(8,128)(2,1)S(1)}, u32[]{:S(2)}, u32[]{:S(2)}) collective-permute-start(bf16[288,512]{1,0:T(8,128)(2,1)} %get-tuple-element.63.refs_1_.refs_8_), channel_id=1, source_target_pairs={{0,1},{1,0},{2,3},{3,2},{4,5},{5,4},{6,7},{7,6},{8,9},{9,8},{10,11... | collective-permute-start | bytes 884744 | tf_op jit(solution)/shard_map/ppermute | solution.py:554
  83.2 17.3 %collective-permute-start.9 = (bf16[288,768]{1,0:T(8,128)(2,1)S(1)}, bf16[288,768]{1,0:T(8,128)(2,1)S(1)}, u32[]{:S(2)}, u32[]{:S(2)}) collective-permute-start(bf16[288,768]{1,0:T(8,128)(2,1)S(1)} %collective-permute-done.8.refs_10_.refs_6_), channel_id=1, source_target_pairs={{0,1},{1,0},{2,3},{3,2},{4,5},{5,4},{6,7},{7,6},{8,9},{9,8},{10,11... | collective-permute-start | bytes 1327112 | tf_op jit(solution)/shard_map/ppermute | solution.py:547
  91.2 9.3 %collective-permute-start.12 = (bf16[288,512]{1,0:T(8,128)(2,1)S(1)}, bf16[288,512]{1,0:T(8,128)(2,1)S(1)}, u32[]{:S(2)}, u32[]{:S(2)}) collective-permute-start(bf16[288,512]{1,0:T(8,128)(2,1)S(1)} %collective-permute-done.11.refs_10_), channel_id=1, source_target_pairs={{0,1},{1,0},{2,3},{3,2},{4,5},{5,4},{6,7},{7,6},{8,9},{9,8},{10,11... | collective-permute-start | bytes 884744 | tf_op jit(solution)/shard_map/ppermute | solution.py:553
  106.0 17.0 %collective-permute-start.16 = (bf16[112,1536]{1,0:T(8,128)(2,1)}, bf16[112,1536]{1,0:T(8,128)(2,1)S(1)}, u32[]{:S(2)}, u32[]{:S(2)}) collective-permute-start(bf16[112,1536]{1,0:T(8,128)(2,1)} %get-tuple-element.77), channel_id=1, source_target_pairs={{0,64},{64,128},{128,192},{192,0},{1,65},{65,129},{129,193},{193,1... | collective-permute-start | bytes 1032200 | tf_op jit(solution)/shard_map/ppermute | solution.py:559
  106.0 17.0 %collective-permute-start.17 = (bf16[112,1536]{1,0:T(8,128)(2,1)}, bf16[112,1536]{1,0:T(8,128)(2,1)S(1)}, u32[]{:S(2)}, u32[]{:S(2)}) collective-permute-start(bf16[112,1536]{1,0:T(8,128)(2,1)} %get-tuple-element.78), channel_id=1, source_target_pairs={{0,128},{64,192},{128,0},{192,64},{1,129},{65,193},{129,1},{193,65... | collective-permute-start | bytes 1032200 | tf_op jit(solution)/shard_map/ppermute | solution.py:559
  108.3 16.9 %collective-permute-start.18 = (bf16[112,1536]{1,0:T(8,128)(2,1)}, bf16[112,1536]{1,0:T(8,128)(2,1)S(1)}, u32[]{:S(2)}, u32[]{:S(2)}) collective-permute-start(bf16[112,1536]{1,0:T(8,128)(2,1)} %get-tuple-element.79), channel_id=1, source_target_pairs={{0,192},{64,0},{128,64},{192,128},{1,193},{65,1},{129,65},{193,129... | collective-permute-start | bytes 1032200 | tf_op jit(solution)/shard_map/ppermute | solution.py:559
  128.0 13.0 %collective-permute-start.19 = (bf16[40,1536]{1,0:T(8,128)(2,1)}, bf16[40,1536]{1,0:T(8,128)(2,1)S(1)}, u32[]{:S(2)}, u32[]{:S(2)}) collective-permute-start(bf16[40,1536]{1,0:T(8,128)(2,1)} %get-tuple-element.86), channel_id=1, source_target_pairs={{0,2},{1,3},{2,4},{3,5},{4,6},{5,7},{6,0},{7,1},{8,10},{9,11},{10,... | collective-permute-start | bytes 368648 | tf_op jit(solution)/shard_map/ppermute | solution.py:571
  130.9 10.2 %collective-permute-start.20 = (bf16[40,1536]{1,0:T(8,128)(2,1)}, bf16[40,1536]{1,0:T(8,128)(2,1)S(1)}, u32[]{:S(2)}, u32[]{:S(2)}) collective-permute-start(bf16[40,1536]{1,0:T(8,128)(2,1)} %get-tuple-element.87), channel_id=1, source_target_pairs={{0,4},{1,5},{2,6},{3,7},{4,0},{5,1},{6,2},{7,3},{8,12},{9,13},{10,... | collective-permute-start | bytes 368648 | tf_op jit(solution)/shard_map/ppermute | solution.py:571
  130.9 10.2 %collective-permute-start.21 = (bf16[40,1536]{1,0:T(8,128)(2,1)}, bf16[40,1536]{1,0:T(8,128)(2,1)S(1)}, u32[]{:S(2)}, u32[]{:S(2)}) collective-permute-start(bf16[40,1536]{1,0:T(8,128)(2,1)} %get-tuple-element.88), channel_id=1, source_target_pairs={{0,6},{1,7},{2,0},{3,1},{4,2},{5,3},{6,4},{7,5},{8,14},{9,15},{10,... | collective-permute-start | bytes 368648 | tf_op jit(solution)/shard_map/ppermute | solution.py:571
  141.1 44.2 %collective-permute-start.22 = (bf16[512,1536]{1,0:T(8,128)(2,1)}, bf16[512,1536]{1,0:T(8,128)(2,1)S(1)}, u32[]{:S(2)}, u32[]{:S(2)}) collective-permute-start(bf16[512,1536]{1,0:T(8,128)(2,1)} %get-tuple-element.89), channel_id=1, source_target_pairs={{1,0},{2,1},{3,2},{4,3},{5,4},{6,5},{7,6},{8,7},{9,8},{10,9},{11,1... | collective-permute-start | bytes 4718600 | tf_op jit(solution)/shard_map/ppermute | solution.py:576
  144.1 41.2 %collective-permute-start.23 = (bf16[512,1536]{1,0:T(8,128)(2,1)}, bf16[512,1536]{1,0:T(8,128)(2,1)S(1)}, u32[]{:S(2)}, u32[]{:S(2)}) collective-permute-start(bf16[512,1536]{1,0:T(8,128)(2,1)} %get-tuple-element.90), channel_id=1, source_target_pairs={{0,1},{1,2},{2,3},{3,4},{4,5},{5,6},{6,7},{7,8},{8,9},{9,10},{10,1... | collective-permute-start | bytes 4718600 | tf_op jit(solution)/shard_map/ppermute | solution.py:576
  150.7 26.1 %collective-permute-start.24 = (bf16[24,1536]{1,0:T(8,128)(2,1)}, bf16[24,1536]{1,0:T(8,128)(2,1)S(1)}, u32[]{:S(2)}, u32[]{:S(2)}) collective-permute-start(bf16[24,1536]{1,0:T(8,128)(2,1)} %get-tuple-element.97), channel_id=1, source_target_pairs={{0,16},{1,17},{2,18},{3,19},{4,20},{5,21},{6,22},{7,23},{8,24},{9,... | collective-permute-start | bytes 221192 | tf_op jit(solution)/shard_map/ppermute | solution.py:579
  154.9 24.2 %collective-permute-start.25 = (bf16[24,1536]{1,0:T(8,128)(2,1)}, bf16[24,1536]{1,0:T(8,128)(2,1)S(1)}, u32[]{:S(2)}, u32[]{:S(2)}) collective-permute-start(bf16[24,1536]{1,0:T(8,128)(2,1)} %get-tuple-element.98), channel_id=1, source_target_pairs={{0,32},{1,33},{2,34},{3,35},{4,36},{5,37},{6,38},{7,39},{8,40},{9,... | collective-permute-start | bytes 221192 | tf_op jit(solution)/shard_map/ppermute | solution.py:579
  158.8 20.3 %collective-permute-start.26 = (bf16[24,1536]{1,0:T(8,128)(2,1)}, bf16[24,1536]{1,0:T(8,128)(2,1)S(1)}, u32[]{:S(2)}, u32[]{:S(2)}) collective-permute-start(bf16[24,1536]{1,0:T(8,128)(2,1)} %get-tuple-element.99), channel_id=1, source_target_pairs={{0,48},{1,49},{2,50},{3,51},{4,52},{5,53},{6,54},{7,55},{8,56},{9,... | collective-permute-start | bytes 221192 | tf_op jit(solution)/shard_map/ppermute | solution.py:579
  (30 other events, 86.4 us)

commit v3 on v2

--- a/solution.py
+++ b/solution.py
@@ -35,12 +35,18 @@
 
 
 def forward_kernel(
-    row_ids, key_ids, q_low, q_own, q_high, k_low, k_own, k_high, v_low, v_own, v_high,
-    context_ref, context_b_ref, probs_ref, bias,
+    ids_low, ids_own, ids_high, q_low, q_own, q_high, k_low, k_own, k_high, v_low, v_own, v_high,
+    context_ref, context_b_ref, probs_ref, row_ids_ref, bias, turned,
 ):
     @pl.when(pl.program_id(0) == 0)
     def _():
-        bias[...] = jnp.where(row_ids[...][:, :1] == key_ids[...], 0.0, -1e30)
+        key_ids = jnp.concatenate(
+            [ids_low[...].astype(F32)[:1], ids_own[...], ids_high[...].astype(F32)[:1]], axis=1
+        )
+        turned[...] = jnp.broadcast_to(key_ids, (128, WINDOW)).T
+        row_ids = turned[ROWS - EDGE : 2 * ROWS + EDGE]
+        row_ids_ref[...] = row_ids
+        bias[...] = jnp.where(row_ids[:, :1] == key_ids, 0.0, -1e30)
 
     scales = half_masks(HD ** -0.5)
     lane = lax.broadcasted_iota(jnp.int32, (1, 2 * HD), 1) < HD
@@ -64,8 +70,8 @@
         context_b_ref[:, cols] = context.astype(BF)
 
 
-def attention_forward(row_ids, key_ids, q, k, v, low, high, chunk):
-    step = 2 * HD
+def attention_forward(own_ids, q, k, v, low, high, chunk):
+    step = 4 * HD
     heads = step // HD
     first = chunk * (CWIDTH // step)
     column = lambda rows: pl.BlockSpec((rows, step), lambda i: (0, i))
@@ -73,6 +79,7 @@
     second = pl.BlockSpec((ROWS, step), lambda i: (1, i))
     edge = pl.BlockSpec((EDGE, step), lambda i: (2 * ROWS // EDGE, i))
     whole = lambda shape: pl.BlockSpec(shape, lambda i: (0, 0))
+    id_block = pl.BlockSpec((16, ROWS), lambda i: ((2 * ROWS + EDGE + CEDGE) // 16, 0))
     return pl.pallas_call(
         forward_kernel,
         grid=(CWIDTH // step,),
@@ -80,23 +87,25 @@
             jax.ShapeDtypeStruct((ROWS, CWIDTH), F32),
             jax.ShapeDtypeStruct((QROWS, CWIDTH), BF),
             jax.ShapeDtypeStruct((CWIDTH // HD, ROWS, WINDOW), BF),
+            jax.ShapeDtypeStruct((QROWS, 128), F32),
         ),
         in_specs=[
-            whole((QROWS, 128)), whole((1, WINDOW)), edge, offset(ROWS), edge,
+            id_block, whole((1, ROWS)), id_block, edge, offset(ROWS), edge,
             column(ROWS), offset(ROWS), column(ROWS), second, offset(ROWS), second,
         ],
         out_specs=(
             column(ROWS),
             column(QROWS),
             pl.BlockSpec((heads, ROWS, WINDOW), lambda i: (i, 0, 0)),
-        ),
-        scratch_shapes=[pltpu.VMEM((QROWS, WINDOW), F32)],
+            whole((QROWS, 128)),
+        ),
+        scratch_shapes=[pltpu.VMEM((QROWS, WINDOW), F32), pltpu.VMEM((WINDOW, 128), F32)],
         compiler_params=pltpu.CompilerParams(vmem_limit_bytes=VMEM),
         cost_estimate=pl.CostEstimate(
             flops=12 << 30, bytes_accessed=10 << 20, transcendentals=0
         ),
         name="attention_forward",
-    )(row_ids, key_ids, low, q, high, low, k, high, low, v, high)
+    )(low, own_ids, high, low, q, high, low, k, high, low, v, high)
 
 
 def conv_kernel_body(*refs):
@@ -228,7 +237,7 @@
 
 
 def context_gradient(out_proj, grads, after):
-    step = 512
+    step = 768
     return pl.pallas_call(
         context_grad_kernel,
         grid=(WIDTH // step,),
@@ -279,24 +288,25 @@
             high_ref[n * ROWS : (n + 1) * ROWS, cols] = whole[2 * ROWS :].astype(BF)
 
 
-def attention_backward(q, k, v, low, high, upstream, context, probs, previous, after, chunk):
-    step = 2 * HD
+def attention_backward(q, k, v, low, high, upstream, context, probs, previous, after, chunk, piece):
+    step = 4 * HD
     heads = step // HD
-    first = chunk * (CWIDTH // step)
-    column = lambda rows: pl.BlockSpec((rows, step), lambda i: (0, i))
+    inner, count = piece
+    first = chunk * (CWIDTH // step) + inner
+    column = lambda rows: pl.BlockSpec((rows, step), lambda i: (0, i + inner))
     offset = lambda rows: pl.BlockSpec((rows, step), lambda i: (0, i + first))
-    second = pl.BlockSpec((ROWS, step), lambda i: (1, i))
+    second = pl.BlockSpec((ROWS, step), lambda i: (1, i + inner))
     own = jax.ShapeDtypeStruct((ROWS, WIDTH), F32)
     both = jax.ShapeDtypeStruct((2 * ROWS, WIDTH), BF)
     carried = list(previous) + after
     return pl.pallas_call(
         backward_kernel,
-        grid=(CWIDTH // step,),
+        grid=(count,),
         out_shape=(jax.ShapeDtypeStruct((ROWS, WIDTH), BF), both, own, own, both),
         in_specs=[
             offset(ROWS), column(ROWS), offset(ROWS), column(ROWS), second, offset(ROWS), second,
             offset(ROWS), column(ROWS),
-            pl.BlockSpec((heads, ROWS, WINDOW), lambda i: (i, 0, 0)),
+            pl.BlockSpec((heads, ROWS, WINDOW), lambda i: (i + inner, 0, 0)),
         ]
         + [pl.BlockSpec(memory_space=pl.ANY)] * len(carried),
         out_specs=(
@@ -305,7 +315,7 @@
         input_output_aliases={10 + n: n for n in range(len(previous))},
         compiler_params=pltpu.CompilerParams(vmem_limit_bytes=VMEM),
         cost_estimate=pl.CostEstimate(
-            flops=10 << 30, bytes_accessed=10 << 20, transcendentals=0
+            flops=count * (3 << 30), bytes_accessed=10 << 20, transcendentals=0
         ),
         name="attention_backward",
     )(q, low, k, high, low, v, high, upstream, context, probs, *carried)
@@ -350,7 +360,7 @@
 
 
 def product_kernel(place_ref, *refs):
-    contexts, grads, outs = refs[:4], refs[4:-4], refs[-4:]
+    contexts, grads, outs = refs[:4], refs[4:-5], refs[-4:]
     at = pl.ds(pl.multiple_of(ROWS + 16 * place_ref[3], 16), 16)
     context = jnp.concatenate([ref[...] for ref in contexts], axis=1)
     for call, (begin, steps) in enumerate(CALLS):
@@ -364,18 +374,20 @@
             outs[block][96:, cols] = taps
 
 
-def product_blocks(place, contexts, grads):
+def product_blocks(place, contexts, grads, after):
     shape = jax.ShapeDtypeStruct((112, WIDTH), BF)
     vmem = pl.BlockSpec(memory_space=pltpu.VMEM)
     return pl.pallas_call(
         product_kernel,
         out_shape=(shape,) * 4,
-        in_specs=[pl.BlockSpec(memory_space=pltpu.SMEM)] + [vmem] * (4 + len(grads)),
+        in_specs=[pl.BlockSpec(memory_space=pltpu.SMEM)]
+        + [vmem] * (4 + len(grads))
+        + [pl.BlockSpec(memory_space=pl.ANY)],
         out_specs=(vmem,) * 4,
         compiler_params=pltpu.CompilerParams(vmem_limit_bytes=VMEM),
         cost_estimate=pl.CostEstimate(flops=3 << 30, bytes_accessed=8 << 20, transcendentals=0),
         name="product_blocks",
-    )(place, *contexts, *grads)
+    )(place, *contexts, *grads, after)
 
 
 def combine_kernel(parts, sources, pieces, count, scale, *refs):
@@ -436,23 +448,23 @@
     )(*blocks)
 
 
-def join_kernel(place_ref, mine, theirs, out, held):
+def join_kernel(place_ref, mine, theirs, after, out, held):
     c = place_ref[3]
     held[pl.ds(pl.multiple_of(16 * c, 16), 16)] = mine[...]
     held[pl.ds(pl.multiple_of(16 * (1 - c), 16), 16)] = theirs[...]
     out[...] = held[:KW]
 
 
-def join_taps(place, mine, theirs):
+def join_taps(place, mine, theirs, after):
     vmem = pl.BlockSpec(memory_space=pltpu.VMEM)
     return pl.pallas_call(
         join_kernel,
         out_shape=jax.ShapeDtypeStruct((KW, WIDTH), F32),
-        in_specs=[pl.BlockSpec(memory_space=pltpu.SMEM), vmem, vmem],
+        in_specs=[pl.BlockSpec(memory_space=pltpu.SMEM), vmem, vmem, pl.BlockSpec(memory_space=pl.ANY)],
         out_specs=vmem,
         scratch_shapes=[pltpu.VMEM((KW + 1, WIDTH), F32)],
         name="join_taps",
-    )(place, mine, theirs)
+    )(place, mine, theirs, after)
 
 
 def finish_kernel(*refs):
@@ -464,10 +476,10 @@
 
 def finish(operands):
     shape = jax.ShapeDtypeStruct((ROWS, WIDTH), BF)
-    column = lambda rows: pl.BlockSpec((rows, 512), lambda i: (0, i))
+    column = lambda rows: pl.BlockSpec((rows, CWIDTH), lambda i: (0, i))
     return pl.pallas_call(
         finish_kernel,
-        grid=(WIDTH // 512,),
+        grid=(CHUNKS,),
         out_shape=(shape, shape),
         in_specs=[column(ROWS), column(ROWS), column(2 * ROWS), column(2 * ROWS)],
         out_specs=(column(ROWS), column(ROWS)),
@@ -510,25 +522,17 @@
         sent_down = [k[:, cols], v[:, cols], q[:EDGE, cols], cot[:CEDGE, cols], id_row]
         lows.append(lax.ppermute(jnp.concatenate(sent_up, axis=0), "seq", UP))
         highs.append(lax.ppermute(jnp.concatenate(sent_down, axis=0), "seq", DOWN))
-    id_at = 2 * ROWS + EDGE + CEDGE
-    ids = jnp.concatenate(
-        [
-            lows[0][id_at, :ROWS].astype(F32),
-            own_ids.astype(F32),
-            highs[0][id_at, :ROWS].astype(F32),
-        ]
-    )
-    row_ids = jnp.broadcast_to(ids[ROWS - EDGE : 2 * ROWS + EDGE, None], (QROWS, 128))
-    key_ids = ids[None]
+    ids_now = own_ids.astype(F32)[None]
     taps = lax.pad(conv_kernel.astype(F32), jnp.zeros((), F32), ((0, 1, 0), (0, 0, 0)))
 
     attended = [
         attention_forward(
-            row_ids, key_ids, q, k, v, lows[chunk], highs[chunk], chunk
+            ids_now, q, k, v, lows[chunk], highs[chunk], chunk
         )
         for chunk in range(CHUNKS)
     ]
     contexts = [entry[1] for entry in attended]
+    row_ids = attended[0][3]
     ordered = order_context(place, contexts)
     ordered = [ordered[0]] + [
         lax.ppermute(part, "seq", pairs) for part, pairs in zip(ordered[1:], (SWAP, PAIR, BOTH))
@@ -555,16 +559,16 @@
         after = ordered[1:] if call == 0 else gathered[1:3]
         gathered += group
     context_grad = context_gradient(out_proj, grads, [gathered[3]])
-    blocks = product_blocks(place, ordered, gathered)
+    blocks = product_blocks(place, ordered, gathered, context_grad)
     got = [lax.ppermute(blocks[n], "dp", [(i, (i + n) % 4) for i in range(4)]) for n in (1, 2, 3)]
 
     results, after = (), [blocks[0]]
-    for chunk in range(CHUNKS):
+    for turn, (chunk, piece) in enumerate(((0, (0, 3)), (1, (0, 1)), (1, (1, 2)))):
         results = attention_backward(
             q, k, v, lows[chunk], highs[chunk], context_grad, attended[chunk][0],
-            attended[chunk][2], results, after, chunk,
+            attended[chunk][2], results, after, chunk, piece,
         )
-        if chunk == 0:
+        if turn == 1:
             held = combine([[blocks[0]] + got], 96, 4, 40, [results[2]])
             after = [held[0]]
             got = [
@@ -580,8 +584,9 @@
     ]
     scale_out = (4 * 64 * ROWS) ** (-0.5)
     grad_out_proj, taps_rows = last_combine([held[0]] + got, scale_out)
-    grad_kernel = join_taps(place, taps_rows, lax.ppermute(taps_rows, "seq", SWAP))
+    taps_theirs = lax.ppermute(taps_rows, "seq", SWAP)
     dk, dv = finish([dk, dv, later, earlier])
+    grad_kernel = join_taps(place, taps_rows, taps_theirs, dk)
     return (block_out[None], dq[None], dk[None], dv[None], grad_kernel, grad_out_proj)
 
 

time: 195 us -> 192 us (0.985); the launches traced: 191 us -> 191 us
  local copies, waits for them, and re-layouts: 11.6 us -> 18 us
  Pallas kernels: 100 us -> 96.4 us
    unnamed x59 -> x63, local copies, waits for them, and re-layouts: 10.1 us -> 17.4 us
    ppermute x1, waiting for transfers between devices: 4.17 us -> 0.01 us  [per_device(): diagonal = lax.ppermute(grad, 'seq', BOTH)]
    pallas_call x2, Pallas kernels: 20.9 us -> 17.8 us  [attention_forward(): pl.pallas_call(forward_kernel, grid=(CWIDTH // step,), out_shape=(jax.Sha...]
    pallas_call x3 -> x4, Pallas kernels: 23.6 us -> 23.6 us  [the longest x3 19.8 us: attention_backward(): pl.pallas_call(backward_kernel, grid=(count,), out_shape=(jax.ShapeDtypeS...]
  transfers between devices with their start and end apart: 28 -> 28, of which waited for: 6 -> 7; matrix products, arithmetic and copies ran while one was open for 3% -> 1% of each run, Pallas kernels for 39% -> 40%
where the time goes in v3:
time: 192 us; the launch traced here: 191 us
  Pallas kernels  96.4 us (50%)
  starting transfers between devices  47.1 us (25%)
  waiting for transfers between devices  26.1 us (14%)
  local copies, waits for them, and re-layouts  18 us (9%)
  other arithmetic  2.82 us (1%)
    pallas_call x3, Pallas kernels, conv_chain(): pl.pallas_call(conv_kernel_body, grid=(steps,), out_shape=(jax.ShapeDtype...  35.4 us
    pallas_call x3, Pallas kernels, attention_backward(): pl.pallas_call(backward_kernel, grid=(count,), out_shape=(jax.ShapeDtypeS...  19.8 us
    ppermute x3, waiting for transfers between devices, per_device(): lax.ppermute(held[n], 'seq', seq_pairs(lambda z, x, c: (z + 2 * n, x, c)))  18.1 us
    pallas_call x2, Pallas kernels, attention_forward(): pl.pallas_call(forward_kernel, grid=(CWIDTH // step,), out_shape=(jax.Sha...  17.8 us
    unnamed x63, local copies, waits for them, and re-layouts  17.4 us
    ppermute x3, starting transfers between devices, per_device(): lax.ppermute(held[n], 'seq', seq_pairs(lambda z, x, c: (z + 2 * n, x, c)))  11.5 us
    ppermute x2, starting transfers between devices, per_device(): lows.append(lax.ppermute(jnp.concatenate(sent_up, axis=0), 'seq', UP))  10.8 us
    ppermute x1, starting transfers between devices, per_device(): lax.ppermute(high, 'seq', UP)  4.95 us
  transfers between devices with their start and end apart: 28, of which 7 were waited for; matrix products, arithmetic and copies ran while one was open for 1% of the time, Pallas kernels for 40%

profile of v3, /device:TPU:31, one launch (start us, length us, event | category | flops | bytes accessed | tf_op | source)
XLA Modules:
  0.0 191.5 jit_solution(2880788308277892266)
XLA Ops:
  11.2 2.6 %collective-permute-start.1 = (bf16[576,768]{1,0:T(8,128)(2,1)}, bf16[576,768]{1,0:T(8,128)(2,1)}, u32[]{:S(2)}, u32[]{:S(2)}) collective-permute-start(bf16[576,768]{1,0:T(8,128)(2,1)} %get-tuple-element.127), channel_id=1, source_target_pairs={{1,0},{2,1},{3,2},{4,3},{5,4},{6,5},{7,6},{8,7},{9,8},{10,9},{11,1... | collective-permute-start | bytes 2654216 | tf_op jit(solution)/shard_map/ppermute | solution.py:524
  13.8 5.1 %collective-permute-start = (bf16[576,768]{1,0:T(8,128)(2,1)}, bf16[576,768]{1,0:T(8,128)(2,1)}, u32[]{:S(2)}, u32[]{:S(2)}) collective-permute-start(bf16[576,768]{1,0:T(8,128)(2,1)} %get-tuple-element.129), channel_id=1, source_target_pairs={{0,1},{1,2},{2,3},{3,4},{4,5},{5,6},{6,7},{7,8},{8,9},{9,10},{10,1... | collective-permute-start | bytes 2654216 | tf_op jit(solution)/shard_map/ppermute | solution.py:523
  20.8 5.8 %collective-permute-start.2 = (bf16[576,768]{1,0:T(8,128)(2,1)S(1)}, bf16[576,768]{1,0:T(8,128)(2,1)S(1)}, u32[]{:S(2)}, u32[]{:S(2)}) collective-permute-start(bf16[576,768]{1,0:T(8,128)(2,1)S(1)} %get-tuple-element.128), channel_id=1, source_target_pairs={{0,1},{1,2},{2,3},{3,4},{4,5},{5,6},{6,7},{7,8},{8,9},{9,10},{10,1... | collective-permute-start | bytes 2654216 | tf_op jit(solution)/shard_map/ppermute | solution.py:523
  29.1 8.8 %attention_forward.2 = (f32[256,768]{1,0:T(8,128)}, bf16[320,768]{1,0:T(8,128)(2,1)}, bf16[12,256,768]{2,1,0:T(8,128)(2,1)}, f32[320,128]{1,0:T(8,128)}) custom-call(bf16[576,768]{1,0:T(8,128)(2,1)} %collective-permute-done.ids_low.q_low.k_low.v_low.refs_5_, f32[1,256]{1,0:T(1,128)} %get-tuple-element.130.ids_own, ...), custom_call_target="tpu_custom_call" | custom-call | flops 12884901888 | bytes 10485760 | tf_op jit(solution)/shard_map/attention_forward/pallas_call | solution.py:83
  39.9 8.9 %attention_forward.3 = (f32[256,768]{1,0:T(8,128)}, bf16[320,768]{1,0:T(8,128)(2,1)}, bf16[12,256,768]{2,1,0:T(8,128)(2,1)}, f32[320,128]{1,0:T(8,128)}) custom-call(bf16[576,768]{1,0:T(8,128)(2,1)} %copy-done.1, f32[1,256]{1,0:T(1,128)} %get-tuple-element.130.ids_own, bf16[576,768]{1,0:T(8,128)(2,1)} %copy-done, bf16[576,768]{1,0:T(8,128)(2,1)} %copy-done.1, ...), custom_call_target="tpu_custom_call" | custom-call | flops 12884901888 | bytes 10485760 | tf_op jit(solution)/shard_map/attention_forward/pallas_call | solution.py:83
  48.8 3.2 %order_context.1 = (bf16[384,256]{1,0:T(8,128)(2,1)}, bf16[384,256]{1,0:T(8,128)(2,1)}, bf16[384,256]{1,0:T(8,128)(2,1)}, bf16[384,256]{1,0:T(8,128)(2,1)}) custom-call(s32[4]{0:T(128)} %pad_add_fusion.place_ref, bf16[320,768]{1,0:T(8,128)(2,1)} %get-tuple-element.61.refs_1_.refs_0_, bf16[320,768]{1,0:T(8,128)(2,1)} %get-tuple-element.62.refs_2_.refs_1_), custom_call_target="tpu_custom_call" | custom-call | tf_op jit(solution)/shard_map/order_context/pallas_call | solution.py:352
  54.1 16.6 %conv_chain.3 = (bf16[256,1536]{1,0:T(8,128)(2,1)}, bf16[288,768]{1,0:T(8,128)(2,1)}) custom-call(f32[320,128]{1,0:T(8,128)} %get-tuple-element.60.refs_0_, bf16[320,768]{1,0:T(8,128)(2,1)} %get-tuple-element.61.refs_1_.refs_0_, bf16[320,768]{1,0:T(8,128)(2,1)} %get-tuple-element.62.refs_2_.refs_1_, bf16[1536,1536]{1,0:T(8,128)(2,1)} %weight_ref.1, ...), custom_call_target="tpu_custom_call" | custom-call | flops 16106127360 | bytes 10485760 | tf_op jit(solution)/shard_map/conv_chain/pallas_call | solution.py:196
  73.2 11.9 %conv_chain.4 = (bf16[256,1536]{1,0:T(8,128)(2,1)}, bf16[288,512]{1,0:T(8,128)(2,1)}) custom-call(f32[320,128]{1,0:T(8,128)} %get-tuple-element.60.refs_0_, bf16[320,768]{1,0:T(8,128)(2,1)} %get-tuple-element.61.refs_1_.refs_0_, bf16[320,768]{1,0:T(8,128)(2,1)} %get-tuple-element.62.refs_2_.refs_1_, ...), custom_call_target="tpu_custom_call", output_to_operand_aliasing={{0}: (8, {})} | custom-call | flops 10737418240 | bytes 10485760 | tf_op jit(solution)/shard_map/conv_chain/pallas_call | solution.py:196
  86.8 7.0 %conv_chain.5 = (bf16[256,1536]{1,0:T(8,128)(2,1)}, bf16[288,256]{1,0:T(8,128)(2,1)}) custom-call(f32[320,128]{1,0:T(8,128)} %get-tuple-element.60.refs_0_, bf16[320,768]{1,0:T(8,128)(2,1)} %get-tuple-element.61.refs_1_.refs_0_, bf16[320,768]{1,0:T(8,128)(2,1)} %get-tuple-element.62.refs_2_.refs_1_, ...), custom_call_target="tpu_custom_call", output_to_operand_aliasing={{0}: (8, {})} | custom-call | flops 5368709120 | bytes 10485760 | tf_op jit(solution)/shard_map/conv_chain/pallas_call | solution.py:196
  96.7 4.4 %context_gradient.1.refs_16_.upstream = bf16[256,1536]{1,0:T(8,128)(2,1)} custom-call(bf16[1536,1536]{1,0:T(8,128)(2,1)} %weight_ref.1, bf16[288,768]{1,0:T(8,128)(2,1)} %get-tuple-element.68.refs_0_.refs_4_, bf16[288,512]{1,0:T(8,128)(2,1)} %get-tuple-element.70.refs_1_.refs_8_, bf16[288,256]{1,0:T(8,128)(2,1)} %get-tuple-element.71.refs_2_.refs_12_, ...), custom_call_target="tpu_custom_call" | custom-call | flops 3221225472 | bytes 8388608 | tf_op jit(solution)/shard_map/context_gradient/pallas_call | solution.py:241
  103.8 4.6 %product_blocks.1 = (bf16[112,1536]{1,0:T(8,128)(2,1)}, bf16[112,1536]{1,0:T(8,128)(2,1)}, bf16[112,1536]{1,0:T(8,128)(2,1)}, bf16[112,1536]{1,0:T(8,128)(2,1)}) custom-call(s32[4]{0:T(128)} %pad_add_fusion.place_ref, bf16[384,256]{1,0:T(8,128)(2,1)} %get-tuple-element.76.refs_0_, bf16[384,256]{1,0:T(8,128)(2,1)} %copy-done.22, bf16[384,256]{1,0:T(8,128)(2,1)} %copy-done.23, ...), custom_call_target="tpu_custom_call" | custom-call | flops 3221225472 | bytes 8388608 | tf_op jit(solution)/shard_map/product_blocks/pallas_call | solution.py:380
  110.7 8.7 %attention_backward.3 = (bf16[256,1536]{1,0:T(8,128)(2,1)}, bf16[512,1536]{1,0:T(8,128)(2,1)}, f32[256,1536]{1,0:T(8,128)}, f32[256,1536]{1,0:T(8,128)}, bf16[512,1536]{1,0:T(8,128)(2,1)}) custom-call(bf16[256,1536]{1,0:T(8,128)(2,1)} %bitcast.28, bf16[576,768]{1,0:T(8,128)(2,1)} %collective-permute-done.ids_low.q_low.k_low.v_low.refs_5_, ...), custom_call_target="tpu_custom_call" | custom-call | flops 9663676416 | bytes 10485760 | tf_op jit(solution)/shard_map/attention_backward/pallas_call | solution.py:302
  119.4 4.6 %attention_backward.4 = (bf16[256,1536]{1,0:T(8,128)(2,1)}, bf16[512,1536]{1,0:T(8,128)(2,1)}, f32[256,1536]{1,0:T(8,128)}, f32[256,1536]{1,0:T(8,128)}, bf16[512,1536]{1,0:T(8,128)(2,1)}) custom-call(bf16[256,1536]{1,0:T(8,128)(2,1)} %bitcast.29, ...), custom_call_target="tpu_custom_call", output_to_operand_aliasing={{0}: (10, {}), {1}: (11, {}), {2}: (12, {}), {3}: (13, {}),... | custom-call | flops 3221225472 | bytes 10485760 | tf_op jit(solution)/shard_map/attention_backward/pallas_call | solution.py:302
  124.0 3.6 %collective-permute-done.18.refs_3_ = bf16[112,1536]{1,0:T(8,128)(2,1)S(1)} collective-permute-done((bf16[112,1536]{1,0:T(8,128)(2,1)}, bf16[112,1536]{1,0:T(8,128)(2,1)S(1)}, u32[]{:S(2)}, u32[]{:S(2)}) %collective-permute-start.18) | collective-permute-done | bytes 344096 | tf_op jit(solution)/shard_map/ppermute | solution.py:563
  130.5 2.8 %collective-permute-start.19 = (bf16[40,1536]{1,0:T(8,128)(2,1)}, bf16[40,1536]{1,0:T(8,128)(2,1)S(1)}, u32[]{:S(2)}, u32[]{:S(2)}) collective-permute-start(bf16[40,1536]{1,0:T(8,128)(2,1)} %get-tuple-element.98), channel_id=1, source_target_pairs={{0,2},{1,3},{2,4},{3,5},{4,6},{5,7},{6,0},{7,1},{8,10},{9,11},{10,... | collective-permute-start | bytes 368648 | tf_op jit(solution)/shard_map/ppermute | solution.py:575
  133.9 6.5 %attention_backward.5 = (bf16[256,1536]{1,0:T(8,128)(2,1)}, bf16[512,1536]{1,0:T(8,128)(2,1)}, f32[256,1536]{1,0:T(8,128)}, f32[256,1536]{1,0:T(8,128)}, bf16[512,1536]{1,0:T(8,128)(2,1)}) custom-call(bf16[256,1536]{1,0:T(8,128)(2,1)} %bitcast.30, ...), custom_call_target="tpu_custom_call", output_to_operand_aliasing={{0}: (10, {}), {1}: (11, {}), {2}: (12, {}), {3}: (13, {}),... | custom-call | flops 6442450944 | bytes 10485760 | tf_op jit(solution)/shard_map/attention_backward/pallas_call | solution.py:302
  142.3 2.7 %collective-permute-start.22 = (bf16[512,1536]{1,0:T(8,128)(2,1)}, bf16[512,1536]{1,0:T(8,128)(2,1)S(1)}, u32[]{:S(2)}, u32[]{:S(2)}) collective-permute-start(bf16[512,1536]{1,0:T(8,128)(2,1)} %get-tuple-element.101), channel_id=1, source_target_pairs={{1,0},{2,1},{3,2},{4,3},{5,4},{6,5},{7,6},{8,7},{9,8},{10,9},{11,1... | collective-permute-start | bytes 4718600 | tf_op jit(solution)/shard_map/ppermute | solution.py:580
  145.0 4.9 %collective-permute-start.23 = (bf16[512,1536]{1,0:T(8,128)(2,1)}, bf16[512,1536]{1,0:T(8,128)(2,1)S(1)}, u32[]{:S(2)}, u32[]{:S(2)}) collective-permute-start(bf16[512,1536]{1,0:T(8,128)(2,1)} %get-tuple-element.102), channel_id=1, source_target_pairs={{0,1},{1,2},{2,3},{3,4},{4,5},{5,6},{6,7},{7,8},{8,9},{9,10},{10,1... | collective-permute-start | bytes 4718600 | tf_op jit(solution)/shard_map/ppermute | solution.py:580
  151.9 3.6 %collective-permute-start.24 = (bf16[24,1536]{1,0:T(8,128)(2,1)}, bf16[24,1536]{1,0:T(8,128)(2,1)S(1)}, u32[]{:S(2)}, u32[]{:S(2)}) collective-permute-start(bf16[24,1536]{1,0:T(8,128)(2,1)} %get-tuple-element.109), channel_id=1, source_target_pairs={{0,16},{1,17},{2,18},{3,19},{4,20},{5,21},{6,22},{7,23},{8,24},{9,... | collective-permute-start | bytes 221192 | tf_op jit(solution)/shard_map/ppermute | solution.py:583
  155.4 5.2 %collective-permute-start.25 = (bf16[24,1536]{1,0:T(8,128)(2,1)}, bf16[24,1536]{1,0:T(8,128)(2,1)S(1)}, u32[]{:S(2)}, u32[]{:S(2)}) collective-permute-start(bf16[24,1536]{1,0:T(8,128)(2,1)} %get-tuple-element.110), channel_id=1, source_target_pairs={{0,32},{1,33},{2,34},{3,35},{4,36},{5,37},{6,38},{7,39},{8,40},{9,... | collective-permute-start | bytes 221192 | tf_op jit(solution)/shard_map/ppermute | solution.py:583
  160.6 2.7 %collective-permute-start.26 = (bf16[24,1536]{1,0:T(8,128)(2,1)}, bf16[24,1536]{1,0:T(8,128)(2,1)S(1)}, u32[]{:S(2)}, u32[]{:S(2)}) collective-permute-start(bf16[24,1536]{1,0:T(8,128)(2,1)} %get-tuple-element.111), channel_id=1, source_target_pairs={{0,48},{1,49},{2,50},{3,51},{4,52},{5,53},{6,54},{7,55},{8,56},{9,... | collective-permute-start | bytes 221192 | tf_op jit(solution)/shard_map/ppermute | solution.py:583
  163.3 14.8 %collective-permute-done.24.refs_1_ = bf16[24,1536]{1,0:T(8,128)(2,1)S(1)} collective-permute-done((bf16[24,1536]{1,0:T(8,128)(2,1)}, bf16[24,1536]{1,0:T(8,128)(2,1)S(1)}, u32[]{:S(2)}, u32[]{:S(2)}) %collective-permute-start.24) | collective-permute-done | bytes 73760 | tf_op jit(solution)/shard_map/ppermute | solution.py:583
  178.2 3.2 %collective-permute-done.25.refs_2_ = bf16[24,1536]{1,0:T(8,128)(2,1)S(1)} collective-permute-done((bf16[24,1536]{1,0:T(8,128)(2,1)}, bf16[24,1536]{1,0:T(8,128)(2,1)S(1)}, u32[]{:S(2)}, u32[]{:S(2)}) %collective-permute-start.25) | collective-permute-done | bytes 73760 | tf_op jit(solution)/shard_map/ppermute | solution.py:583
  185.4 3.8 %finish.1 = (bf16[256,1536]{1,0:T(8,128)(2,1)}, bf16[256,1536]{1,0:T(8,128)(2,1)}) custom-call(f32[256,1536]{1,0:T(8,128)} %get-tuple-element.94.refs_0_.refs_4_, f32[256,1536]{1,0:T(8,128)} %get-tuple-element.95.refs_1_, bf16[512,1536]{1,0:T(8,128)(2,1)} %copy-done.3, bf16[512,1536]{1,0:T(8,128)(2,1)} %copy-done.4), custom_call_target="tpu_custom_call" | custom-call | bytes 1024 | tf_op jit(solution)/shard_map/finish/pallas_call | solution.py:480
  (115 shorter events, 44.4 us)
Async XLA Ops:
  11.2 17.7 %collective-permute-start.1 = (bf16[576,768]{1,0:T(8,128)(2,1)}, bf16[576,768]{1,0:T(8,128)(2,1)}, u32[]{:S(2)}, u32[]{:S(2)}) collective-permute-start(bf16[576,768]{1,0:T(8,128)(2,1)} %get-tuple-element.127), channel_id=1, source_target_pairs={{1,0},{2,1},{3,2},{4,3},{5,4},{6,5},{7,6},{8,7},{9,8},{10,9},{11,1... | collective-permute-start | bytes 2654216 | tf_op jit(solution)/shard_map/ppermute | solution.py:524
  13.8 15.4 %collective-permute-start = (bf16[576,768]{1,0:T(8,128)(2,1)}, bf16[576,768]{1,0:T(8,128)(2,1)}, u32[]{:S(2)}, u32[]{:S(2)}) collective-permute-start(bf16[576,768]{1,0:T(8,128)(2,1)} %get-tuple-element.129), channel_id=1, source_target_pairs={{0,1},{1,2},{2,3},{3,4},{4,5},{5,6},{6,7},{7,8},{8,9},{9,10},{10,1... | collective-permute-start | bytes 2654216 | tf_op jit(solution)/shard_map/ppermute | solution.py:523
  18.9 19.1 %collective-permute-start.3 = (bf16[576,768]{1,0:T(8,128)(2,1)S(1)}, bf16[576,768]{1,0:T(8,128)(2,1)S(1)}, u32[]{:S(2)}, u32[]{:S(2)}) collective-permute-start(bf16[576,768]{1,0:T(8,128)(2,1)S(1)} %get-tuple-element.126), channel_id=1, source_target_pairs={{1,0},{2,1},{3,2},{4,3},{5,4},{6,5},{7,6},{8,7},{9,8},{10,9},{11,1... | collective-permute-start | bytes 2654216 | tf_op jit(solution)/shard_map/ppermute | solution.py:524
  20.8 17.7 %collective-permute-start.2 = (bf16[576,768]{1,0:T(8,128)(2,1)S(1)}, bf16[576,768]{1,0:T(8,128)(2,1)S(1)}, u32[]{:S(2)}, u32[]{:S(2)}) collective-permute-start(bf16[576,768]{1,0:T(8,128)(2,1)S(1)} %get-tuple-element.128), channel_id=1, source_target_pairs={{0,1},{1,2},{2,3},{3,4},{4,5},{5,6},{6,7},{7,8},{8,9},{9,10},{10,1... | collective-permute-start | bytes 2654216 | tf_op jit(solution)/shard_map/ppermute | solution.py:523
  52.0 20.4 %collective-permute-start.4 = (bf16[384,256]{1,0:T(8,128)(2,1)}, bf16[384,256]{1,0:T(8,128)(2,1)S(1)}, u32[]{:S(2)}, u32[]{:S(2)}) collective-permute-start(bf16[384,256]{1,0:T(8,128)(2,1)} %get-tuple-element.64), channel_id=1, source_target_pairs={{0,1},{1,0},{2,3},{3,2},{4,5},{5,4},{6,7},{7,6},{8,9},{9,8},{10,11... | collective-permute-start | bytes 589832 | tf_op jit(solution)/shard_map/ppermute | solution.py:538
  52.0 20.4 %collective-permute-start.5 = (bf16[384,256]{1,0:T(8,128)(2,1)}, bf16[384,256]{1,0:T(8,128)(2,1)S(1)}, u32[]{:S(2)}, u32[]{:S(2)}) collective-permute-start(bf16[384,256]{1,0:T(8,128)(2,1)} %get-tuple-element.65), channel_id=1, source_target_pairs={{0,8},{1,9},{2,10},{3,11},{4,12},{5,13},{6,14},{7,15},{8,0},{9,1},... | collective-permute-start | bytes 589832 | tf_op jit(solution)/shard_map/ppermute | solution.py:538
  53.6 18.7 %collective-permute-start.6 = (bf16[384,256]{1,0:T(8,128)(2,1)}, bf16[384,256]{1,0:T(8,128)(2,1)S(1)}, u32[]{:S(2)}, u32[]{:S(2)}) collective-permute-start(bf16[384,256]{1,0:T(8,128)(2,1)} %get-tuple-element.66), channel_id=1, source_target_pairs={{0,9},{1,8},{2,11},{3,10},{4,13},{5,12},{6,15},{7,14},{8,1},{9,0},... | collective-permute-start | bytes 589832 | tf_op jit(solution)/shard_map/ppermute | solution.py:538
  70.7 15.2 %collective-permute-start.8 = (bf16[288,768]{1,0:T(8,128)(2,1)}, bf16[288,768]{1,0:T(8,128)(2,1)S(1)}, u32[]{:S(2)}, u32[]{:S(2)}) collective-permute-start(bf16[288,768]{1,0:T(8,128)(2,1)} %get-tuple-element.68.refs_0_.refs_4_), channel_id=1, source_target_pairs={{0,8},{1,9},{2,10},{3,11},{4,12},{5,13},{6,14},{7,15},{8,0},{9,1},... | collective-permute-start | bytes 1327112 | tf_op jit(solution)/shard_map/ppermute | solution.py:549
  72.3 13.7 %collective-permute-start.7 = (bf16[288,768]{1,0:T(8,128)(2,1)}, bf16[288,768]{1,0:T(8,128)(2,1)S(1)}, u32[]{:S(2)}, u32[]{:S(2)}) collective-permute-start(bf16[288,768]{1,0:T(8,128)(2,1)} %get-tuple-element.68.refs_0_.refs_4_), channel_id=1, source_target_pairs={{0,1},{1,0},{2,3},{3,2},{4,5},{5,4},{6,7},{7,6},{8,9},{9,8},{10,11... | collective-permute-start | bytes 1327112 | tf_op jit(solution)/shard_map/ppermute | solution.py:558
  85.0 10.5 %collective-permute-start.11 = (bf16[288,512]{1,0:T(8,128)(2,1)}, bf16[288,512]{1,0:T(8,128)(2,1)S(1)}, u32[]{:S(2)}, u32[]{:S(2)}) collective-permute-start(bf16[288,512]{1,0:T(8,128)(2,1)} %get-tuple-element.70.refs_1_.refs_8_), channel_id=1, source_target_pairs={{0,8},{1,9},{2,10},{3,11},{4,12},{5,13},{6,14},{7,15},{8,0},{9,1},... | collective-permute-start | bytes 884744 | tf_op jit(solution)/shard_map/ppermute | solution.py:549
  85.5 15.7 %collective-permute-start.10 = (bf16[288,512]{1,0:T(8,128)(2,1)}, bf16[288,512]{1,0:T(8,128)(2,1)S(1)}, u32[]{:S(2)}, u32[]{:S(2)}) collective-permute-start(bf16[288,512]{1,0:T(8,128)(2,1)} %get-tuple-element.70.refs_1_.refs_8_), channel_id=1, source_target_pairs={{0,1},{1,0},{2,3},{3,2},{4,5},{5,4},{6,7},{7,6},{8,9},{9,8},{10,11... | collective-permute-start | bytes 884744 | tf_op jit(solution)/shard_map/ppermute | solution.py:558
  85.9 10.0 %collective-permute-start.9 = (bf16[288,768]{1,0:T(8,128)(2,1)S(1)}, bf16[288,768]{1,0:T(8,128)(2,1)S(1)}, u32[]{:S(2)}, u32[]{:S(2)}) collective-permute-start(bf16[288,768]{1,0:T(8,128)(2,1)S(1)} %collective-permute-done.8.refs_10_.refs_6_), channel_id=1, source_target_pairs={{0,1},{1,0},{2,3},{3,2},{4,5},{5,4},{6,7},{7,6},{8,9},{9,8},{10,11... | collective-permute-start | bytes 1327112 | tf_op jit(solution)/shard_map/ppermute | solution.py:551
  95.4 7.5 %collective-permute-start.14 = (bf16[288,256]{1,0:T(8,128)(2,1)}, bf16[288,256]{1,0:T(8,128)(2,1)S(1)}, u32[]{:S(2)}, u32[]{:S(2)}) collective-permute-start(bf16[288,256]{1,0:T(8,128)(2,1)} %get-tuple-element.71.refs_2_.refs_12_), channel_id=1, source_target_pairs={{0,8},{1,9},{2,10},{3,11},{4,12},{5,13},{6,14},{7,15},{8,0},{9,1},... | collective-permute-start | bytes 442376 | tf_op jit(solution)/shard_map/ppermute | solution.py:549
  95.5 7.4 %collective-permute-start.13 = (bf16[288,256]{1,0:T(8,128)(2,1)}, bf16[288,256]{1,0:T(8,128)(2,1)S(1)}, u32[]{:S(2)}, u32[]{:S(2)}) collective-permute-start(bf16[288,256]{1,0:T(8,128)(2,1)} %get-tuple-element.71.refs_2_.refs_12_), channel_id=1, source_target_pairs={{0,1},{1,0},{2,3},{3,2},{4,5},{5,4},{6,7},{7,6},{8,9},{9,8},{10,11... | collective-permute-start | bytes 442376 | tf_op jit(solution)/shard_map/ppermute | solution.py:558
  108.4 15.5 %collective-permute-start.16 = (bf16[112,1536]{1,0:T(8,128)(2,1)}, bf16[112,1536]{1,0:T(8,128)(2,1)S(1)}, u32[]{:S(2)}, u32[]{:S(2)}) collective-permute-start(bf16[112,1536]{1,0:T(8,128)(2,1)} %get-tuple-element.89), channel_id=1, source_target_pairs={{0,64},{64,128},{128,192},{192,0},{1,65},{65,129},{129,193},{193,1... | collective-permute-start | bytes 1032200 | tf_op jit(solution)/shard_map/ppermute | solution.py:563
  108.5 15.5 %collective-permute-start.17 = (bf16[112,1536]{1,0:T(8,128)(2,1)}, bf16[112,1536]{1,0:T(8,128)(2,1)S(1)}, u32[]{:S(2)}, u32[]{:S(2)}) collective-permute-start(bf16[112,1536]{1,0:T(8,128)(2,1)} %get-tuple-element.90), channel_id=1, source_target_pairs={{0,128},{64,192},{128,0},{192,64},{1,129},{65,193},{129,1},{193,65... | collective-permute-start | bytes 1032200 | tf_op jit(solution)/shard_map/ppermute | solution.py:563
  110.7 16.9 %collective-permute-start.18 = (bf16[112,1536]{1,0:T(8,128)(2,1)}, bf16[112,1536]{1,0:T(8,128)(2,1)S(1)}, u32[]{:S(2)}, u32[]{:S(2)}) collective-permute-start(bf16[112,1536]{1,0:T(8,128)(2,1)} %get-tuple-element.91), channel_id=1, source_target_pairs={{0,192},{64,0},{128,64},{192,128},{1,193},{65,1},{129,65},{193,129... | collective-permute-start | bytes 1032200 | tf_op jit(solution)/shard_map/ppermute | solution.py:563
  130.5 9.9 %collective-permute-start.19 = (bf16[40,1536]{1,0:T(8,128)(2,1)}, bf16[40,1536]{1,0:T(8,128)(2,1)S(1)}, u32[]{:S(2)}, u32[]{:S(2)}) collective-permute-start(bf16[40,1536]{1,0:T(8,128)(2,1)} %get-tuple-element.98), channel_id=1, source_target_pairs={{0,2},{1,3},{2,4},{3,5},{4,6},{5,7},{6,0},{7,1},{8,10},{9,11},{10,... | collective-permute-start | bytes 368648 | tf_op jit(solution)/shard_map/ppermute | solution.py:575
  133.3 9.0 %collective-permute-start.21 = (bf16[40,1536]{1,0:T(8,128)(2,1)}, bf16[40,1536]{1,0:T(8,128)(2,1)S(1)}, u32[]{:S(2)}, u32[]{:S(2)}) collective-permute-start(bf16[40,1536]{1,0:T(8,128)(2,1)} %get-tuple-element.100), channel_id=1, source_target_pairs={{0,6},{1,7},{2,0},{3,1},{4,2},{5,3},{6,4},{7,5},{8,14},{9,15},{10,... | collective-permute-start | bytes 368648 | tf_op jit(solution)/shard_map/ppermute | solution.py:575
  142.3 41.5 %collective-permute-start.22 = (bf16[512,1536]{1,0:T(8,128)(2,1)}, bf16[512,1536]{1,0:T(8,128)(2,1)S(1)}, u32[]{:S(2)}, u32[]{:S(2)}) collective-permute-start(bf16[512,1536]{1,0:T(8,128)(2,1)} %get-tuple-element.101), channel_id=1, source_target_pairs={{1,0},{2,1},{3,2},{4,3},{5,4},{6,5},{7,6},{8,7},{9,8},{10,9},{11,1... | collective-permute-start | bytes 4718600 | tf_op jit(solution)/shard_map/ppermute | solution.py:580
  145.0 38.8 %collective-permute-start.23 = (bf16[512,1536]{1,0:T(8,128)(2,1)}, bf16[512,1536]{1,0:T(8,128)(2,1)S(1)}, u32[]{:S(2)}, u32[]{:S(2)}) collective-permute-start(bf16[512,1536]{1,0:T(8,128)(2,1)} %get-tuple-element.102), channel_id=1, source_target_pairs={{0,1},{1,2},{2,3},{3,4},{4,5},{5,6},{6,7},{7,8},{8,9},{9,10},{10,1... | collective-permute-start | bytes 4718600 | tf_op jit(solution)/shard_map/ppermute | solution.py:580
  151.9 26.3 %collective-permute-start.24 = (bf16[24,1536]{1,0:T(8,128)(2,1)}, bf16[24,1536]{1,0:T(8,128)(2,1)S(1)}, u32[]{:S(2)}, u32[]{:S(2)}) collective-permute-start(bf16[24,1536]{1,0:T(8,128)(2,1)} %get-tuple-element.109), channel_id=1, source_target_pairs={{0,16},{1,17},{2,18},{3,19},{4,20},{5,21},{6,22},{7,23},{8,24},{9,... | collective-permute-start | bytes 221192 | tf_op jit(solution)/shard_map/ppermute | solution.py:583
  155.4 26.0 %collective-permute-start.25 = (bf16[24,1536]{1,0:T(8,128)(2,1)}, bf16[24,1536]{1,0:T(8,128)(2,1)S(1)}, u32[]{:S(2)}, u32[]{:S(2)}) collective-permute-start(bf16[24,1536]{1,0:T(8,128)(2,1)} %get-tuple-element.110), channel_id=1, source_target_pairs={{0,32},{1,33},{2,34},{3,35},{4,36},{5,37},{6,38},{7,39},{8,40},{9,... | collective-permute-start | bytes 221192 | tf_op jit(solution)/shard_map/ppermute | solution.py:583
  160.6 20.8 %collective-permute-start.26 = (bf16[24,1536]{1,0:T(8,128)(2,1)}, bf16[24,1536]{1,0:T(8,128)(2,1)S(1)}, u32[]{:S(2)}, u32[]{:S(2)}) collective-permute-start(bf16[24,1536]{1,0:T(8,128)(2,1)} %get-tuple-element.111), channel_id=1, source_target_pairs={{0,48},{1,49},{2,50},{3,51},{4,52},{5,53},{6,54},{7,55},{8,56},{9,... | collective-permute-start | bytes 221192 | tf_op jit(solution)/shard_map/ppermute | solution.py:583
  (32 other events, 94.6 us)

commit v4 on v3

--- a/solution.py
+++ b/solution.py
@@ -32,6 +32,37 @@
     return [
         jnp.where((lane < HD) == (half == 0), scale, 0.0).astype(BF) for half in range(2)
     ]
+
+
+def pack_kernel(ids, k, v, q_first, q_last, cot_first, cot_last, up, down):
+    for out, q_edge, cot_edge in ((up, q_last, cot_last), (down, q_first, cot_first)):
+        out[:ROWS] = k[...]
+        out[ROWS : 2 * ROWS] = v[...]
+        out[2 * ROWS : 2 * ROWS + EDGE] = q_edge[...]
+        out[2 * ROWS + EDGE : 2 * ROWS + EDGE + CEDGE] = cot_edge[...]
+        out[2 * ROWS + EDGE + CEDGE :] = jnp.broadcast_to(ids[...], (16, ROWS)).astype(BF)
+
+
+def pack_halo(ids, q, k, v, cot, chunk):
+    first = chunk * (CWIDTH // ROWS)
+    block = lambda rows, at=0: pl.BlockSpec((rows, ROWS), lambda i: (at, i + first))
+    rows = 2 * ROWS + EDGE + CEDGE + 16
+    shape = jax.ShapeDtypeStruct((rows, CWIDTH), BF)
+    column = pl.BlockSpec((rows, ROWS), lambda i: (0, i))
+    return pl.pallas_call(
+        pack_kernel,
+        grid=(CWIDTH // ROWS,),
+        out_shape=(shape, shape),
+        in_specs=[
+            pl.BlockSpec((1, ROWS), lambda i: (0, 0)), block(ROWS), block(ROWS),
+            block(EDGE), block(EDGE, ROWS // EDGE - 1),
+            block(CEDGE), block(CEDGE, ROWS // CEDGE - 1),
+        ],
+        out_specs=(column, column),
+        compiler_params=pltpu.CompilerParams(vmem_limit_bytes=VMEM),
+        cost_estimate=pl.CostEstimate(flops=0, bytes_accessed=1024, transcendentals=0),
+        name="pack_halo",
+    )(ids, k, v, q, q, cot, cot)
 
 
 def forward_kernel(
@@ -512,17 +543,12 @@
     place = jnp.stack([dp, seq // 8, (seq // 2) % 4, seq % 2]).astype(jnp.int32)
     own_ids = segments[0] + 1
 
-    id_row = lax.pad(
-        own_ids.astype(BF)[None], jnp.zeros((), BF), ((0, 15, 0), (0, CWIDTH - ROWS, 0))
-    )
+    ids_now = own_ids.astype(F32)[None]
     lows, highs = [], []
     for chunk in range(CHUNKS):
-        cols = slice(chunk * CWIDTH, (chunk + 1) * CWIDTH)
-        sent_up = [k[:, cols], v[:, cols], q[ROWS - EDGE :, cols], cot[ROWS - CEDGE :, cols], id_row]
-        sent_down = [k[:, cols], v[:, cols], q[:EDGE, cols], cot[:CEDGE, cols], id_row]
-        lows.append(lax.ppermute(jnp.concatenate(sent_up, axis=0), "seq", UP))
-        highs.append(lax.ppermute(jnp.concatenate(sent_down, axis=0), "seq", DOWN))
-    ids_now = own_ids.astype(F32)[None]
+        sent_up, sent_down = pack_halo(ids_now, q, k, v, cot, chunk)
+        lows.append(lax.ppermute(sent_up, "seq", UP))
+        highs.append(lax.ppermute(sent_down, "seq", DOWN))
     taps = lax.pad(conv_kernel.astype(F32), jnp.zeros((), F32), ((0, 1, 0), (0, 0, 0)))
 
     attended = [

time: 192 us -> 187 us (0.974)
  local copies, waits for them, and re-layouts: 18 us -> 7.62 us
  Pallas kernels: 96.4 us -> 103 us
  starting transfers between devices: 47.1 us -> 43.5 us
  waiting for transfers between devices: 26.1 us -> 28.4 us
    unnamed x63 -> x56, local copies, waits for them, and re-layouts: 17.4 us -> 7.62 us
    pallas_call x0 -> x2, Pallas kernels: none -> 6.76 us  [pack_halo(): pl.pallas_call(pack_kernel, grid=(CWIDTH // ROWS,), out_shape=(shape, sha...]
    ppermute x4, waiting for transfers between devices: 0.8 us -> 4.55 us  [the longest x2 4.55 us: per_device(): highs.append(lax.ppermute(sent_down, 'seq', DOWN))]
    ppermute x3, starting transfers between devices: 3.42 us -> 1.46 us  [per_device(): lax.ppermute(held[n], 'seq', seq_pairs(lambda z, x, c: (z, x + n, c)))]
  transfers between devices with their start and end apart: 28 -> 28, of which waited for: 7 -> 7; matrix products, arithmetic and copies ran while one was open for 1% -> 1% of each run, Pallas kernels for 40% -> 43%
where the time goes in v4:
time: 187 us; the launch traced here: 186 us
  Pallas kernels  103 us (55%)
  starting transfers between devices  43.5 us (23%)
  waiting for transfers between devices  28.4 us (15%)
  local copies, waits for them, and re-layouts  7.62 us (4%)
  other arithmetic  2.54 us (1%)
    pallas_call x3, Pallas kernels, conv_chain(): pl.pallas_call(conv_kernel_body, grid=(steps,), out_shape=(jax.ShapeDtype...  35.4 us
    pallas_call x3, Pallas kernels, attention_backward(): pl.pallas_call(backward_kernel, grid=(count,), out_shape=(jax.ShapeDtypeS...  19.8 us
    pallas_call x2, Pallas kernels, attention_forward(): pl.pallas_call(forward_kernel, grid=(CWIDTH // step,), out_shape=(jax.Sha...  17.7 us
    ppermute x3, waiting for transfers between devices, per_device(): lax.ppermute(held[n], 'seq', seq_pairs(lambda z, x, c: (z + 2 * n, x, c)))  16.8 us
    ppermute x3, starting transfers between devices, per_device(): lax.ppermute(held[n], 'seq', seq_pairs(lambda z, x, c: (z + 2 * n, x, c)))  11.4 us
    ppermute x2, starting transfers between devices, per_device(): lows.append(lax.ppermute(sent_up, 'seq', UP))  9.75 us
    unnamed x56, local copies, waits for them, and re-layouts  7.62 us
    pallas_call x2, Pallas kernels, pack_halo(): pl.pallas_call(pack_kernel, grid=(CWIDTH // ROWS,), out_shape=(shape, sha...  6.76 us
  transfers between devices with their start and end apart: 28, of which 7 were waited for; matrix products, arithmetic and copies ran while one was open for 1% of the time, Pallas kernels for 43%

profile of v4, /device:TPU:31, one launch (start us, length us, event | category | flops | bytes accessed | tf_op | source)
XLA Modules:
  0.0 186.2 jit_solution(6029943460179148469)
XLA Ops:
  1.9 3.4 %pack_halo.2 = (bf16[576,768]{1,0:T(8,128)(2,1)}, bf16[576,768]{1,0:T(8,128)(2,1)}) custom-call(f32[1,256]{1,0:T(1,128)} %add_convert_fusion.ids.ids_own, bf16[256,1536]{1,0:T(8,128)(2,1)} %bitcast.28, bf16[256,1536]{1,0:T(8,128)(2,1)} %bitcast.35, bf16[256,1536]{1,0:T(8,128)(2,1)} %bitcast.12, bf16[256,1536]{1,0:T(8,128)(2,1)} %bitcast.13, ...), custom_call_target="tpu_custom_call" | custom-call | bytes 1024 | tf_op jit(solution)/shard_map/pack_halo/pallas_call | solution.py:52
  5.3 4.0 %collective-permute-start = (bf16[576,768]{1,0:T(8,128)(2,1)}, bf16[576,768]{1,0:T(8,128)(2,1)S(1)}, u32[]{:S(2)}, u32[]{:S(2)}) collective-permute-start(bf16[576,768]{1,0:T(8,128)(2,1)} %get-tuple-element.64), channel_id=1, source_target_pairs={{0,1},{1,2},{2,3},{3,4},{4,5},{5,6},{6,7},{7,8},{8,9},{9,10},{10,1... | collective-permute-start | bytes 2654216 | tf_op jit(solution)/shard_map/ppermute | solution.py:550
  11.3 3.4 %pack_halo.3 = (bf16[576,768]{1,0:T(8,128)(2,1)}, bf16[576,768]{1,0:T(8,128)(2,1)}) custom-call(f32[1,256]{1,0:T(1,128)} %add_convert_fusion.ids.ids_own, bf16[256,1536]{1,0:T(8,128)(2,1)} %bitcast.29, bf16[256,1536]{1,0:T(8,128)(2,1)} %bitcast.36, bf16[256,1536]{1,0:T(8,128)(2,1)} %bitcast.14, bf16[256,1536]{1,0:T(8,128)(2,1)} %bitcast.15, ...), custom_call_target="tpu_custom_call" | custom-call | bytes 1024 | tf_op jit(solution)/shard_map/pack_halo/pallas_call | solution.py:52
  14.7 5.7 %collective-permute-start.2 = (bf16[576,768]{1,0:T(8,128)(2,1)}, bf16[576,768]{1,0:T(8,128)(2,1)S(1)}, u32[]{:S(2)}, u32[]{:S(2)}) collective-permute-start(bf16[576,768]{1,0:T(8,128)(2,1)} %get-tuple-element.68), channel_id=1, source_target_pairs={{0,1},{1,2},{2,3},{3,4},{4,5},{5,6},{6,7},{7,8},{8,9},{9,10},{10,1... | collective-permute-start | bytes 2654216 | tf_op jit(solution)/shard_map/ppermute | solution.py:550
  23.8 2.5 %collective-permute-done.1.ids_high.q_high.k_high.v_high.refs_7_ = bf16[576,768]{1,0:T(8,128)(2,1)} collective-permute-done((bf16[576,768]{1,0:T(8,128)(2,1)}, bf16[576,768]{1,0:T(8,128)(2,1)}, u32[]{:S(2)}, u32[]{:S(2)}) %collective-permute-start.1) | collective-permute-done | bytes 884768 | tf_op jit(solution)/shard_map/ppermute | solution.py:551
  26.2 8.8 %attention_forward.2 = (f32[256,768]{1,0:T(8,128)}, bf16[320,768]{1,0:T(8,128)(2,1)}, bf16[12,256,768]{2,1,0:T(8,128)(2,1)}, f32[320,128]{1,0:T(8,128)}) custom-call(bf16[576,768]{1,0:T(8,128)(2,1)} %copy-done.15, f32[1,256]{1,0:T(1,128)} %add_convert_fusion.ids.ids_own, bf16[576,768]{1,0:T(8,128)(2,1)} %collective-permute-done.1.ids_high.q_high.k_high.v_high.refs_7_, ...), custom_call_target="tpu_custom_call" | custom-call | flops 12884901888 | bytes 10485760 | tf_op jit(solution)/shard_map/attention_forward/pallas_call | solution.py:114
  38.1 8.9 %attention_forward.3 = (f32[256,768]{1,0:T(8,128)}, bf16[320,768]{1,0:T(8,128)(2,1)}, bf16[12,256,768]{2,1,0:T(8,128)(2,1)}, f32[320,128]{1,0:T(8,128)}) custom-call(bf16[576,768]{1,0:T(8,128)(2,1)} %copy-done, f32[1,256]{1,0:T(1,128)} %add_convert_fusion.ids.ids_own, bf16[576,768]{1,0:T(8,128)(2,1)} %copy-done.1, bf16[576,768]{1,0:T(8,128)(2,1)} %copy-done, ...), custom_call_target="tpu_custom_call" | custom-call | flops 12884901888 | bytes 10485760 | tf_op jit(solution)/shard_map/attention_forward/pallas_call | solution.py:114
  47.0 3.2 %order_context.1 = (bf16[384,256]{1,0:T(8,128)(2,1)}, bf16[384,256]{1,0:T(8,128)(2,1)}, bf16[384,256]{1,0:T(8,128)(2,1)}, bf16[384,256]{1,0:T(8,128)(2,1)}) custom-call(s32[4]{0:T(128)} %pad_add_fusion.place_ref, bf16[320,768]{1,0:T(8,128)(2,1)} %get-tuple-element.67.refs_1_.refs_0_, bf16[320,768]{1,0:T(8,128)(2,1)} %get-tuple-element.70.refs_2_.refs_1_), custom_call_target="tpu_custom_call" | custom-call | tf_op jit(solution)/shard_map/order_context/pallas_call | solution.py:383
  52.4 16.6 %conv_chain.3 = (bf16[256,1536]{1,0:T(8,128)(2,1)}, bf16[288,768]{1,0:T(8,128)(2,1)}) custom-call(f32[320,128]{1,0:T(8,128)} %get-tuple-element.66.refs_0_, bf16[320,768]{1,0:T(8,128)(2,1)} %get-tuple-element.67.refs_1_.refs_0_, bf16[320,768]{1,0:T(8,128)(2,1)} %get-tuple-element.70.refs_2_.refs_1_, bf16[1536,1536]{1,0:T(8,128)(2,1)} %weight_ref.1, ...), custom_call_target="tpu_custom_call" | custom-call | flops 16106127360 | bytes 10485760 | tf_op jit(solution)/shard_map/conv_chain/pallas_call | solution.py:227
  71.4 11.9 %conv_chain.4 = (bf16[256,1536]{1,0:T(8,128)(2,1)}, bf16[288,512]{1,0:T(8,128)(2,1)}) custom-call(f32[320,128]{1,0:T(8,128)} %get-tuple-element.66.refs_0_, bf16[320,768]{1,0:T(8,128)(2,1)} %get-tuple-element.67.refs_1_.refs_0_, bf16[320,768]{1,0:T(8,128)(2,1)} %get-tuple-element.70.refs_2_.refs_1_, ...), custom_call_target="tpu_custom_call", output_to_operand_aliasing={{0}: (8, {})} | custom-call | flops 10737418240 | bytes 10485760 | tf_op jit(solution)/shard_map/conv_chain/pallas_call | solution.py:227
  85.1 7.0 %conv_chain.5 = (bf16[256,1536]{1,0:T(8,128)(2,1)}, bf16[288,256]{1,0:T(8,128)(2,1)}) custom-call(f32[320,128]{1,0:T(8,128)} %get-tuple-element.66.refs_0_, bf16[320,768]{1,0:T(8,128)(2,1)} %get-tuple-element.67.refs_1_.refs_0_, bf16[320,768]{1,0:T(8,128)(2,1)} %get-tuple-element.70.refs_2_.refs_1_, ...), custom_call_target="tpu_custom_call", output_to_operand_aliasing={{0}: (8, {})} | custom-call | flops 5368709120 | bytes 10485760 | tf_op jit(solution)/shard_map/conv_chain/pallas_call | solution.py:227
  95.0 4.4 %context_gradient.1.refs_16_.upstream = bf16[256,1536]{1,0:T(8,128)(2,1)} custom-call(bf16[1536,1536]{1,0:T(8,128)(2,1)} %weight_ref.1, bf16[288,768]{1,0:T(8,128)(2,1)} %get-tuple-element.76.refs_0_.refs_4_, bf16[288,512]{1,0:T(8,128)(2,1)} %get-tuple-element.78.refs_1_.refs_8_, bf16[288,256]{1,0:T(8,128)(2,1)} %get-tuple-element.79.refs_2_.refs_12_, ...), custom_call_target="tpu_custom_call" | custom-call | flops 3221225472 | bytes 8388608 | tf_op jit(solution)/shard_map/context_gradient/pallas_call | solution.py:272
  102.1 4.6 %product_blocks.1 = (bf16[112,1536]{1,0:T(8,128)(2,1)}, bf16[112,1536]{1,0:T(8,128)(2,1)}, bf16[112,1536]{1,0:T(8,128)(2,1)}, bf16[112,1536]{1,0:T(8,128)(2,1)}) custom-call(s32[4]{0:T(128)} %pad_add_fusion.place_ref, bf16[384,256]{1,0:T(8,128)(2,1)} %get-tuple-element.84.refs_0_, bf16[384,256]{1,0:T(8,128)(2,1)} %copy-done.22, bf16[384,256]{1,0:T(8,128)(2,1)} %copy-done.23, ...), custom_call_target="tpu_custom_call" | custom-call | flops 3221225472 | bytes 8388608 | tf_op jit(solution)/shard_map/product_blocks/pallas_call | solution.py:411
  108.9 8.7 %attention_backward.3 = (bf16[256,1536]{1,0:T(8,128)(2,1)}, bf16[512,1536]{1,0:T(8,128)(2,1)}, f32[256,1536]{1,0:T(8,128)}, f32[256,1536]{1,0:T(8,128)}, bf16[512,1536]{1,0:T(8,128)(2,1)}) custom-call(bf16[256,1536]{1,0:T(8,128)(2,1)} %bitcast.18, bf16[576,768]{1,0:T(8,128)(2,1)} %copy-done.15, bf16[256,1536]{1,0:T(8,128)(2,1)} %bitcast.32, ...), custom_call_target="tpu_custom_call" | custom-call | flops 9663676416 | bytes 10485760 | tf_op jit(solution)/shard_map/attention_backward/pallas_call | solution.py:333
  117.6 4.6 %attention_backward.4 = (bf16[256,1536]{1,0:T(8,128)(2,1)}, bf16[512,1536]{1,0:T(8,128)(2,1)}, f32[256,1536]{1,0:T(8,128)}, f32[256,1536]{1,0:T(8,128)}, bf16[512,1536]{1,0:T(8,128)(2,1)}) custom-call(bf16[256,1536]{1,0:T(8,128)(2,1)} %bitcast.19, ...), custom_call_target="tpu_custom_call", output_to_operand_aliasing={{0}: (10, {}), {1}: (11, {}), {2}: (12, {}), {3}: (13, {}),... | custom-call | flops 3221225472 | bytes 10485760 | tf_op jit(solution)/shard_map/attention_backward/pallas_call | solution.py:333
  122.3 3.6 %collective-permute-done.18.refs_3_ = bf16[112,1536]{1,0:T(8,128)(2,1)S(1)} collective-permute-done((bf16[112,1536]{1,0:T(8,128)(2,1)}, bf16[112,1536]{1,0:T(8,128)(2,1)S(1)}, u32[]{:S(2)}, u32[]{:S(2)}) %collective-permute-start.18) | collective-permute-done | bytes 344096 | tf_op jit(solution)/shard_map/ppermute | solution.py:589
  130.2 6.5 %attention_backward.5 = (bf16[256,1536]{1,0:T(8,128)(2,1)}, bf16[512,1536]{1,0:T(8,128)(2,1)}, f32[256,1536]{1,0:T(8,128)}, f32[256,1536]{1,0:T(8,128)}, bf16[512,1536]{1,0:T(8,128)(2,1)}) custom-call(bf16[256,1536]{1,0:T(8,128)(2,1)} %bitcast.20, ...), custom_call_target="tpu_custom_call", output_to_operand_aliasing={{0}: (10, {}), {1}: (11, {}), {2}: (12, {}), {3}: (13, {}),... | custom-call | flops 6442450944 | bytes 10485760 | tf_op jit(solution)/shard_map/attention_backward/pallas_call | solution.py:333
  138.3 2.4 %collective-permute-start.22 = (bf16[512,1536]{1,0:T(8,128)(2,1)}, bf16[512,1536]{1,0:T(8,128)(2,1)S(1)}, u32[]{:S(2)}, u32[]{:S(2)}) collective-permute-start(bf16[512,1536]{1,0:T(8,128)(2,1)} %get-tuple-element.109), channel_id=1, source_target_pairs={{1,0},{2,1},{3,2},{4,3},{5,4},{6,5},{7,6},{8,7},{9,8},{10,9},{11,1... | collective-permute-start | bytes 4718600 | tf_op jit(solution)/shard_map/ppermute | solution.py:606
  140.7 5.3 %collective-permute-start.23 = (bf16[512,1536]{1,0:T(8,128)(2,1)}, bf16[512,1536]{1,0:T(8,128)(2,1)S(1)}, u32[]{:S(2)}, u32[]{:S(2)}) collective-permute-start(bf16[512,1536]{1,0:T(8,128)(2,1)} %get-tuple-element.110), channel_id=1, source_target_pairs={{0,1},{1,2},{2,3},{3,4},{4,5},{5,6},{6,7},{7,8},{8,9},{9,10},{10,1... | collective-permute-start | bytes 4718600 | tf_op jit(solution)/shard_map/ppermute | solution.py:606
  147.9 6.6 %collective-permute-start.24 = (bf16[24,1536]{1,0:T(8,128)(2,1)}, bf16[24,1536]{1,0:T(8,128)(2,1)S(1)}, u32[]{:S(2)}, u32[]{:S(2)}) collective-permute-start(bf16[24,1536]{1,0:T(8,128)(2,1)} %get-tuple-element.117), channel_id=1, source_target_pairs={{0,16},{1,17},{2,18},{3,19},{4,20},{5,21},{6,22},{7,23},{8,24},{9,... | collective-permute-start | bytes 221192 | tf_op jit(solution)/shard_map/ppermute | solution.py:609
  155.7 3.5 %collective-permute-start.26 = (bf16[24,1536]{1,0:T(8,128)(2,1)}, bf16[24,1536]{1,0:T(8,128)(2,1)S(1)}, u32[]{:S(2)}, u32[]{:S(2)}) collective-permute-start(bf16[24,1536]{1,0:T(8,128)(2,1)} %get-tuple-element.119), channel_id=1, source_target_pairs={{0,48},{1,49},{2,50},{3,51},{4,52},{5,53},{6,54},{7,55},{8,56},{9,... | collective-permute-start | bytes 221192 | tf_op jit(solution)/shard_map/ppermute | solution.py:609
  159.3 13.0 %collective-permute-done.24.refs_1_ = bf16[24,1536]{1,0:T(8,128)(2,1)S(1)} collective-permute-done((bf16[24,1536]{1,0:T(8,128)(2,1)}, bf16[24,1536]{1,0:T(8,128)(2,1)S(1)}, u32[]{:S(2)}, u32[]{:S(2)}) %collective-permute-start.24) | collective-permute-done | bytes 73760 | tf_op jit(solution)/shard_map/ppermute | solution.py:609
  172.3 3.8 %collective-permute-done.25.refs_2_ = bf16[24,1536]{1,0:T(8,128)(2,1)S(1)} collective-permute-done((bf16[24,1536]{1,0:T(8,128)(2,1)}, bf16[24,1536]{1,0:T(8,128)(2,1)S(1)}, u32[]{:S(2)}, u32[]{:S(2)}) %collective-permute-start.25) | collective-permute-done | bytes 73760 | tf_op jit(solution)/shard_map/ppermute | solution.py:609
  180.1 3.8 %finish.1 = (bf16[256,1536]{1,0:T(8,128)(2,1)}, bf16[256,1536]{1,0:T(8,128)(2,1)}) custom-call(f32[256,1536]{1,0:T(8,128)} %get-tuple-element.102.refs_0_.refs_4_, f32[256,1536]{1,0:T(8,128)} %get-tuple-element.103.refs_1_, bf16[512,1536]{1,0:T(8,128)(2,1)} %copy-done.2, bf16[512,1536]{1,0:T(8,128)(2,1)} %copy-done.3), custom_call_target="tpu_custom_call" | custom-call | bytes 1024 | tf_op jit(solution)/shard_map/finish/pallas_call | solution.py:511
  (109 shorter events, 38.9 us)
Async XLA Ops:
  5.3 18.5 %collective-permute-start = (bf16[576,768]{1,0:T(8,128)(2,1)}, bf16[576,768]{1,0:T(8,128)(2,1)S(1)}, u32[]{:S(2)}, u32[]{:S(2)}) collective-permute-start(bf16[576,768]{1,0:T(8,128)(2,1)} %get-tuple-element.64), channel_id=1, source_target_pairs={{0,1},{1,2},{2,3},{3,4},{4,5},{5,6},{6,7},{7,8},{8,9},{9,10},{10,1... | collective-permute-start | bytes 2654216 | tf_op jit(solution)/shard_map/ppermute | solution.py:550
  9.3 16.9 %collective-permute-start.1 = (bf16[576,768]{1,0:T(8,128)(2,1)}, bf16[576,768]{1,0:T(8,128)(2,1)}, u32[]{:S(2)}, u32[]{:S(2)}) collective-permute-start(bf16[576,768]{1,0:T(8,128)(2,1)} %get-tuple-element.65), channel_id=1, source_target_pairs={{1,0},{2,1},{3,2},{4,3},{5,4},{6,5},{7,6},{8,7},{9,8},{10,9},{11,1... | collective-permute-start | bytes 2654216 | tf_op jit(solution)/shard_map/ppermute | solution.py:551
  14.7 20.3 %collective-permute-start.2 = (bf16[576,768]{1,0:T(8,128)(2,1)}, bf16[576,768]{1,0:T(8,128)(2,1)S(1)}, u32[]{:S(2)}, u32[]{:S(2)}) collective-permute-start(bf16[576,768]{1,0:T(8,128)(2,1)} %get-tuple-element.68), channel_id=1, source_target_pairs={{0,1},{1,2},{2,3},{3,4},{4,5},{5,6},{6,7},{7,8},{8,9},{9,10},{10,1... | collective-permute-start | bytes 2654216 | tf_op jit(solution)/shard_map/ppermute | solution.py:550
  20.5 16.7 %collective-permute-start.3 = (bf16[576,768]{1,0:T(8,128)(2,1)}, bf16[576,768]{1,0:T(8,128)(2,1)S(1)}, u32[]{:S(2)}, u32[]{:S(2)}) collective-permute-start(bf16[576,768]{1,0:T(8,128)(2,1)} %get-tuple-element.69), channel_id=1, source_target_pairs={{1,0},{2,1},{3,2},{4,3},{5,4},{6,5},{7,6},{8,7},{9,8},{10,9},{11,1... | collective-permute-start | bytes 2654216 | tf_op jit(solution)/shard_map/ppermute | solution.py:551
  50.2 20.3 %collective-permute-start.4 = (bf16[384,256]{1,0:T(8,128)(2,1)}, bf16[384,256]{1,0:T(8,128)(2,1)S(1)}, u32[]{:S(2)}, u32[]{:S(2)}) collective-permute-start(bf16[384,256]{1,0:T(8,128)(2,1)} %get-tuple-element.72), channel_id=1, source_target_pairs={{0,1},{1,0},{2,3},{3,2},{4,5},{5,4},{6,7},{7,6},{8,9},{9,8},{10,11... | collective-permute-start | bytes 589832 | tf_op jit(solution)/shard_map/ppermute | solution.py:564
  50.2 20.3 %collective-permute-start.5 = (bf16[384,256]{1,0:T(8,128)(2,1)}, bf16[384,256]{1,0:T(8,128)(2,1)S(1)}, u32[]{:S(2)}, u32[]{:S(2)}) collective-permute-start(bf16[384,256]{1,0:T(8,128)(2,1)} %get-tuple-element.73), channel_id=1, source_target_pairs={{0,8},{1,9},{2,10},{3,11},{4,12},{5,13},{6,14},{7,15},{8,0},{9,1},... | collective-permute-start | bytes 589832 | tf_op jit(solution)/shard_map/ppermute | solution.py:564
  51.8 18.7 %collective-permute-start.6 = (bf16[384,256]{1,0:T(8,128)(2,1)}, bf16[384,256]{1,0:T(8,128)(2,1)S(1)}, u32[]{:S(2)}, u32[]{:S(2)}) collective-permute-start(bf16[384,256]{1,0:T(8,128)(2,1)} %get-tuple-element.74), channel_id=1, source_target_pairs={{0,9},{1,8},{2,11},{3,10},{4,13},{5,12},{6,15},{7,14},{8,1},{9,0},... | collective-permute-start | bytes 589832 | tf_op jit(solution)/shard_map/ppermute | solution.py:564
  68.9 15.3 %collective-permute-start.8 = (bf16[288,768]{1,0:T(8,128)(2,1)}, bf16[288,768]{1,0:T(8,128)(2,1)S(1)}, u32[]{:S(2)}, u32[]{:S(2)}) collective-permute-start(bf16[288,768]{1,0:T(8,128)(2,1)} %get-tuple-element.76.refs_0_.refs_4_), channel_id=1, source_target_pairs={{0,8},{1,9},{2,10},{3,11},{4,12},{5,13},{6,14},{7,15},{8,0},{9,1},... | collective-permute-start | bytes 1327112 | tf_op jit(solution)/shard_map/ppermute | solution.py:575
  70.5 13.7 %collective-permute-start.7 = (bf16[288,768]{1,0:T(8,128)(2,1)}, bf16[288,768]{1,0:T(8,128)(2,1)S(1)}, u32[]{:S(2)}, u32[]{:S(2)}) collective-permute-start(bf16[288,768]{1,0:T(8,128)(2,1)} %get-tuple-element.76.refs_0_.refs_4_), channel_id=1, source_target_pairs={{0,1},{1,0},{2,3},{3,2},{4,5},{5,4},{6,7},{7,6},{8,9},{9,8},{10,11... | collective-permute-start | bytes 1327112 | tf_op jit(solution)/shard_map/ppermute | solution.py:584
  83.3 10.5 %collective-permute-start.11 = (bf16[288,512]{1,0:T(8,128)(2,1)}, bf16[288,512]{1,0:T(8,128)(2,1)S(1)}, u32[]{:S(2)}, u32[]{:S(2)}) collective-permute-start(bf16[288,512]{1,0:T(8,128)(2,1)} %get-tuple-element.78.refs_1_.refs_8_), channel_id=1, source_target_pairs={{0,8},{1,9},{2,10},{3,11},{4,12},{5,13},{6,14},{7,15},{8,0},{9,1},... | collective-permute-start | bytes 884744 | tf_op jit(solution)/shard_map/ppermute | solution.py:575
  83.7 15.7 %collective-permute-start.10 = (bf16[288,512]{1,0:T(8,128)(2,1)}, bf16[288,512]{1,0:T(8,128)(2,1)S(1)}, u32[]{:S(2)}, u32[]{:S(2)}) collective-permute-start(bf16[288,512]{1,0:T(8,128)(2,1)} %get-tuple-element.78.refs_1_.refs_8_), channel_id=1, source_target_pairs={{0,1},{1,0},{2,3},{3,2},{4,5},{5,4},{6,7},{7,6},{8,9},{9,8},{10,11... | collective-permute-start | bytes 884744 | tf_op jit(solution)/shard_map/ppermute | solution.py:584
  84.2 10.0 %collective-permute-start.9 = (bf16[288,768]{1,0:T(8,128)(2,1)S(1)}, bf16[288,768]{1,0:T(8,128)(2,1)S(1)}, u32[]{:S(2)}, u32[]{:S(2)}) collective-permute-start(bf16[288,768]{1,0:T(8,128)(2,1)S(1)} %collective-permute-done.8.refs_10_.refs_6_), channel_id=1, source_target_pairs={{0,1},{1,0},{2,3},{3,2},{4,5},{5,4},{6,7},{7,6},{8,9},{9,8},{10,11... | collective-permute-start | bytes 1327112 | tf_op jit(solution)/shard_map/ppermute | solution.py:577
  93.7 7.6 %collective-permute-start.14 = (bf16[288,256]{1,0:T(8,128)(2,1)}, bf16[288,256]{1,0:T(8,128)(2,1)S(1)}, u32[]{:S(2)}, u32[]{:S(2)}) collective-permute-start(bf16[288,256]{1,0:T(8,128)(2,1)} %get-tuple-element.79.refs_2_.refs_12_), channel_id=1, source_target_pairs={{0,8},{1,9},{2,10},{3,11},{4,12},{5,13},{6,14},{7,15},{8,0},{9,1},... | collective-permute-start | bytes 442376 | tf_op jit(solution)/shard_map/ppermute | solution.py:575
  106.7 15.5 %collective-permute-start.16 = (bf16[112,1536]{1,0:T(8,128)(2,1)}, bf16[112,1536]{1,0:T(8,128)(2,1)S(1)}, u32[]{:S(2)}, u32[]{:S(2)}) collective-permute-start(bf16[112,1536]{1,0:T(8,128)(2,1)} %get-tuple-element.97), channel_id=1, source_target_pairs={{0,64},{64,128},{128,192},{192,0},{1,65},{65,129},{129,193},{193,1... | collective-permute-start | bytes 1032200 | tf_op jit(solution)/shard_map/ppermute | solution.py:589
  106.7 15.5 %collective-permute-start.17 = (bf16[112,1536]{1,0:T(8,128)(2,1)}, bf16[112,1536]{1,0:T(8,128)(2,1)S(1)}, u32[]{:S(2)}, u32[]{:S(2)}) collective-permute-start(bf16[112,1536]{1,0:T(8,128)(2,1)} %get-tuple-element.98), channel_id=1, source_target_pairs={{0,128},{64,192},{128,0},{192,64},{1,129},{65,193},{129,1},{193,65... | collective-permute-start | bytes 1032200 | tf_op jit(solution)/shard_map/ppermute | solution.py:589
  108.9 16.9 %collective-permute-start.18 = (bf16[112,1536]{1,0:T(8,128)(2,1)}, bf16[112,1536]{1,0:T(8,128)(2,1)S(1)}, u32[]{:S(2)}, u32[]{:S(2)}) collective-permute-start(bf16[112,1536]{1,0:T(8,128)(2,1)} %get-tuple-element.99), channel_id=1, source_target_pairs={{0,192},{64,0},{128,64},{192,128},{1,193},{65,1},{129,65},{193,129... | collective-permute-start | bytes 1032200 | tf_op jit(solution)/shard_map/ppermute | solution.py:589
  128.7 8.0 %collective-permute-start.19 = (bf16[40,1536]{1,0:T(8,128)(2,1)}, bf16[40,1536]{1,0:T(8,128)(2,1)S(1)}, u32[]{:S(2)}, u32[]{:S(2)}) collective-permute-start(bf16[40,1536]{1,0:T(8,128)(2,1)} %get-tuple-element.106), channel_id=1, source_target_pairs={{0,2},{1,3},{2,4},{3,5},{4,6},{5,7},{6,0},{7,1},{8,10},{9,11},{10,... | collective-permute-start | bytes 368648 | tf_op jit(solution)/shard_map/ppermute | solution.py:601
  128.7 8.0 %collective-permute-start.20 = (bf16[40,1536]{1,0:T(8,128)(2,1)}, bf16[40,1536]{1,0:T(8,128)(2,1)S(1)}, u32[]{:S(2)}, u32[]{:S(2)}) collective-permute-start(bf16[40,1536]{1,0:T(8,128)(2,1)} %get-tuple-element.107), channel_id=1, source_target_pairs={{0,4},{1,5},{2,6},{3,7},{4,0},{5,1},{6,2},{7,3},{8,12},{9,13},{10,... | collective-permute-start | bytes 368648 | tf_op jit(solution)/shard_map/ppermute | solution.py:601
  128.8 9.6 %collective-permute-start.21 = (bf16[40,1536]{1,0:T(8,128)(2,1)}, bf16[40,1536]{1,0:T(8,128)(2,1)S(1)}, u32[]{:S(2)}, u32[]{:S(2)}) collective-permute-start(bf16[40,1536]{1,0:T(8,128)(2,1)} %get-tuple-element.108), channel_id=1, source_target_pairs={{0,6},{1,7},{2,0},{3,1},{4,2},{5,3},{6,4},{7,5},{8,14},{9,15},{10,... | collective-permute-start | bytes 368648 | tf_op jit(solution)/shard_map/ppermute | solution.py:601
  138.3 40.1 %collective-permute-start.22 = (bf16[512,1536]{1,0:T(8,128)(2,1)}, bf16[512,1536]{1,0:T(8,128)(2,1)S(1)}, u32[]{:S(2)}, u32[]{:S(2)}) collective-permute-start(bf16[512,1536]{1,0:T(8,128)(2,1)} %get-tuple-element.109), channel_id=1, source_target_pairs={{1,0},{2,1},{3,2},{4,3},{5,4},{6,5},{7,6},{8,7},{9,8},{10,9},{11,1... | collective-permute-start | bytes 4718600 | tf_op jit(solution)/shard_map/ppermute | solution.py:606
  140.7 37.7 %collective-permute-start.23 = (bf16[512,1536]{1,0:T(8,128)(2,1)}, bf16[512,1536]{1,0:T(8,128)(2,1)S(1)}, u32[]{:S(2)}, u32[]{:S(2)}) collective-permute-start(bf16[512,1536]{1,0:T(8,128)(2,1)} %get-tuple-element.110), channel_id=1, source_target_pairs={{0,1},{1,2},{2,3},{3,4},{4,5},{5,6},{6,7},{7,8},{8,9},{9,10},{10,1... | collective-permute-start | bytes 4718600 | tf_op jit(solution)/shard_map/ppermute | solution.py:606
  147.9 24.4 %collective-permute-start.24 = (bf16[24,1536]{1,0:T(8,128)(2,1)}, bf16[24,1536]{1,0:T(8,128)(2,1)S(1)}, u32[]{:S(2)}, u32[]{:S(2)}) collective-permute-start(bf16[24,1536]{1,0:T(8,128)(2,1)} %get-tuple-element.117), channel_id=1, source_target_pairs={{0,16},{1,17},{2,18},{3,19},{4,20},{5,21},{6,22},{7,23},{8,24},{9,... | collective-permute-start | bytes 221192 | tf_op jit(solution)/shard_map/ppermute | solution.py:609
  154.5 21.6 %collective-permute-start.25 = (bf16[24,1536]{1,0:T(8,128)(2,1)}, bf16[24,1536]{1,0:T(8,128)(2,1)S(1)}, u32[]{:S(2)}, u32[]{:S(2)}) collective-permute-start(bf16[24,1536]{1,0:T(8,128)(2,1)} %get-tuple-element.118), channel_id=1, source_target_pairs={{0,32},{1,33},{2,34},{3,35},{4,36},{5,37},{6,38},{7,39},{8,40},{9,... | collective-permute-start | bytes 221192 | tf_op jit(solution)/shard_map/ppermute | solution.py:609
  155.7 20.4 %collective-permute-start.26 = (bf16[24,1536]{1,0:T(8,128)(2,1)}, bf16[24,1536]{1,0:T(8,128)(2,1)S(1)}, u32[]{:S(2)}, u32[]{:S(2)}) collective-permute-start(bf16[24,1536]{1,0:T(8,128)(2,1)} %get-tuple-element.119), channel_id=1, source_target_pairs={{0,48},{1,49},{2,50},{3,51},{4,52},{5,53},{6,54},{7,55},{8,56},{9,... | collective-permute-start | bytes 221192 | tf_op jit(solution)/shard_map/ppermute | solution.py:609
  (32 other events, 105.4 us)
